TPU v7x, 32 devices: a whole 2x2x4 slice. The times are simulated.
32 devices in a mesh: wide: 4 (over y, core), narrow: 8 (over z, x).
Axes of the slice: x: 2, y: 2, z: 4, core: 2. Of those that a mesh axis runs over, the one named last changes fastest.
Arguments:
- site_basis: bfloat16 [512, 512], P(('wide', 'narrow')), may hold values from -0.25 to 0.25
- left_ops: bfloat16 [96, 512, 512], P(('wide', 'narrow')), may hold values from -0.25 to 0.25
- right_ops: bfloat16 [96, 512, 512], P(('wide', 'narrow')), may hold values from -0.25 to 0.25
- integrals: bfloat16 [96, 96], replicated, may hold values from -0.625 to 0.625
- wavefunction: bfloat16 [512, 512], P(('wide', 'narrow')), may hold values from -6 to 6
- pair_order: int32 [96], replicated, may hold values from 0 to 95, each once
- sector_sizes: int32 [8], replicated, may hold values from 1 to 128, 512 in all
Outputs:
- propagated: float32 [512, 512], P(('wide', 'narrow'))
Inputs may be any that keep to these rules, and one draw needn't show every extreme that they name: `pair_order`: each orbital pair stands in exactly one of the 96 slots. `sector_sizes`: the sizes sum to 512.
All inputs are finite; a program needn't handle non-finite values.
Results may differ from a plain program's by a relative error of at most 0.008.
Values may be sent and summed in bfloat16 or wider, within the bound.
No kernel may reach another device: no remote copies, remote signals or barrier semaphores. Data moves between devices by JAX's collectives and lax.ppermute only.
A program may use at most 64 MiB of HBM per device.

v0:
```python
import math

import jax
import jax.numpy as jnp
from jax import lax
from jax.sharding import PartitionSpec as P

ORDER = 3


def sector_mask(sector_sizes, row_ids, col_ids):
    block_ends = jnp.cumsum(sector_sizes)
    row_block = jnp.sum((row_ids[:, None] >= block_ends[None, :]).astype(jnp.int32), axis=1)
    col_block = jnp.sum((col_ids[:, None] >= block_ends[None, :]).astype(jnp.int32), axis=1)
    return (jnp.abs(row_block[:, None] - col_block[None, :]) <= 2).astype(jnp.float32)


def mix_rows(mixing, operands):
    flat = operands.reshape(operands.shape[0], -1)
    mixed = jnp.dot(mixing, flat, preferred_element_type=jnp.float32).astype(jnp.bfloat16)
    return mixed.reshape(operands.shape)


def contract_joined(left, right):
    return lax.dot_general(
        left, right, (((1,), (1,)), ((), ())), preferred_element_type=jnp.float32
    )


def local(site_basis, left_ops, right_ops, integrals, wavefunction, pair_order, sector_sizes):
    row_count = wavefunction.shape[0]
    states = wavefunction.shape[1]
    pair_local = left_ops.shape[0]
    pair_total = integrals.shape[0]
    full_basis = lax.all_gather(site_basis, ("wide", "narrow"), axis=0, tiled=True)
    rotated = jnp.dot(
        left_ops.reshape(pair_local * states, states),
        full_basis,
        preferred_element_type=jnp.float32,
    ).astype(jnp.bfloat16)
    side_by_side = (
        rotated.reshape(pair_local, states, states)
        .transpose(1, 0, 2)
        .reshape(states, pair_local * states)
    )
    built_wide = jnp.dot(full_basis.T, side_by_side, preferred_element_type=jnp.float32).astype(
        jnp.bfloat16
    )
    built_ops = built_wide.reshape(states, pair_local, states).transpose(1, 0, 2)
    built_rows = built_ops.reshape(pair_local * states, states)
    mixing = jnp.take(jnp.take(integrals, pair_order, axis=0), pair_order, axis=1)
    mixed_ops = mix_rows(
        mixing,
        lax.all_to_all(right_ops, ("wide", "narrow"), split_axis=1, concat_axis=0, tiled=True),
    )
    comp_ops = lax.all_to_all(
        mixed_ops, ("wide", "narrow"), split_axis=0, concat_axis=1, tiled=True
    )
    comp_joined = comp_ops.transpose(1, 0, 2).reshape(states, pair_local * states)
    first_row = lax.axis_index(("wide", "narrow")) * row_count
    row_ids = first_row + jnp.arange(row_count, dtype=jnp.int32)
    col_ids = jnp.arange(states, dtype=jnp.int32)
    local_mask = sector_mask(sector_sizes, row_ids, col_ids)
    local_state = (wavefunction.astype(jnp.float32) * local_mask).astype(jnp.bfloat16)
    summed = local_state.astype(jnp.float32)
    full_state = lax.all_gather(local_state, ("wide", "narrow"), axis=0, tiled=True)
    step_size = 2.0 / math.sqrt(pair_total)
    full_mask = sector_mask(sector_sizes, col_ids, col_ids)
    for order_index in range(1, ORDER + 1):
        applied = jnp.dot(built_rows, full_state, preferred_element_type=jnp.float32).astype(
            jnp.bfloat16
        )
        applied_joined = (
            applied.reshape(pair_local, states, states)
            .transpose(1, 0, 2)
            .reshape(states, pair_local * states)
        )
        factor = -(step_size / order_index)
        partial_term = contract_joined(applied_joined, comp_joined)
        full_term = lax.psum(partial_term, ("wide", "narrow"))
        full_state = (factor * full_mask * full_term).astype(jnp.bfloat16)
        own_rows = lax.dynamic_slice_in_dim(full_state, first_row, row_count, 0)
        summed = summed + own_rows.astype(jnp.float32)
    return summed


def solution(mesh):
    placed = (
        P(("wide", "narrow"), None),
        P(("wide", "narrow"), None, None),
        P(("wide", "narrow"), None, None),
        P(),
        P(("wide", "narrow"), None),
        P(),
        P(),
    )
    return jax.shard_map(
        local, mesh=mesh, in_specs=placed, out_specs=P(("wide", "narrow"), None), check_vma=False
    )
```

profile of v0, /device:TPU:0, one launch (start us, length us, event | category | flops | bytes accessed | tf_op | source)
XLA Modules:
  0.0 663.9 jit_solution(11819695531645070585)
XLA Ops:
  6.5 4.2 copy.24
  10.7 7.4 %all-to-all-start = ((bf16[3,512,512]{2,0,1:T(4,128)(2,1)}), bf16[3,512,512]{2,0,1:T(4,128)(2,1)}, u32[]{:S(2)}, u32[]{:S(2)}) async-start(bf16[3,512,512]{2,0,1:T(4,128)(2,1)} %copy.24), calls=%async_computation | async-start | bytes 4194304 | tf_op jit(solution)/shard_map/all_to_all | solution.py:54
  18.2 0.0 copy-done.11
  18.2 0.7 gather_fusion
  18.9 0.1 broadcast_select_fusion
  19.0 0.1 copy.23
  19.1 0.7 gather_fusion.1
  19.8 48.4 %all-to-all-done = bf16[3,512,512]{2,0,1:T(4,128)(2,1)} async-done(((bf16[3,512,512]{2,0,1:T(4,128)(2,1)}), bf16[3,512,512]{2,0,1:T(4,128)(2,1)}, u32[]{:S(2)}, u32[]{:S(2)}) %all-to-all-start) | async-done | bytes 1572896 | tf_op jit(solution)/shard_map/all_to_all | solution.py:54
  68.2 2.1 copy.25
  70.3 1.0 copy.27
  71.3 0.7 convolution_convert_fusion
  72.0 1.7 copy.28
  73.7 3.2 all-to-all-start.1
  77.0 0.0 all-reduce.4.cloned.1.call-start
  77.1 95.8 %all_gather.6 = bf16[512,512]{1,0:T(8,128)(2,1)S(1)} all-gather(bf16[16,512]{1,0:T(8,128)(2,1)S(1)} %copy-done.10), channel_id=1, replica_groups=mesh['wide'=4,'narrow'=8] {'wide','narrow'}, dimensions={0}, use_global_device_ids=true | all-gather | bytes 540672 | tf_op jit(solution)/shard_map/all_gather | solution.py:35
  172.9 2.1 convolution_convert_fusion.5
  175.0 2.6 copy.21
  177.6 3.7 convolution_convert_fusion.4
  181.3 2.6 copy.22
  183.9 0.2 reduce-window.8
  184.1 0.1 convert_reduce_fusion
  184.2 0.1 convert_reduce_fusion.1
  184.3 0.1 select_convert_fusion
  184.4 66.3 %all_gather.7 = bf16[512,512]{1,0:T(8,128)(2,1)S(1)} all-gather(bf16[16,512]{1,0:T(8,128)(2,1)S(1)} %select_convert_fusion), channel_id=1, replica_groups=mesh['wide'=4,'narrow'=8] {'wide','narrow'}, dimensions={0}, use_global_device_ids=true | all-gather | bytes 540672 | tf_op jit(solution)/shard_map/all_gather | solution.py:66
  250.6 3.6 convolution_convert_fusion.3
  254.2 0.0 all-to-all-done.1
  254.2 0.1 copy.26
  254.3 1.1 copy-done.2
  255.5 0.7 copy-done.13
  256.2 2.0 convolution_bitcast_fusion.2
  258.1 0.0 all-reduce.4.cloned.1.call-update
  258.2 0.0 all-reduce.6.cloned.1.call-start
  258.2 128.8 %all-reduce.4.cloned.1.call-done = f32[512,512]{1,0:T(8,128)} async-done(((f32[512,512]{1,0:T(8,128)}), f32[512,512]{1,0:T(8,128)}) %all-reduce.4.cloned.1.call-update) | async-done | bytes 1048592 | tf_op jit(solution)/shard_map/psum | solution.py:80
  387.0 1.5 multiply_convert_fusion.1
  388.6 1.0 convolution_convert_fusion.2
  389.6 0.6 copy-done.3
  390.2 2.0 convolution_bitcast_fusion.1
  392.2 0.0 all-reduce.6.cloned.1.call-update
  392.2 0.0 all-reduce.8.cloned.1.call-start
  392.2 129.5 %all-reduce.6.cloned.1.call-done = f32[512,512]{1,0:T(8,128)} async-done(((f32[512,512]{1,0:T(8,128)}), f32[512,512]{1,0:T(8,128)}) %all-reduce.6.cloned.1.call-update) | async-done | bytes 1048592 | tf_op jit(solution)/shard_map/psum | solution.py:80
  521.8 1.5 multiply_convert_fusion
  523.4 1.0 convolution_convert_fusion.1
  524.3 0.6 copy-done.4
  524.9 2.0 convolution_bitcast_fusion
  527.0 0.0 all-reduce.8.cloned.1.call-update
  527.0 0.3 abs_compare_fusion
  527.3 128.6 %all-reduce.8.cloned.1.call-done = f32[512,512]{1,0:T(8,128)} async-done(((f32[512,512]{1,0:T(8,128)}), f32[512,512]{1,0:T(8,128)}) %all-reduce.8.cloned.1.call-update) | async-done | bytes 1048592 | tf_op jit(solution)/shard_map/psum | solution.py:80
  655.9 1.5 convert_add_fusion
  (27 shorter events, 0.1 us)
Async XLA Ops:
  6.5 166.4 %copy-start = (bf16[3,512,512]{2,1,0:T(8,128)(2,1)S(1)}, bf16[3,512,512]{2,1,0:T(8,128)(2,1)}, u32[]{:S(2)}) copy-start(bf16[3,512,512]{2,1,0:T(8,128)(2,1)} %param.8) | copy-start | bytes 4718596
  10.7 7.4 %copy-start.11 = (s32[96]{0:T(128)S(1)}, s32[96]{0:T(128)}, u32[]{:S(2)}) copy-start(s32[96]{0:T(128)} %param.12) | copy-start | bytes 1156
  10.7 7.5 %copy-start.5 = (bf16[96,96]{1,0:T(8,128)(2,1)S(1)}, bf16[96,96]{1,0:T(8,128)(2,1)}, u32[]{:S(2)}) copy-start(bf16[96,96]{1,0:T(8,128)(2,1)} %param.10) | copy-start | bytes 55300
  10.7 57.5 %all-to-all-start = ((bf16[3,512,512]{2,0,1:T(4,128)(2,1)}), bf16[3,512,512]{2,0,1:T(4,128)(2,1)}, u32[]{:S(2)}, u32[]{:S(2)}) async-start(bf16[3,512,512]{2,0,1:T(4,128)(2,1)} %copy.24), calls=%async_computation | async-start | bytes 4194304 | tf_op jit(solution)/shard_map/all_to_all | solution.py:54
  73.7 3.3 copy-start.10
  73.7 180.4 %all-to-all-start.1 = ((bf16[96,16,512]{2,1,0:T(8,128)(2,1)}), bf16[96,16,512]{2,1,0:T(8,128)(2,1)S(1)}, u32[]{:S(2)}, u32[]{:S(2)}) async-start(bf16[96,16,512]{2,1,0:T(8,128)(2,1)} %bitcast.60), calls=%async_computation.1 | async-start | bytes 3145728 | tf_op jit(solution)/shard_map/all_to_all | solution.py:56
  77.0 310.0 %all-reduce.4.cloned.1.call-start = ((), (), s32[]{:S(2)}) async-start(), calls=%async_computation.2 | async-start | bytes 2097152 | tf_op jit(solution)/shard_map/psum | solution.py:80
  172.9 2.1 copy-start.8
  181.3 2.6 copy-start.12
  181.3 3.0 copy-start.9
  254.2 2.0 copy-start.13
  254.3 1.1 copy-start.2
  258.1 130.4 %copy-start.1 = (bf16[512,3,512]{2,0,1:T(8,128)(2,1)S(1)}, bf16[512,3,512]{2,0,1:T(8,128)(2,1)}, u32[]{:S(2)}) copy-start(bf16[512,3,512]{2,0,1:T(8,128)(2,1)} %copy.22) | copy-start | bytes 4718596
  258.2 263.6 %all-reduce.6.cloned.1.call-start = ((), (), s32[]{:S(2)}) async-start(), calls=%async_computation.3 | async-start | bytes 2097152 | tf_op jit(solution)/shard_map/psum | solution.py:80
  388.6 1.0 copy-start.6
  388.6 1.6 copy-start.3
  392.2 263.7 %all-reduce.8.cloned.1.call-start = ((), (), s32[]{:S(2)}) async-start(), calls=%async_computation.4 | async-start | bytes 2097152 | tf_op jit(solution)/shard_map/psum | solution.py:80
  523.3 1.0 copy-start.7
  523.3 1.6 copy-start.4
Sparse Core Ops, SparseCore 0:
  258.3 128.6 all-reduce.3
  393.0 128.7 all-reduce.5
  527.1 128.7 all-reduce.7
where the time goes:
time: 665 us; the launch traced here: 664 us
  waiting for transfers between devices  435 us (65%)
  blocking collectives  162 us (24%)
  local copies, waits for them, and re-layouts  18.9 us (3%)
  matrix products  18 us (3%)
  between operations  13.3 us (2%)
  starting transfers between devices  10.8 us (2%)
    psum x3, waiting for transfers between devices, local(): full_term = lax.psum(partial_term, ('wide', 'narrow'))  387 us
    all_gather x1, blocking collectives, local(): lax.all_gather(site_basis, ('wide', 'narrow'), axis=0, tiled=True)  95.8 us
    all_gather x1, blocking collectives, local(): lax.all_gather(local_state, ('wide', 'narrow'), axis=0, tiled=True)  66.3 us
    all_to_all x1, waiting for transfers between devices, local(): lax.all_to_all(right_ops, ('wide', 'narrow'), split_axis=1, concat_axis=0...  48.4 us
  transfers between devices with their start and end apart: 5, of which 4 were waited for; matrix products, arithmetic and copies ran while one was open for 3% of the time, Pallas kernels for 0%

commit v1 on v0

v1 whole, which is shorter than its diff:
```python
import functools
import math

import jax
import jax.numpy as jnp
from jax import lax
from jax.experimental import pallas as pl
from jax.experimental.pallas import tpu as pltpu
from jax.sharding import Mesh, PartitionSpec as P

ORDER = 3
OUTER, CORE, NARROW = "outer", "core", "narrow"
ALL = (OUTER, CORE, NARROW)
CHIPS = (OUTER, NARROW)
VMEM_LIMIT = 48 * 1024 * 1024
F32, BF16 = jnp.float32, jnp.bfloat16


def whole_block(shape):
    return pl.BlockSpec(shape, lambda *_: (0,) * len(shape))


def kernel_params():
    return pltpu.CompilerParams(vmem_limit_bytes=VMEM_LIMIT)


def block_ids(sector_sizes, count):
    ends = jnp.cumsum(sector_sizes)
    ids = jnp.arange(count, dtype=jnp.int32)
    return jnp.sum((ids[:, None] >= ends[None, :]).astype(jnp.int32), axis=1)


def swap_cores(value):
    return lax.ppermute(value, CORE, [(0, 1), (1, 0)])


def gather_over(value, axis, size):
    value = value[None]
    if size & (size - 1):
        return lax.all_gather(value, axis, axis=0, tiled=True)
    position = lax.axis_index(axis)
    if size == 1:
        return value
    steps = [1 << bit for bit in range(size.bit_length() - 1)]
    done = []
    for step in steps[1:] + steps[:1]:
        got = lax.ppermute(value, axis, [(i, i ^ step) for i in range(size)])
        high = (position // step) % 2 == 1
        low_part = jnp.where(high, got, value)
        high_part = jnp.where(high, value, got)
        value = jnp.stack([low_part, high_part])
        done = [step] + done
    bits = len(done)
    tail = value.shape[bits + 1 :]
    value = value.reshape((2,) * bits + tail)
    order = sorted(range(bits), key=lambda dim: -done[dim])
    value = value.transpose(tuple(order) + tuple(range(bits, bits + len(tail))))
    return value.reshape((size,) + tail)


def build_kernel(basis_ref, left_ref, built_ref):
    basis = basis_ref[...]
    rotated = jnp.dot(left_ref[0], basis, preferred_element_type=F32).astype(BF16)
    built = lax.dot_general(basis, rotated, (((0,), (0,)), ((), ())), preferred_element_type=F32)
    built_ref[0] = built.astype(BF16)


def build(basis, left_ops):
    pairs, states, _ = left_ops.shape
    flops = 4 * pairs * states**3
    return pl.pallas_call(
        build_kernel,
        grid=(pairs,),
        in_specs=[
            whole_block((states, states)),
            pl.BlockSpec((1, states, states), lambda s: (s, 0, 0)),
        ],
        out_specs=pl.BlockSpec((1, states, states), lambda s: (s, 0, 0)),
        out_shape=jax.ShapeDtypeStruct(left_ops.shape, BF16),
        compiler_params=kernel_params(),
        cost_estimate=pl.CostEstimate(flops=flops, bytes_accessed=4 * left_ops.size, transcendentals=0),
        name="build",
    )(basis, left_ops)


def spread_kernel(rows, row_pair_ref, col_pair_ref, integrals_ref, spread_ref):
    height, width = spread_ref.shape
    total = integrals_ref.shape[0]
    pick_row = (row_pair_ref[...] == lax.broadcasted_iota(jnp.int32, (height, total), 1)).astype(F32)
    pick_col = (col_pair_ref[...] == lax.broadcasted_iota(jnp.int32, (total, width), 0)).astype(F32)
    picked = jnp.dot(pick_row.astype(BF16), integrals_ref[...], preferred_element_type=F32)
    mixing = jnp.dot(picked.astype(BF16), pick_col.astype(BF16), preferred_element_type=F32)
    row_id = lax.broadcasted_iota(jnp.int32, (height, width), 0) + pl.program_id(0) * height
    col_id = lax.broadcasted_iota(jnp.int32, (height, width), 1)
    same = lax.rem(row_id, rows) == lax.rem(col_id, rows)
    spread_ref[...] = jnp.where(same, mixing, 0.0).astype(BF16)


def spread_mixing(integrals, pair_order, rows, parts):
    total = integrals.shape[0]
    size = total * rows
    height = size // parts
    repeated = jnp.repeat(pair_order, rows)
    return pl.pallas_call(
        functools.partial(spread_kernel, rows),
        grid=(parts,),
        in_specs=[
            pl.BlockSpec((height, 1), lambda w: (w, 0)),
            whole_block((1, size)),
            whole_block((total, total)),
        ],
        out_specs=pl.BlockSpec((height, size), lambda w: (w, 0)),
        out_shape=jax.ShapeDtypeStruct((size, size), BF16),
        compiler_params=kernel_params(),
        cost_estimate=pl.CostEstimate(flops=2 * size * size * total, bytes_accessed=2 * size * size, transcendentals=0),
        name="spread_mixing",
    )(repeated[:, None], repeated[None, :], integrals)


def mix_kernel(spread_ref, right_ref, out_ref):
    mixed = jnp.dot(spread_ref[...], right_ref[...], preferred_element_type=F32).astype(BF16)
    narrow, block, half = out_ref.shape[2], out_ref.shape[4], out_ref.shape[5]
    for h in range(2):
        out_ref[0, h, :, 0] = mixed[:, h * half : (h + 1) * half].reshape(narrow, block, half)


def mix(spread, right_rows, wide, narrow, block):
    size, states = right_rows.shape
    height = size // wide
    half = states // 2
    if block % 16:
        mixed = jnp.dot(spread, right_rows, preferred_element_type=F32).astype(BF16)
        mixed = mixed.reshape(wide // 2, 2, narrow, block, 2, half)
        return mixed.transpose(0, 4, 2, 1, 3, 5)
    return pl.pallas_call(
        mix_kernel,
        grid=(wide,),
        in_specs=[
            pl.BlockSpec((height, size), lambda w: (w, 0)),
            whole_block((size, states)),
        ],
        out_specs=pl.BlockSpec((1, 2, narrow, 1, block, half), lambda w: (w // 2, 0, 0, w % 2, 0, 0)),
        out_shape=jax.ShapeDtypeStruct((wide // 2, 2, narrow, 2, block, half), BF16),
        compiler_params=kernel_params(),
        cost_estimate=pl.CostEstimate(flops=2 * size * size * states, bytes_accessed=2 * size * size, transcendentals=0),
        name="mix",
    )(spread, right_rows)


def apply_kernel(core_ref, state_ref, own_ref, other_ref, comp_ref, keep_ref, send_ref, applied_ref):
    outer, narrow, _, rows, half = state_ref.shape
    pairs, states, _ = own_ref.shape
    chips = outer * narrow
    core = core_ref[0]
    state = jnp.concatenate(
        [state_ref[y, :, c].reshape(narrow * rows, half) for y in range(outer) for c in range(2)]
    )
    for side, ref in enumerate((own_ref, other_ref)):
        for q in range(pairs):
            one = jnp.dot(ref[q], state, preferred_element_type=F32).astype(BF16)
            column = (side * pairs + q) * half
            applied_ref[:, column : column + half] = one
    applied = applied_ref[...]
    for out_ref, place in ((send_ref, 1 - core), (keep_ref, core)):
        columns = []
        for side in (core, 1 - core):
            for q in range(pairs):
                part = comp_ref[pl.ds(place * chips, chips), side * pairs + q]
                columns.append(part.reshape(chips * rows, half))
        joined = jnp.concatenate(columns, axis=1)
        term = lax.dot_general(applied, joined, (((1,), (1,)), ((), ())), preferred_element_type=F32)
        term = term.astype(out_ref.dtype).reshape(outer, 2, narrow, rows, half)
        for c in range(2):
            out_ref[:, :, c] = term[:, c]


def apply_pairs(core, state, own, other, comp):
    outer, narrow, _, rows, half = state.shape
    pairs, states, _ = own.shape
    if rows % 16:
        full = state.transpose(0, 2, 1, 3, 4).reshape(states, half)
        built = jnp.concatenate([own, other])
        applied = jnp.einsum("sil,lk->sik", built, full, preferred_element_type=F32).astype(BF16)
        joined = comp.transpose(1, 0, 2, 3).reshape(2, pairs, states, half)
        joined = jnp.concatenate([joined[core[0]], joined[1 - core[0]]])
        term = jnp.einsum("sik,sjk->ij", applied, joined, preferred_element_type=F32)
        term = term.reshape(outer, 2, narrow, rows, 2, half).transpose(4, 0, 2, 1, 3, 5)
        return term[core[0]], term[1 - core[0]].astype(BF16)
    return pl.pallas_call(
        apply_kernel,
        in_specs=[pl.BlockSpec(memory_space=pltpu.SMEM)] + [pl.BlockSpec(memory_space=pltpu.VMEM)] * 4,
        out_specs=[pl.BlockSpec(memory_space=pltpu.VMEM)] * 2,
        out_shape=[
            jax.ShapeDtypeStruct(state.shape, F32),
            jax.ShapeDtypeStruct(state.shape, BF16),
        ],
        scratch_shapes=[pltpu.VMEM((states, 2 * pairs * half), BF16)],
        compiler_params=kernel_params(),
        cost_estimate=pl.CostEstimate(
            flops=8 * pairs * states**2 * half, bytes_accessed=8 * pairs * states**2, transcendentals=0
        ),
        name="apply_pairs",
    )(core, state, own, other, comp)


def local(site_basis, left_ops, right_ops, integrals, wavefunction, pair_order, sector_sizes):
    outer, narrow = lax.axis_size(OUTER), lax.axis_size(NARROW)
    wide = 2 * outer
    devices = wide * narrow
    rows, states = wavefunction.shape
    half = states // 2
    pairs = left_ops.shape[0]
    pair_total = integrals.shape[0]
    chips = outer * narrow
    own_outer, own_core, own_narrow = (lax.axis_index(name) for name in ALL)
    is_high = own_core == 1

    def own_half(value):
        return jnp.where(is_high, value[..., half:], value[..., :half])

    def other_half(value):
        return jnp.where(is_high, value[..., :half], value[..., half:])

    def by_core(own, other):
        return jnp.stack([jnp.where(is_high, other, own), jnp.where(is_high, own, other)])

    parts = right_ops.reshape(pairs, devices, rows, states).transpose(1, 0, 2, 3)
    parts = parts.reshape(devices, pairs * rows, states)
    right_rows = lax.all_to_all(parts, ALL, split_axis=0, concat_axis=0, tiled=True)
    right_rows = right_rows.reshape(pair_total * rows, states)
    spread = spread_mixing(integrals, pair_order, rows, wide)

    blocks = block_ids(sector_sizes, states).astype(F32)
    by_device = blocks.reshape(outer, 2, narrow, rows)
    chip_rows = lax.dynamic_slice(by_device, (own_outer, 0, own_narrow, 0), (1, 2, 1, rows)).reshape(2, rows)
    own_columns = own_half(blocks)
    local_mask = (jnp.abs(chip_rows[:, :, None] - own_columns[None, None, :]) <= 2.0).astype(F32)

    piece = by_core(own_half(wavefunction), swap_cores(other_half(wavefunction)))
    piece = (piece.astype(F32) * local_mask).astype(BF16)
    summed = piece.astype(F32)

    together = jnp.concatenate([site_basis.reshape(rows * 2, half), piece.reshape(2 * rows, half)])
    gathered = gather_over(gather_over(together, NARROW, narrow), OUTER, outer)
    basis_rows = gathered[:, :, : 2 * rows].reshape(outer, narrow, rows, states)
    state = gathered[:, :, 2 * rows :].reshape(outer, narrow, 2, rows, half)
    basis = by_core(basis_rows, swap_cores(basis_rows))
    basis = basis.transpose(1, 0, 2, 3, 4).reshape(states, states)
    own_built = build(basis, left_ops)
    other_built = swap_cores(own_built)

    mixed = mix(spread, right_rows, wide, narrow, pairs * rows)
    mixed = mixed.reshape(devices, 2 * pairs * rows, half)
    comp = lax.all_to_all(mixed, ALL, split_axis=0, concat_axis=0, tiled=True)
    comp = comp.reshape(devices, 2 * pairs, rows, half)

    step_size = 2.0 / math.sqrt(pair_total)
    core = own_core.reshape(1)
    for order_index in range(1, ORDER + 1):
        keep, send = apply_pairs(core, state, own_built, other_built, comp)
        partial = (keep + swap_cores(send).astype(F32)).astype(BF16)
        partial = partial.reshape(chips, 2 * rows, half)
        arrived = lax.all_to_all(partial, CHIPS, split_axis=0, concat_axis=0, tiled=True)
        term = jnp.sum(arrived.astype(F32), axis=0).reshape(2, rows, half)
        piece = (-(step_size / order_index) * local_mask * term).astype(BF16)
        summed = summed + piece.astype(F32)
        if order_index < ORDER:
            copies = jnp.broadcast_to(piece.reshape(1, 2 * rows, half), (chips, 2 * rows, half))
            state = lax.all_to_all(copies, CHIPS, split_axis=0, concat_axis=0, tiled=True)
            state = state.reshape(outer, narrow, 2, rows, half)

    mine = jnp.where(is_high, summed[1], summed[0])
    theirs = jnp.where(is_high, summed[0], summed[1])
    left, right = by_core(mine, swap_cores(theirs))
    return jnp.concatenate([left, right], axis=1)


def solution(mesh):
    wide, narrow = mesh.shape["wide"], mesh.shape["narrow"]
    finer = Mesh(mesh.devices.reshape(wide // 2, 2, narrow), ALL)
    placed = (
        P(ALL, None),
        P(ALL, None, None),
        P(ALL, None, None),
        P(),
        P(ALL, None),
        P(),
        P(),
    )
    return jax.shard_map(local, mesh=finer, in_specs=placed, out_specs=P(ALL, None), check_vma=False)
```

time: 665 us -> 187 us (0.28)
  waiting for transfers between devices: 435 us -> 68.6 us
  blocking collectives: 162 us -> 65.1 us
  matrix products: 18 us -> 0 us
  Pallas kernels: 0 us -> 16.4 us
  between operations: 13.3 us -> 0.36 us
  starting transfers between devices: 10.8 us -> 20.4 us
  local copies, waits for them, and re-layouts: 18.9 us -> 12.1 us
    psum x3 -> x0, waiting for transfers between devices: 387 us -> none  [local(): full_term = lax.psum(partial_term, ('wide', 'narrow'))]
    all_gather x2 -> x0, blocking collectives: 162 us -> none  [the longest x1 95.8 us: local(): lax.all_gather(site_basis, ('wide', 'narrow'), axis=0, tiled=True)]
    all_to_all x0 -> x5, blocking collectives: none -> 65.1 us  [the longest x3 40.1 us: local(): lax.all_to_all(partial, CHIPS, split_axis=0, concat_axis=0, tiled=True)]
    ppermute x0 -> x11, waiting for transfers between devices: none -> 41.2 us  [the longest x4 31.7 us: gather_over(): got = lax.ppermute(value, axis, [(i, i ^ step) for i in range(size)])]
    all_to_all x2, waiting for transfers between devices: 48.4 us -> 27.4 us  [the longest x1 27.4 us: local(): comp = lax.all_to_all(mixed, ALL, split_axis=0, concat_axis=0, tiled=True)]
    dot_general x9 -> x0, matrix products: 18 us -> none  [the longest x3 6 us: contract_joined(): lax.dot_general(left, right, (((1,), (1,)), ((), ())), preferred_element_...]
    pallas_call x0 -> x6, Pallas kernels: none -> 16.4 us  [the longest x1 5.98 us: mix(): pl.pallas_call(mix_kernel, grid=(wide,), in_specs=[pl.BlockSpec((height,...]
    ppermute x0 -> x11, starting transfers between devices: none -> 10.4 us  [the longest x4 9.48 us: gather_over(): got = lax.ppermute(value, axis, [(i, i ^ step) for i in range(size)])]
  transfers between devices with their start and end apart: 5 -> 13, of which waited for: 4 -> 9; matrix products, arithmetic and copies ran while one was open for 3% -> 3% of each run, Pallas kernels for 0% -> 6%
where the time goes in v1:
time: 187 us; the launch traced here: 186 us
  waiting for transfers between devices  68.6 us (37%)
  blocking collectives  65.1 us (35%)
  starting transfers between devices  20.4 us (11%)
  Pallas kernels  16.4 us (9%)
  local copies, waits for them, and re-layouts  12.1 us (6%)
  other arithmetic  2.91 us (2%)
    all_to_all x3, blocking collectives, local(): lax.all_to_all(partial, CHIPS, split_axis=0, concat_axis=0, tiled=True)  40.1 us
    ppermute x4, waiting for transfers between devices, gather_over(): got = lax.ppermute(value, axis, [(i, i ^ step) for i in range(size)])  31.7 us
    all_to_all x1, waiting for transfers between devices, local(): comp = lax.all_to_all(mixed, ALL, split_axis=0, concat_axis=0, tiled=True)  27.4 us
    all_to_all x2, blocking collectives, local(): lax.all_to_all(copies, CHIPS, split_axis=0, concat_axis=0, tiled=True)  25 us
    ppermute x4, starting transfers between devices, gather_over(): got = lax.ppermute(value, axis, [(i, i ^ step) for i in range(size)])  9.48 us
    ppermute x7, waiting for transfers between devices, swap_cores(): return lax.ppermute(value, CORE, [(0, 1), (1, 0)])  9.47 us
    all_to_all x1, starting transfers between devices, local(): lax.all_to_all(parts, ALL, split_axis=0, concat_axis=0, tiled=True)  7.3 us
    pallas_call x1, Pallas kernels, mix(): pl.pallas_call(mix_kernel, grid=(wide,), in_specs=[pl.BlockSpec((height,...  5.98 us
  transfers between devices with their start and end apart: 13, of which 9 were waited for; matrix products, arithmetic and copies ran while one was open for 3% of the time, Pallas kernels for 6%

profile of v1, /device:TPU:0, one launch (start us, length us, event | category | flops | bytes accessed | tf_op | source)
XLA Modules:
  0.0 185.8 jit_solution(1758035693946735947)
XLA Ops:
  0.0 2.7 %copy.45 = bf16[32,3,16,512]{3,2,1,0:T(8,128)(2,1)} copy(bf16[32,3,16,512]{3,2,0,1:T(8,128)(2,1)} %bitcast.103) | data formatting | bytes 3145728 | tf_op jit(solution)/shard_map/transpose | solution.py:227
  2.7 7.3 %all-to-all-start = ((bf16[32,48,512]{2,1,0:T(8,128)(2,1)}), bf16[32,48,512]{2,1,0:T(8,128)(2,1)S(1)}, u32[]{:S(2)}, u32[]{:S(2)}) async-start(bf16[32,48,512]{2,1,0:T(8,128)(2,1)} %bitcast.35), calls=%async_computation | async-start | bytes 3145728 | tf_op jit(solution)/shard_map/all_to_all | solution.py:229
  10.1 0.3 collective-permute-start
  10.4 0.2 reduce-window.8
  10.6 0.1 convert_reduce_fusion.3
  10.8 0.5 broadcast.78
  11.3 0.7 fusion.5
  12.0 0.1 sub.46
  12.2 1.7 collective-permute-start.1
  13.9 22.8 %collective-permute-done.1 = bf16[1,64,256]{2,1,0:T(8,128)(2,1)S(1)} collective-permute-done((bf16[1,64,256]{2,1,0:T(8,128)(2,1)S(1)}, bf16[1,64,256]{2,1,0:T(8,128)(2,1)S(1)}, u32[]{:S(2)}, u32[]{:S(2)}) %collective-permute-start.1) | collective-permute-done | bytes 32800 | tf_op jit(solution)/shard_map/ppermute | solution.py:47
  36.8 4.6 %collective-permute-start.2 = (bf16[2,1,64,256]{3,2,0,1:T(8,128)(2,1)S(1)}, bf16[2,1,64,256]{3,2,0,1:T(8,128)(2,1)S(1)}, u32[]{:S(2)}, u32[]{:S(2)}) collective-permute-start(bf16[2,1,64,256]{3,2,0,1:T(8,128)(2,1)S(1)} %fusion.3), channel_id=1, source_target_pairs={{0,4},{1,5},{2,6},{3,7},{4,0},{5,1},{6,2},{7,3},{8,12},{9,13},{10,... | collective-permute-start | bytes 196616 | tf_op jit(solution)/shard_map/ppermute | solution.py:47
  41.5 8.9 %collective-permute-done.2 = bf16[2,1,64,256]{3,2,0,1:T(8,128)(2,1)S(1)} collective-permute-done((bf16[2,1,64,256]{3,2,0,1:T(8,128)(2,1)S(1)}, bf16[2,1,64,256]{3,2,0,1:T(8,128)(2,1)S(1)}, u32[]{:S(2)}, u32[]{:S(2)}) %collective-permute-start.2) | collective-permute-done | bytes 65568 | tf_op jit(solution)/shard_map/ppermute | solution.py:47
  50.4 1.5 collective-permute-start.3
  52.0 0.1 broadcast_in_dim_reshape.12.col_pair_ref
  52.1 0.4 broadcast_in_dim_reshape.13.row_pair_ref
  52.5 2.7 %spread_mixing.1.spread_ref = bf16[1536,1536]{1,0:T(8,128)(2,1)S(1)} custom-call(s32[1536,1]{1,0:T(8,128)S(1)} %broadcast_in_dim_reshape.13.row_pair_ref, s32[1,1536]{1,0:T(1,128)S(1)} %broadcast_in_dim_reshape.12.col_pair_ref, bf16[96,96]{1,0:T(8,128)(2,1)S(1)} %copy-done.1), custom_call_target="tpu_custom_call" | custom-call | flops 452984832 | bytes 4718592 | tf_op jit(solution)/shard_map/spread_mixing/pallas_call | solution.py:104
  55.2 2.1 %copy-done = bf16[1536,1536]{1,0:T(8,128)(2,1)} copy-done((bf16[1536,1536]{1,0:T(8,128)(2,1)}, bf16[1536,1536]{1,0:T(8,128)(2,1)S(1)}, u32[]{:S(2)}) %copy-start) | copy-done | bytes 4718616
  57.5 1.6 collective-permute-start.4
  59.0 6.0 %mix.1 = bf16[2,2,8,2,48,256]{5,4,3,2,1,0:T(8,128)(2,1)} custom-call(bf16[1536,1536]{1,0:T(8,128)(2,1)} %copy-done, bf16[1536,512]{1,0:T(8,128)(2,1)S(1)} %bitcast.95), custom_call_target="tpu_custom_call" | custom-call | flops 2415919104 | bytes 4718592 | tf_op jit(solution)/shard_map/mix/pallas_call | solution.py:135
  65.0 2.7 %all-to-all-start.1 = ((bf16[32,96,256]{2,1,0:T(8,128)(2,1)}), bf16[32,96,256]{2,1,0:T(8,128)(2,1)S(1)}, u32[]{:S(2)}, u32[]{:S(2)}) async-start(bf16[32,96,256]{2,1,0:T(8,128)(2,1)} %bitcast.37), calls=%async_computation.1 | async-start | bytes 3145728 | tf_op jit(solution)/shard_map/all_to_all | solution.py:254
  67.8 0.7 fusion.6
  68.6 1.9 reshape.153
  70.4 0.1 collective-permute-start.5
  70.5 1.6 collective-permute-done.5
  72.2 1.0 select_bitcast_fusion.1
  73.2 2.4 %build.1.own_ref = bf16[3,512,512]{2,1,0:T(8,128)(2,1)S(1)} custom-call(bf16[512,512]{1,0:T(8,128)(2,1)S(1)} %bitcast.99, bf16[3,512,512]{2,1,0:T(8,128)(2,1)S(1)} %copy-done.2), custom_call_target="tpu_custom_call" | custom-call | flops 1610612736 | bytes 3145728 | tf_op jit(solution)/shard_map/build/pallas_call | solution.py:71
  75.6 0.2 collective-permute-start.6
  75.8 1.2 copy-done.3
  77.0 2.1 %collective-permute-done.6.other_ref = bf16[3,512,512]{2,1,0:T(8,128)(2,1)S(1)} collective-permute-done((bf16[3,512,512]{2,1,0:T(8,128)(2,1)S(1)}, bf16[3,512,512]{2,1,0:T(8,128)(2,1)S(1)}, u32[]{:S(2)}, u32[]{:S(2)}) %collective-permute-start.6) | collective-permute-done | bytes 1572896 | tf_op jit(solution)/shard_map/ppermute | solution.py:34
  79.1 27.4 %all-to-all-done.1 = bf16[32,96,256]{2,1,0:T(8,128)(2,1)S(1)} async-done(((bf16[32,96,256]{2,1,0:T(8,128)(2,1)}), bf16[32,96,256]{2,1,0:T(8,128)(2,1)S(1)}, u32[]{:S(2)}, u32[]{:S(2)}) %all-to-all-start.1) | async-done | bytes 1572896 | tf_op jit(solution)/shard_map/all_to_all | solution.py:254
  106.5 1.4 copy-done.4
  107.9 1.8 apply_pairs.3
  109.8 1.5 collective-permute-done.7
  111.3 0.1 add_convert_fusion.2
  111.4 13.4 %all_to_all.35 = bf16[16,32,256]{2,1,0:T(8,128)(2,1)S(1)} all-to-all(bf16[16,32,256]{2,1,0:T(8,128)(2,1)S(1)} %bitcast.106), channel_id=1, replica_groups=mesh['outer'=2,'core'=2,'narrow'=8] {'outer','narrow'}, dimensions={0} | all-to-all | bytes 524288 | tf_op jit(solution)/shard_map/all_to_all | solution.py:263
  125.0 12.5 %all_to_all.36 = bf16[16,32,256]{2,1,0:T(8,128)(2,1)S(1)} all-to-all(bf16[16,32,256]{2,1,0:T(8,128)(2,1)S(1)} %broadcast_in_dim.10), channel_id=1, replica_groups=mesh['outer'=2,'core'=2,'narrow'=8] {'outer','narrow'}, dimensions={0} | all-to-all | bytes 524288 | tf_op jit(solution)/shard_map/all_to_all | solution.py:269
  137.5 1.8 apply_pairs.4
  139.4 1.5 collective-permute-done.8
  140.9 0.1 add_convert_fusion.1
  141.0 13.3 %all_to_all.37 = bf16[16,32,256]{2,1,0:T(8,128)(2,1)S(1)} all-to-all(bf16[16,32,256]{2,1,0:T(8,128)(2,1)S(1)} %bitcast.107), channel_id=1, replica_groups=mesh['outer'=2,'core'=2,'narrow'=8] {'outer','narrow'}, dimensions={0} | all-to-all | bytes 524288 | tf_op jit(solution)/shard_map/all_to_all | solution.py:263
  154.5 12.5 %all_to_all.38 = bf16[16,32,256]{2,1,0:T(8,128)(2,1)S(1)} all-to-all(bf16[16,32,256]{2,1,0:T(8,128)(2,1)S(1)} %broadcast_in_dim.22), channel_id=1, replica_groups=mesh['outer'=2,'core'=2,'narrow'=8] {'outer','narrow'}, dimensions={0} | all-to-all | bytes 524288 | tf_op jit(solution)/shard_map/all_to_all | solution.py:269
  167.0 1.8 apply_pairs.5
  168.8 1.5 collective-permute-done.9
  170.4 0.1 add_convert_fusion
  170.5 13.3 %all_to_all.39 = bf16[16,32,256]{2,1,0:T(8,128)(2,1)S(1)} all-to-all(bf16[16,32,256]{2,1,0:T(8,128)(2,1)S(1)} %bitcast.108), channel_id=1, replica_groups=mesh['outer'=2,'core'=2,'narrow'=8] {'outer','narrow'}, dimensions={0} | all-to-all | bytes 524288 | tf_op jit(solution)/shard_map/all_to_all | solution.py:263
  183.8 0.1 convert_add_fusion
  184.0 1.2 collective-permute-done.10
  185.2 0.6 pad_maximum_fusion.3
  (54 shorter events, 1.2 us)
Async XLA Ops:
  2.7 7.3 %copy-start.5 = (bf16[16,512]{1,0:T(8,128)(2,1)S(1)}, bf16[16,512]{1,0:T(8,128)(2,1)}, u32[]{:S(2)}) copy-start(bf16[16,512]{1,0:T(8,128)(2,1)} %param.11) | copy-start | bytes 49156
  2.7 7.7 %copy-start.8 = (s32[8]{0:T(128)S(1)}, s32[8]{0:T(128)}, u32[]{:S(2)}) copy-start(s32[8]{0:T(128)} %param.13) | copy-start | bytes 100
  2.7 9.3 %copy-start.6 = (bf16[16,512]{1,0:T(8,128)(2,1)S(1)}, bf16[16,512]{1,0:T(8,128)(2,1)}, u32[]{:S(2)}) copy-start(bf16[16,512]{1,0:T(8,128)(2,1)} %param.7) | copy-start | bytes 49156
  2.7 49.2 %copy-start.7 = (s32[96]{0:T(128)S(1)}, s32[96]{0:T(128)}, u32[]{:S(2)}) copy-start(s32[96]{0:T(128)} %param.12) | copy-start | bytes 1156
  2.7 56.3 %all-to-all-start = ((bf16[32,48,512]{2,1,0:T(8,128)(2,1)}), bf16[32,48,512]{2,1,0:T(8,128)(2,1)S(1)}, u32[]{:S(2)}, u32[]{:S(2)}) async-start(bf16[32,48,512]{2,1,0:T(8,128)(2,1)} %bitcast.35), calls=%async_computation | async-start | bytes 3145728 | tf_op jit(solution)/shard_map/all_to_all | solution.py:229
  10.0 42.5 %copy-start.1 = (bf16[96,96]{1,0:T(8,128)(2,1)S(1)}, bf16[96,96]{1,0:T(8,128)(2,1)}, u32[]{:S(2)}) copy-start(bf16[96,96]{1,0:T(8,128)(2,1)} %integrals_ref.1) | copy-start | bytes 55300
  10.1 2.0 %collective-permute-start = (bf16[16,256]{1,0:T(8,128)(2,1)S(1)}, bf16[16,256]{1,0:T(8,128)(2,1)S(1)}, u32[]{:S(2)}, u32[]{:S(2)}) collective-permute-start(bf16[16,256]{1,0:T(8,128)(2,1)S(1)} %broadcast_select_fusion.1), channel_id=1, source_target_pairs={{0,8},{8,0},{1,9},{9,1},{2,10},{10,2},{3,11},{11,3},{4,12},{12,4},... | collective-permute-start | bytes 24584 | tf_op jit(solution)/shard_map/ppermute | solution.py:34
  12.2 24.6 %collective-permute-start.1 = (bf16[1,64,256]{2,1,0:T(8,128)(2,1)S(1)}, bf16[1,64,256]{2,1,0:T(8,128)(2,1)S(1)}, u32[]{:S(2)}, u32[]{:S(2)}) collective-permute-start(bf16[1,64,256]{2,1,0:T(8,128)(2,1)S(1)} %maximum_bitcast_fusion.2), channel_id=1, source_target_pairs={{0,2},{1,3},{2,0},{3,1},{4,6},{5,7},{6,4},{7,5},{8,10},{9,11},{10,... | collective-permute-start | bytes 98312 | tf_op jit(solution)/shard_map/ppermute | solution.py:47
  36.8 13.5 %collective-permute-start.2 = (bf16[2,1,64,256]{3,2,0,1:T(8,128)(2,1)S(1)}, bf16[2,1,64,256]{3,2,0,1:T(8,128)(2,1)S(1)}, u32[]{:S(2)}, u32[]{:S(2)}) collective-permute-start(bf16[2,1,64,256]{3,2,0,1:T(8,128)(2,1)S(1)} %fusion.3), channel_id=1, source_target_pairs={{0,4},{1,5},{2,6},{3,7},{4,0},{5,1},{6,2},{7,3},{8,12},{9,13},{10,... | collective-permute-start | bytes 196616 | tf_op jit(solution)/shard_map/ppermute | solution.py:47
  50.4 7.0 %collective-permute-start.3 = (bf16[2,2,1,64,256]{4,3,1,0,2:T(8,128)(2,1)S(1)}, bf16[2,2,1,64,256]{4,3,1,0,2:T(8,128)(2,1)S(1)}, u32[]{:S(2)}, u32[]{:S(2)}) collective-permute-start(bf16[2,2,1,64,256]{4,3,1,0,2:T(8,128)(2,1)S(1)} %fusion.1), channel_id=1, source_target_pairs={{0,1},{1,0},{2,3},{3,2},{4,5},{5,4},{6,7},{7,6},{8,9},{9,8},{10,11... | collective-permute-start | bytes 393224 | tf_op jit(solution)/shard_map/ppermute | solution.py:47
  55.2 2.1 %copy-start = (bf16[1536,1536]{1,0:T(8,128)(2,1)}, bf16[1536,1536]{1,0:T(8,128)(2,1)S(1)}, u32[]{:S(2)}) copy-start(bf16[1536,1536]{1,0:T(8,128)(2,1)S(1)} %spread_mixing.1.spread_ref) | copy-start | bytes 14155780
  57.5 10.2 %collective-permute-start.4 = (bf16[1,8,64,256]{3,2,1,0:T(8,128)(2,1)S(1)}, bf16[1,8,64,256]{3,2,1,0:T(8,128)(2,1)S(1)}, u32[]{:S(2)}, u32[]{:S(2)}) collective-permute-start(bf16[1,8,64,256]{3,2,1,0:T(8,128)(2,1)S(1)} %bitcast.104), channel_id=1, source_target_pairs={{0,16},{16,0},{1,17},{17,1},{2,18},{18,2},{3,19},{19,3},{4,20},{20... | collective-permute-start | bytes 786440 | tf_op jit(solution)/shard_map/ppermute | solution.py:47
  65.0 41.5 %all-to-all-start.1 = ((bf16[32,96,256]{2,1,0:T(8,128)(2,1)}), bf16[32,96,256]{2,1,0:T(8,128)(2,1)S(1)}, u32[]{:S(2)}, u32[]{:S(2)}) async-start(bf16[32,96,256]{2,1,0:T(8,128)(2,1)} %bitcast.37), calls=%async_computation.1 | async-start | bytes 3145728 | tf_op jit(solution)/shard_map/all_to_all | solution.py:254
  68.6 4.7 %copy-start.2 = (bf16[3,512,512]{2,1,0:T(8,128)(2,1)S(1)}, bf16[3,512,512]{2,1,0:T(8,128)(2,1)}, u32[]{:S(2)}) copy-start(bf16[3,512,512]{2,1,0:T(8,128)(2,1)} %left_ref.1) | copy-start | bytes 4718596
  70.4 1.7 collective-permute-start.5
  75.6 3.5 %collective-permute-start.6 = (bf16[3,512,512]{2,1,0:T(8,128)(2,1)S(1)}, bf16[3,512,512]{2,1,0:T(8,128)(2,1)S(1)}, u32[]{:S(2)}, u32[]{:S(2)}) collective-permute-start(bf16[3,512,512]{2,1,0:T(8,128)(2,1)S(1)} %build.1.own_ref), channel_id=1, source_target_pairs={{0,8},{8,0},{1,9},{9,1},{2,10},{10,2},{3,11},{11,3},{4,12},{12,4},... | collective-permute-start | bytes 4718600 | tf_op jit(solution)/shard_map/ppermute | solution.py:34
  75.8 1.2 copy-start.3
  106.5 1.4 copy-start.4
  109.7 1.6 collective-permute-start.7
  139.3 1.6 collective-permute-start.8
  168.8 1.6 collective-permute-start.9
  183.9 1.2 collective-permute-start.10

commit v2 on v1

v2 whole, which is shorter than its diff:
```python
import functools
import math

import jax
import jax.numpy as jnp
from jax import lax
from jax.experimental import pallas as pl
from jax.experimental.pallas import tpu as pltpu
from jax.sharding import Mesh, PartitionSpec as P

ORDER = 3
OUTER, CORE, FAR, NEAR = "outer", "core", "far", "near"
ALL = (OUTER, CORE, FAR, NEAR)
CHIPS = (OUTER, FAR, NEAR)
MIB = 1024 * 1024
LANES = 128
IN_HBM, IN_VMEM = pl.BlockSpec(memory_space=pltpu.HBM), pl.BlockSpec(memory_space=pltpu.VMEM)
F32, BF16 = jnp.float32, jnp.bfloat16


def whole_block(shape):
    return pl.BlockSpec(shape, lambda *_: (0,) * len(shape))


def kernel_params(mib):
    return pltpu.CompilerParams(vmem_limit_bytes=mib * MIB)


def block_ids(sector_sizes, count):
    ends = jnp.cumsum(sector_sizes)
    ids = jnp.arange(count, dtype=jnp.int32)
    return jnp.sum((ids[:, None] >= ends[None, :]).astype(jnp.int32), axis=1)


def swap_cores(value):
    return lax.ppermute(value, CORE, [(0, 1), (1, 0)])


def gather_over(value, axes, size):
    if size & (size - 1):
        return lax.all_gather(value, axes)
    position = lax.axis_index(axes)
    slots = [value]
    for k in range(1, size):
        slots.append(lax.ppermute(value, axes, [(i, i ^ k) for i in range(size)]))
    gathered = jnp.stack(slots)
    for bit in range(size.bit_length() - 1):
        pairs = gathered.reshape((-1, 2, 1 << bit) + value.shape)
        pairs = jnp.where((position >> bit) % 2 == 1, pairs[:, ::-1], pairs)
        gathered = pairs.reshape(gathered.shape)
    return gathered


def deal_kernel(right_ref, out_ref, held, in_sems, out_sems):
    pairs = held.shape[0]
    loads = [pltpu.make_async_copy(right_ref.at[s], held.at[s], in_sems.at[s]) for s in range(pairs)]
    stores = [
        pltpu.make_async_copy(held.at[s], out_ref.at[:, s], out_sems.at[s]) for s in range(pairs)
    ]
    for load in loads:
        load.start()
    for load, store in zip(loads, stores):
        load.wait()
        store.start()
    for store in stores:
        store.wait()


def deal_rows(right_ops, devices):
    pairs, states, _ = right_ops.shape
    rows = states // devices
    split = right_ops.reshape(pairs, devices, rows, states)
    if rows % 16:
        return split.transpose(1, 0, 2, 3)
    return pl.pallas_call(
        deal_kernel,
        in_specs=[IN_HBM],
        out_specs=IN_HBM,
        out_shape=jax.ShapeDtypeStruct((devices, pairs, rows, states), BF16),
        scratch_shapes=[
            pltpu.VMEM(split.shape, BF16),
            pltpu.SemaphoreType.DMA((pairs,)),
            pltpu.SemaphoreType.DMA((pairs,)),
        ],
        compiler_params=kernel_params(2),
        name="deal_rows",
    )(split)


def build_kernel(basis_ref, left_ref, built_ref):
    basis = basis_ref[...]
    rotated = jnp.dot(left_ref[0], basis, preferred_element_type=F32).astype(BF16)
    built = lax.dot_general(basis, rotated, (((0,), (0,)), ((), ())), preferred_element_type=F32)
    built_ref[0] = built.astype(BF16)


def build(basis, left_ops):
    pairs, states, _ = left_ops.shape
    return pl.pallas_call(
        build_kernel,
        grid=(pairs,),
        in_specs=[
            whole_block((states, states)),
            pl.BlockSpec((1, states, states), lambda s: (s, 0, 0)),
        ],
        out_specs=pl.BlockSpec((1, states, states), lambda s: (s, 0, 0)),
        out_shape=jax.ShapeDtypeStruct(left_ops.shape, BF16),
        compiler_params=kernel_params(12),
        cost_estimate=pl.CostEstimate(flops=0, bytes_accessed=0, transcendentals=0),
        name="build",
    )(basis, left_ops)


def mix_kernel(mixing_ref, right_ref, out_ref, taken, given, mixed, sems):
    total = mixing_ref.shape[0]
    wide, narrow, block, half = mixed.shape[1:]
    rows = right_ref.shape[0] // total
    lanes = half // LANES
    mixing = mixing_ref[...]
    stores = [
        pltpu.make_async_copy(mixed.at[h, w], out_ref.at[w // 2, h, :, w % 2], sems.at[h, w])
        for h in range(2)
        for w in range(wide)
    ]
    for h in range(2):
        places = range(h * lanes, (h + 1) * lanes)
        for place in places:
            taken[place] = right_ref[:, place * LANES : (place + 1) * LANES].astype(F32)
        for row in range(rows):
            every = pl.ds(row, total, stride=rows)
            one = jnp.concatenate([taken[place, every] for place in places], axis=1).astype(BF16)
            one = jnp.dot(mixing, one, preferred_element_type=F32)
            for lane, place in enumerate(places):
                given[place, every] = one[:, lane * LANES : (lane + 1) * LANES]
        for lane, place in enumerate(places):
            done = given[place].astype(BF16).reshape(wide, narrow, block, LANES)
            mixed[h, :, :, :, lane * LANES : (lane + 1) * LANES] = done
        for w in range(wide):
            stores[h * wide + w].start()
    for store in stores:
        store.wait()


def mix(mixing, right_rows, wide, narrow, block):
    size, states = right_rows.shape
    total = mixing.shape[0]
    half = states // 2
    if block % 16:
        mixed = jnp.einsum(
            "st,tx->sx", mixing, right_rows.reshape(total, -1), preferred_element_type=F32
        )
        mixed = mixed.astype(BF16).reshape(wide // 2, 2, narrow, block, 2, half)
        return mixed.transpose(0, 4, 2, 1, 3, 5)
    return pl.pallas_call(
        mix_kernel,
        in_specs=[IN_VMEM, IN_VMEM],
        out_specs=IN_HBM,
        out_shape=jax.ShapeDtypeStruct((wide // 2, 2, narrow, 2, block, half), BF16),
        scratch_shapes=[
            pltpu.VMEM((states // LANES, size, LANES), F32),
            pltpu.VMEM((states // LANES, size, LANES), F32),
            pltpu.VMEM((2, wide, narrow, block, half), BF16),
            pltpu.SemaphoreType.DMA((2, wide)),
        ],
        compiler_params=kernel_params(16),
        cost_estimate=pl.CostEstimate(flops=2 * size * total * states, bytes_accessed=4 * size * states, transcendentals=0),
        name="mix",
    )(mixing, right_rows)


def fetch_kernel(core_ref, state_ref, own_hbm, other_ref, comp_ref, keep_ref, send_ref, applied_ref, own_ref, sem):
    load = pltpu.make_async_copy(own_hbm, own_ref, sem)
    load.start()
    apply_kernel(core_ref, state_ref, own_ref, other_ref, comp_ref, keep_ref, send_ref, applied_ref, load)


def apply_kernel(core_ref, state_ref, own_ref, other_ref, comp_ref, keep_ref, send_ref, applied_ref, load=None):
    outer, narrow, _, rows, half = state_ref.shape
    pairs = own_ref.shape[0]
    chips = outer * narrow
    core = core_ref[0]
    state = jnp.concatenate(
        [state_ref[y, :, c].reshape(narrow * rows, half) for y in range(outer) for c in range(2)]
    )
    for side, ref in ((1, other_ref), (0, own_ref)):
        if side == 0 and load is not None:
            load.wait()
        for q in range(pairs):
            one = jnp.dot(ref[q], state, preferred_element_type=F32).astype(BF16)
            column = (side * pairs + q) * half
            applied_ref[:, column : column + half] = one
    applied = applied_ref[...]
    for out_ref, place in ((send_ref, 1 - core), (keep_ref, core)):
        columns = []
        for side in (core, 1 - core):
            for q in range(pairs):
                part = comp_ref[pl.ds(place * chips, chips), side * pairs + q]
                columns.append(part.reshape(chips * rows, half))
        joined = jnp.concatenate(columns, axis=1)
        term = lax.dot_general(applied, joined, (((1,), (1,)), ((), ())), preferred_element_type=F32)
        term = term.astype(out_ref.dtype).reshape(outer, 2, narrow, rows, half)
        for c in range(2):
            out_ref[:, :, c] = term[:, c]


def apply_pairs(core, state, own, other, comp, fetch):
    outer, narrow, _, rows, half = state.shape
    pairs, states, _ = own.shape
    if rows % 16:
        full = state.transpose(0, 2, 1, 3, 4).reshape(states, half)
        built = jnp.concatenate([own, other])
        applied = jnp.einsum("sil,lk->sik", built, full, preferred_element_type=F32).astype(BF16)
        joined = comp.transpose(1, 0, 2, 3).reshape(2, pairs, states, half)
        joined = jnp.concatenate([joined[core[0]], joined[1 - core[0]]])
        term = jnp.einsum("sik,sjk->ij", applied, joined, preferred_element_type=F32)
        term = term.reshape(outer, 2, narrow, rows, 2, half).transpose(4, 0, 2, 1, 3, 5)
        return term[core[0]], term[1 - core[0]].astype(BF16)
    scratch = [pltpu.VMEM((states, 2 * pairs * half), BF16)]
    if fetch:
        scratch += [pltpu.VMEM(own.shape, BF16), pltpu.SemaphoreType.DMA]
    return pl.pallas_call(
        fetch_kernel if fetch else apply_kernel,
        in_specs=[pl.BlockSpec(memory_space=pltpu.SMEM), IN_VMEM, IN_HBM if fetch else IN_VMEM, IN_VMEM, IN_VMEM],
        out_specs=[IN_VMEM] * 2,
        out_shape=[
            jax.ShapeDtypeStruct(state.shape, F32),
            jax.ShapeDtypeStruct(state.shape, BF16),
        ],
        scratch_shapes=scratch,
        compiler_params=kernel_params(58 if fetch else 12),
        cost_estimate=pl.CostEstimate(
            flops=8 * pairs * states**2 * half, bytes_accessed=8 * pairs * states**2, transcendentals=0
        ),
        name="apply_pairs",
    )(core, state, own, other, comp)


def local(site_basis, left_ops, right_ops, integrals, wavefunction, pair_order, sector_sizes):
    outer, far, near = (lax.axis_size(name) for name in CHIPS)
    narrow = far * near
    wide = 2 * outer
    devices = wide * narrow
    rows, states = wavefunction.shape
    half = states // 2
    pairs = left_ops.shape[0]
    pair_total = integrals.shape[0]
    chips = outer * narrow
    own_outer, own_core, own_narrow = (lax.axis_index(name) for name in (OUTER, CORE, (FAR, NEAR)))
    is_high = own_core == 1

    def own_half(value):
        return jnp.where(is_high, value[..., half:], value[..., :half])

    def other_half(value):
        return jnp.where(is_high, value[..., :half], value[..., half:])

    def by_core(own, other):
        return jnp.stack([jnp.where(is_high, other, own), jnp.where(is_high, own, other)])

    parts = deal_rows(right_ops, devices).reshape(devices, pairs * rows, states)
    parts, wavefunction, site_basis = lax.optimization_barrier((parts, wavefunction, site_basis))
    right_rows = lax.all_to_all(parts, ALL, split_axis=0, concat_axis=0, tiled=True)
    right_rows = right_rows.reshape(pair_total * rows, states)
    mixing = jnp.take(jnp.take(integrals, pair_order, axis=0), pair_order, axis=1)

    blocks = block_ids(sector_sizes, states).astype(F32)
    by_device = blocks.reshape(outer, 2, narrow, rows)
    chip_rows = lax.dynamic_slice(by_device, (own_outer, 0, own_narrow, 0), (1, 2, 1, rows)).reshape(2, rows)
    own_columns = own_half(blocks)
    local_mask = (jnp.abs(chip_rows[:, :, None] - own_columns[None, None, :]) <= 2.0).astype(F32)

    piece = by_core(own_half(wavefunction), swap_cores(other_half(wavefunction)))
    piece = (piece.astype(F32) * local_mask).astype(BF16)
    summed = piece.astype(F32)

    together = jnp.concatenate([site_basis.reshape(rows * 2, half), piece.reshape(2 * rows, half)])
    mixed = mix(mixing, right_rows, wide, narrow, pairs * rows)
    gathered, mixed = lax.optimization_barrier((gather_over(together, FAR, far), mixed))
    gathered = gather_over(gathered, (OUTER, NEAR), outer * near)
    gathered = gathered.reshape(outer, near, far, 4 * rows, half).transpose(0, 2, 1, 3, 4)
    basis_rows = gathered[..., : 2 * rows, :].reshape(outer, narrow, rows, states)
    state = gathered[..., 2 * rows :, :].reshape(outer, narrow, 2, rows, half)
    basis = by_core(basis_rows, swap_cores(basis_rows))
    basis = basis.transpose(1, 0, 2, 3, 4).reshape(states, states)
    own_built = build(basis, left_ops)
    other_built = swap_cores(own_built)

    mixed = mixed.reshape(devices, 2 * pairs * rows, half)
    comp = lax.all_to_all(mixed, ALL, split_axis=0, concat_axis=0, tiled=True)
    comp = comp.reshape(devices, 2 * pairs, rows, half)

    step_size = 2.0 / math.sqrt(pair_total)
    core = own_core.reshape(1)
    for order_index in range(1, ORDER + 1):
        keep, send = apply_pairs(core, state, own_built, other_built, comp, False)
        partial = (keep + swap_cores(send).astype(F32)).astype(BF16)
        partial = partial.reshape(chips, 2 * rows, half)
        arrived = lax.all_to_all(partial, CHIPS, split_axis=0, concat_axis=0, tiled=True)
        term = jnp.sum(arrived.astype(F32), axis=0).reshape(2, rows, half)
        piece = (-(step_size / order_index) * local_mask * term).astype(BF16)
        summed = summed + piece.astype(F32)
        if order_index < ORDER:
            copies = jnp.broadcast_to(piece.reshape(1, 2 * rows, half), (chips, 2 * rows, half))
            state = lax.all_to_all(copies, CHIPS, split_axis=0, concat_axis=0, tiled=True)
            state = state.reshape(outer, narrow, 2, rows, half)

    mine = jnp.where(is_high, summed[1], summed[0])
    theirs = jnp.where(is_high, summed[0], summed[1])
    left, right = by_core(mine, swap_cores(theirs))
    return jnp.concatenate([left, right], axis=1)


def solution(mesh):
    wide, narrow = mesh.shape["wide"], mesh.shape["narrow"]
    near = math.gcd(narrow, 2)
    finer = Mesh(mesh.devices.reshape(wide // 2, 2, narrow // near, near), ALL)
    placed = (
        P(ALL, None),
        P(ALL, None, None),
        P(ALL, None, None),
        P(),
        P(ALL, None),
        P(),
        P(),
    )
    return jax.shard_map(local, mesh=finer, in_specs=placed, out_specs=P(ALL, None), check_vma=False)
```

time: 187 us -> 179 us (0.957)
  local copies, waits for them, and re-layouts: 12.1 us -> 7.87 us
  Pallas kernels: 16.4 us -> 12.5 us
  waiting for transfers between devices: 68.6 us -> 71.3 us
    pallas_call x5, Pallas kernels: 14 us -> 10.1 us  [the longest x3 5.37 us: apply_pairs(): pl.pallas_call(fetch_kernel if fetch else apply_kernel, in_specs=[pl.Bloc...]
    transpose x2 -> x1, local copies, waits for them, and re-layouts: 2.74 us -> 0.04 us  [local(): basis = basis.transpose(1, 0, 2, 3, 4).reshape(states, states)]
    ppermute x4 -> x6, waiting for transfers between devices: 31.7 us -> 34.3 us  [gather_over(): slots.append(lax.ppermute(value, axes, [(i, i ^ k) for i in range(size)]))]
    ppermute x4 -> x6, starting transfers between devices: 9.48 us -> 8.01 us  [gather_over(): slots.append(lax.ppermute(value, axes, [(i, i ^ k) for i in range(size)]))]
    unnamed x18 -> x20, local copies, waits for them, and re-layouts: 4.73 us -> 4 us
  transfers between devices with their start and end apart: 13 -> 15, of which waited for: 9 -> 11; matrix products, arithmetic and copies ran while one was open for 3% -> 3% of each run, Pallas kernels for 6% -> 1%
where the time goes in v2:
time: 179 us
  waiting for transfers between devices  71.3 us (40%)
  blocking collectives  65.2 us (36%)
  starting transfers between devices  19.3 us (11%)
  Pallas kernels  12.5 us (7%)
  local copies, waits for them, and re-layouts  7.87 us (4%)
  other arithmetic  2.16 us (1%)
    all_to_all x3, blocking collectives, local(): lax.all_to_all(partial, CHIPS, split_axis=0, concat_axis=0, tiled=True)  40.2 us
    ppermute x6, waiting for transfers between devices, gather_over(): slots.append(lax.ppermute(value, axes, [(i, i ^ k) for i in range(size)]))  34.3 us
    all_to_all x1, waiting for transfers between devices, local(): comp = lax.all_to_all(mixed, ALL, split_axis=0, concat_axis=0, tiled=True)  26.3 us
    all_to_all x2, blocking collectives, local(): lax.all_to_all(copies, CHIPS, split_axis=0, concat_axis=0, tiled=True)  25 us
    ppermute x7, waiting for transfers between devices, swap_cores(): return lax.ppermute(value, CORE, [(0, 1), (1, 0)])  10.5 us
    ppermute x6, starting transfers between devices, gather_over(): slots.append(lax.ppermute(value, axes, [(i, i ^ k) for i in range(size)]))  8.01 us
    all_to_all x1, starting transfers between devices, local(): lax.all_to_all(parts, ALL, split_axis=0, concat_axis=0, tiled=True)  7.3 us
    pallas_call x3, Pallas kernels, apply_pairs(): pl.pallas_call(fetch_kernel if fetch else apply_kernel, in_specs=[pl.Bloc...  5.37 us
  transfers between devices with their start and end apart: 15, of which 11 were waited for; matrix products, arithmetic and copies ran while one was open for 3% of the time, Pallas kernels for 1%

profile of v2, /device:TPU:0, one launch (start us, length us, event | category | flops | bytes accessed | tf_op | source)
XLA Modules:
  0.0 178.7 jit_solution(2259483650586859262)
XLA Ops:
  0.0 1.4 copy-done.2
  1.4 1.3 deal_rows.1
  2.8 7.3 %all-to-all-start = ((bf16[32,48,512]{2,1,0:T(8,128)(2,1)}), bf16[32,48,512]{2,1,0:T(8,128)(2,1)S(1)}, u32[]{:S(2)}, u32[]{:S(2)}) async-start(bf16[32,48,512]{2,1,0:T(8,128)(2,1)} %bitcast.4), calls=%async_computation | async-start | bytes 3145728 | tf_op jit(solution)/shard_map/all_to_all | solution.py:262
  10.1 0.3 collective-permute-start
  10.5 0.2 reduce-window.8
  10.8 0.7 gather_fusion
  11.5 0.1 copy.20
  11.7 0.6 broadcast.88
  12.2 0.6 fusion.5
  13.0 0.7 gather_fusion.1
  13.6 0.1 copy.21
  13.9 2.7 %collective-permute-start.2 = (bf16[64,256]{1,0:T(8,128)(2,1)S(1)}, bf16[64,256]{1,0:T(8,128)(2,1)S(1)}, u32[]{:S(2)}, u32[]{:S(2)}) collective-permute-start(bf16[64,256]{1,0:T(8,128)(2,1)S(1)} %get-tuple-element.36), channel_id=1, source_target_pairs={{0,4},{2,6},{4,0},{6,2},{1,5},{3,7},{5,1},{7,3},{8,12},{10,14},{12... | collective-permute-start | bytes 98312 | tf_op jit(solution)/shard_map/ppermute | solution.py:45
  16.6 1.5 collective-permute-start.1
  18.1 0.3 collective-permute-start.3
  18.4 31.7 %collective-permute-done.2 = bf16[64,256]{1,0:T(8,128)(2,1)S(1)} collective-permute-done((bf16[64,256]{1,0:T(8,128)(2,1)S(1)}, bf16[64,256]{1,0:T(8,128)(2,1)S(1)}, u32[]{:S(2)}, u32[]{:S(2)}) %collective-permute-start.2) | collective-permute-done | bytes 32800 | tf_op jit(solution)/shard_map/ppermute | solution.py:45
  50.1 0.2 all-to-all-done
  50.3 3.4 %mix.1 = bf16[2,2,8,2,48,256]{5,4,3,2,1,0:T(8,128)(2,1)} custom-call(bf16[96,96]{1,0:T(8,128)(2,1)S(1)} %select_bitcast_fusion.2.mixing_ref, bf16[1536,512]{1,0:T(8,128)(2,1)S(1)} %bitcast.62), custom_call_target="tpu_custom_call" | custom-call | flops 150994944 | bytes 3145728 | tf_op jit(solution)/shard_map/mix/pallas_call | solution.py:154
  53.8 2.3 %collective-permute-start.6 = (bf16[4,64,256]{2,1,0:T(8,128)(2,1)S(1)}, bf16[4,64,256]{2,1,0:T(8,128)(2,1)S(1)}, u32[]{:S(2)}, u32[]{:S(2)}) collective-permute-start(bf16[4,64,256]{2,1,0:T(8,128)(2,1)S(1)} %bitcast.76), channel_id=1, source_target_pairs={{0,17},{1,16},{16,1},{17,0},{2,19},{3,18},{18,3},{19,2},{4,21},{5,... | collective-permute-start | bytes 393224 | tf_op jit(solution)/shard_map/ppermute | solution.py:45
  56.0 0.5 collective-permute-start.5
  56.6 0.8 collective-permute-start.4
  57.3 3.1 %all-to-all-start.1 = ((bf16[32,96,256]{2,1,0:T(8,128)(2,1)}), bf16[32,96,256]{2,1,0:T(8,128)(2,1)S(1)}, u32[]{:S(2)}, u32[]{:S(2)}) async-start(bf16[32,96,256]{2,1,0:T(8,128)(2,1)} %bitcast.32), calls=%async_computation.1 | async-start | bytes 3145728 | tf_op jit(solution)/shard_map/all_to_all | solution.py:289
  60.4 0.7 collective-permute-done.6
  61.1 1.9 %collective-permute-done.5 = bf16[4,64,256]{2,1,0:T(8,128)(2,1)S(1)} collective-permute-done((bf16[4,64,256]{2,1,0:T(8,128)(2,1)S(1)}, bf16[4,64,256]{2,1,0:T(8,128)(2,1)S(1)}, u32[]{:S(2)}, u32[]{:S(2)}) %collective-permute-start.5) | collective-permute-done | bytes 131104 | tf_op jit(solution)/shard_map/ppermute | solution.py:45
  63.1 0.1 fusion
  63.2 0.1 fusion.1
  63.4 0.7 fusion.6
  64.3 1.5 collective-permute-done.7
  66.0 2.4 %build.1.own_ref = bf16[3,512,512]{2,1,0:T(8,128)(2,1)S(1)} custom-call(bf16[512,512]{1,0:T(8,128)(2,1)S(1)} %bitcast.63, bf16[3,512,512]{2,1,0:T(8,128)(2,1)S(1)} %copy-done.1), custom_call_target="tpu_custom_call" | custom-call | tf_op jit(solution)/shard_map/build/pallas_call | solution.py:99
  68.4 0.2 collective-permute-start.8
  68.6 3.3 %collective-permute-done.8.other_ref = bf16[3,512,512]{2,1,0:T(8,128)(2,1)S(1)} collective-permute-done((bf16[3,512,512]{2,1,0:T(8,128)(2,1)S(1)}, bf16[3,512,512]{2,1,0:T(8,128)(2,1)S(1)}, u32[]{:S(2)}, u32[]{:S(2)}) %collective-permute-start.8) | collective-permute-done | bytes 1572896 | tf_op jit(solution)/shard_map/ppermute | solution.py:36
  71.9 1.1 copy-done.3
  73.0 26.3 %all-to-all-done.1 = bf16[32,96,256]{2,1,0:T(8,128)(2,1)S(1)} async-done(((bf16[32,96,256]{2,1,0:T(8,128)(2,1)}), bf16[32,96,256]{2,1,0:T(8,128)(2,1)S(1)}, u32[]{:S(2)}, u32[]{:S(2)}) %all-to-all-start.1) | async-done | bytes 1572896 | tf_op jit(solution)/shard_map/all_to_all | solution.py:289
  99.3 1.4 copy-done.4
  100.7 1.8 %apply_pairs.3 = (f32[2,8,2,16,256]{4,3,2,1,0:T(8,128)S(1)}, bf16[2,8,2,16,256]{4,3,2,1,0:T(8,128)(2,1)S(1)}) custom-call(s32[1]{0:T(128)} %bitcast.7.core_ref, bf16[2,8,2,16,256]{4,3,2,1,0:T(8,128)(2,1)S(1)} %bitcast.68, bf16[3,512,512]{2,1,0:T(8,128)(2,1)S(1)} %build.1.own_ref, bf16[3,512,512]{2,1,0:T(8,128)(2,1)S(1)} %copy-done.4, ...), custom_call_target="tpu_custom_call" | custom-call | flops 1610612736 | bytes 6291456 | tf_op jit(solution)/shard_map/apply_pairs/pallas_call | solution.py:221
  102.6 1.5 collective-permute-done.9
  104.1 0.1 add_convert_fusion.2
  104.2 13.5 %all_to_all.35 = bf16[16,32,256]{2,1,0:T(8,128)(2,1)S(1)} all-to-all(bf16[16,32,256]{2,1,0:T(8,128)(2,1)S(1)} %bitcast.72), channel_id=1, replica_groups=mesh['outer'=2,'core'=2,'far'=4,'near'=2] {'outer','far','near'}, dimensions={0} | all-to-all | bytes 524288 | tf_op jit(solution)/shard_map/all_to_all | solution.py:298
  117.9 12.5 %all_to_all.36 = bf16[16,32,256]{2,1,0:T(8,128)(2,1)S(1)} all-to-all(bf16[16,32,256]{2,1,0:T(8,128)(2,1)S(1)} %broadcast_in_dim.37), channel_id=1, replica_groups=mesh['outer'=2,'core'=2,'far'=4,'near'=2] {'outer','far','near'}, dimensions={0} | all-to-all | bytes 524288 | tf_op jit(solution)/shard_map/all_to_all | solution.py:304
  130.4 1.8 %apply_pairs.4 = (f32[2,8,2,16,256]{4,3,2,1,0:T(8,128)S(1)}, bf16[2,8,2,16,256]{4,3,2,1,0:T(8,128)(2,1)S(1)}) custom-call(s32[1]{0:T(128)} %bitcast.7.core_ref, bf16[2,8,2,16,256]{4,3,2,1,0:T(8,128)(2,1)S(1)} %bitcast.70, bf16[3,512,512]{2,1,0:T(8,128)(2,1)S(1)} %build.1.own_ref, bf16[3,512,512]{2,1,0:T(8,128)(2,1)S(1)} %copy-done.4, ...), custom_call_target="tpu_custom_call" | custom-call | flops 1610612736 | bytes 6291456 | tf_op jit(solution)/shard_map/apply_pairs/pallas_call | solution.py:221
  132.2 1.5 collective-permute-done.10
  133.9 13.3 %all_to_all.37 = bf16[16,32,256]{2,1,0:T(8,128)(2,1)S(1)} all-to-all(bf16[16,32,256]{2,1,0:T(8,128)(2,1)S(1)} %bitcast.73), channel_id=1, replica_groups=mesh['outer'=2,'core'=2,'far'=4,'near'=2] {'outer','far','near'}, dimensions={0} | all-to-all | bytes 524288 | tf_op jit(solution)/shard_map/all_to_all | solution.py:298
  147.3 12.5 %all_to_all.38 = bf16[16,32,256]{2,1,0:T(8,128)(2,1)S(1)} all-to-all(bf16[16,32,256]{2,1,0:T(8,128)(2,1)S(1)} %broadcast_in_dim.38), channel_id=1, replica_groups=mesh['outer'=2,'core'=2,'far'=4,'near'=2] {'outer','far','near'}, dimensions={0} | all-to-all | bytes 524288 | tf_op jit(solution)/shard_map/all_to_all | solution.py:304
  159.8 1.8 %apply_pairs.5 = (f32[2,8,2,16,256]{4,3,2,1,0:T(8,128)S(1)}, bf16[2,8,2,16,256]{4,3,2,1,0:T(8,128)(2,1)S(1)}) custom-call(s32[1]{0:T(128)} %bitcast.7.core_ref, bf16[2,8,2,16,256]{4,3,2,1,0:T(8,128)(2,1)S(1)} %bitcast.69, bf16[3,512,512]{2,1,0:T(8,128)(2,1)S(1)} %build.1.own_ref, bf16[3,512,512]{2,1,0:T(8,128)(2,1)S(1)} %copy-done.4, ...), custom_call_target="tpu_custom_call" | custom-call | flops 1610612736 | bytes 6291456 | tf_op jit(solution)/shard_map/apply_pairs/pallas_call | solution.py:221
  161.7 1.5 collective-permute-done.11
  163.3 13.3 %all_to_all.39 = bf16[16,32,256]{2,1,0:T(8,128)(2,1)S(1)} all-to-all(bf16[16,32,256]{2,1,0:T(8,128)(2,1)S(1)} %bitcast.74), channel_id=1, replica_groups=mesh['outer'=2,'core'=2,'far'=4,'near'=2] {'outer','far','near'}, dimensions={0} | all-to-all | bytes 524288 | tf_op jit(solution)/shard_map/all_to_all | solution.py:298
  176.7 0.1 convert_add_fusion
  176.9 1.2 collective-permute-done.12
  178.1 0.6 pad_maximum_fusion.3
  (63 shorter events, 1.7 us)
Async XLA Ops:
  0.0 10.8 %copy-start = (bf16[96,96]{1,0:T(8,128)(2,1)S(1)}, bf16[96,96]{1,0:T(8,128)(2,1)}, u32[]{:S(2)}) copy-start(bf16[96,96]{1,0:T(8,128)(2,1)} %param.10) | copy-start | bytes 55300
  0.0 1.4 copy-start.2
  2.7 7.4 %copy-start.6 = (bf16[16,512]{1,0:T(8,128)(2,1)S(1)}, bf16[16,512]{1,0:T(8,128)(2,1)}, u32[]{:S(2)}) copy-start(bf16[16,512]{1,0:T(8,128)(2,1)} %param.11) | copy-start | bytes 49156
  2.8 7.7 %copy-start.8 = (s32[8]{0:T(128)S(1)}, s32[8]{0:T(128)}, u32[]{:S(2)}) copy-start(s32[8]{0:T(128)} %param.13) | copy-start | bytes 100
  2.8 8.0 %copy-start.9 = (s32[96]{0:T(128)S(1)}, s32[96]{0:T(128)}, u32[]{:S(2)}) copy-start(s32[96]{0:T(128)} %param.12) | copy-start | bytes 1156
  2.8 11.0 %copy-start.7 = (bf16[16,512]{1,0:T(8,128)(2,1)S(1)}, bf16[16,512]{1,0:T(8,128)(2,1)}, u32[]{:S(2)}) copy-start(bf16[16,512]{1,0:T(8,128)(2,1)} %param.7) | copy-start | bytes 49156
  2.8 47.5 %all-to-all-start = ((bf16[32,48,512]{2,1,0:T(8,128)(2,1)}), bf16[32,48,512]{2,1,0:T(8,128)(2,1)S(1)}, u32[]{:S(2)}, u32[]{:S(2)}) async-start(bf16[32,48,512]{2,1,0:T(8,128)(2,1)} %bitcast.4), calls=%async_computation | async-start | bytes 3145728 | tf_op jit(solution)/shard_map/all_to_all | solution.py:262
  10.1 3.6 %collective-permute-start = (bf16[16,256]{1,0:T(8,128)(2,1)S(1)}, bf16[16,256]{1,0:T(8,128)(2,1)S(1)}, u32[]{:S(2)}, u32[]{:S(2)}) collective-permute-start(bf16[16,256]{1,0:T(8,128)(2,1)S(1)} %broadcast_select_fusion.2), channel_id=1, source_target_pairs={{0,8},{8,0},{1,9},{9,1},{2,10},{10,2},{3,11},{11,3},{4,12},{12,4},... | collective-permute-start | bytes 24584 | tf_op jit(solution)/shard_map/ppermute | solution.py:36
  13.9 36.1 %collective-permute-start.2 = (bf16[64,256]{1,0:T(8,128)(2,1)S(1)}, bf16[64,256]{1,0:T(8,128)(2,1)S(1)}, u32[]{:S(2)}, u32[]{:S(2)}) collective-permute-start(bf16[64,256]{1,0:T(8,128)(2,1)S(1)} %get-tuple-element.36), channel_id=1, source_target_pairs={{0,4},{2,6},{4,0},{6,2},{1,5},{3,7},{5,1},{7,3},{8,12},{10,14},{12... | collective-permute-start | bytes 98312 | tf_op jit(solution)/shard_map/ppermute | solution.py:45
  16.6 33.5 %collective-permute-start.1 = (bf16[64,256]{1,0:T(8,128)(2,1)S(1)}, bf16[64,256]{1,0:T(8,128)(2,1)S(1)}, u32[]{:S(2)}, u32[]{:S(2)}) collective-permute-start(bf16[64,256]{1,0:T(8,128)(2,1)S(1)} %get-tuple-element.36), channel_id=1, source_target_pairs={{0,2},{2,0},{4,6},{6,4},{1,3},{3,1},{5,7},{7,5},{8,10},{10,8},{12,... | collective-permute-start | bytes 98312 | tf_op jit(solution)/shard_map/ppermute | solution.py:45
  18.1 32.0 %collective-permute-start.3 = (bf16[64,256]{1,0:T(8,128)(2,1)S(1)}, bf16[64,256]{1,0:T(8,128)(2,1)S(1)}, u32[]{:S(2)}, u32[]{:S(2)}) collective-permute-start(bf16[64,256]{1,0:T(8,128)(2,1)S(1)} %get-tuple-element.36), channel_id=1, source_target_pairs={{0,6},{2,4},{4,2},{6,0},{1,7},{3,5},{5,3},{7,1},{8,14},{10,12},{12... | collective-permute-start | bytes 98312 | tf_op jit(solution)/shard_map/ppermute | solution.py:45
  53.8 7.4 %collective-permute-start.6 = (bf16[4,64,256]{2,1,0:T(8,128)(2,1)S(1)}, bf16[4,64,256]{2,1,0:T(8,128)(2,1)S(1)}, u32[]{:S(2)}, u32[]{:S(2)}) collective-permute-start(bf16[4,64,256]{2,1,0:T(8,128)(2,1)S(1)} %bitcast.76), channel_id=1, source_target_pairs={{0,17},{1,16},{16,1},{17,0},{2,19},{3,18},{18,3},{19,2},{4,21},{5,... | collective-permute-start | bytes 393224 | tf_op jit(solution)/shard_map/ppermute | solution.py:45
  56.0 7.0 %collective-permute-start.5 = (bf16[4,64,256]{2,1,0:T(8,128)(2,1)S(1)}, bf16[4,64,256]{2,1,0:T(8,128)(2,1)S(1)}, u32[]{:S(2)}, u32[]{:S(2)}) collective-permute-start(bf16[4,64,256]{2,1,0:T(8,128)(2,1)S(1)} %bitcast.77), channel_id=1, source_target_pairs={{0,16},{1,17},{16,0},{17,1},{2,18},{3,19},{18,2},{19,3},{4,20},{5,... | collective-permute-start | bytes 393224 | tf_op jit(solution)/shard_map/ppermute | solution.py:45
  56.6 6.5 %collective-permute-start.4 = (bf16[4,64,256]{2,1,0:T(8,128)(2,1)S(1)}, bf16[4,64,256]{2,1,0:T(8,128)(2,1)S(1)}, u32[]{:S(2)}, u32[]{:S(2)}) collective-permute-start(bf16[4,64,256]{2,1,0:T(8,128)(2,1)S(1)} %bitcast.78), channel_id=1, source_target_pairs={{0,1},{1,0},{16,17},{17,16},{2,3},{3,2},{18,19},{19,18},{4,5},{5,4... | collective-permute-start | bytes 393224 | tf_op jit(solution)/shard_map/ppermute | solution.py:45
  57.3 42.0 %all-to-all-start.1 = ((bf16[32,96,256]{2,1,0:T(8,128)(2,1)}), bf16[32,96,256]{2,1,0:T(8,128)(2,1)S(1)}, u32[]{:S(2)}, u32[]{:S(2)}) async-start(bf16[32,96,256]{2,1,0:T(8,128)(2,1)} %bitcast.32), calls=%async_computation.1 | async-start | bytes 3145728 | tf_op jit(solution)/shard_map/all_to_all | solution.py:289
  64.2 1.8 copy-start.1
  64.2 1.6 collective-permute-start.7
  66.0 2.6 %copy-start.5 = (bf16[2,4,2,32,256]{4,3,1,2,0:T(8,128)(2,1)S(1)}, bf16[2,4,2,32,256]{4,3,1,2,0:T(8,128)(2,1)}, u32[]{:S(2)}) copy-start(bf16[2,4,2,32,256]{4,3,1,2,0:T(8,128)(2,1)} %get-tuple-element.32) | copy-start | bytes 786436
  68.4 3.5 %collective-permute-start.8 = (bf16[3,512,512]{2,1,0:T(8,128)(2,1)S(1)}, bf16[3,512,512]{2,1,0:T(8,128)(2,1)S(1)}, u32[]{:S(2)}, u32[]{:S(2)}) collective-permute-start(bf16[3,512,512]{2,1,0:T(8,128)(2,1)S(1)} %build.1.own_ref), channel_id=1, source_target_pairs={{0,8},{8,0},{1,9},{9,1},{2,10},{10,2},{3,11},{11,3},{4,12},{12,4},... | collective-permute-start | bytes 4718600 | tf_op jit(solution)/shard_map/ppermute | solution.py:36
  71.9 1.1 copy-start.3
  99.3 1.4 copy-start.4
  102.5 1.6 collective-permute-start.9
  132.2 1.6 collective-permute-start.10
  161.6 1.6 collective-permute-start.11
  176.8 1.2 collective-permute-start.12

commit v3 on v2

--- a/solution.py
+++ b/solution.py
@@ -36,26 +36,55 @@
     return lax.ppermute(value, CORE, [(0, 1), (1, 0)])
 
 
-def gather_over(value, axes, size):
+def partner(position, k, size):
     if size & (size - 1):
-        return lax.all_gather(value, axes)
-    position = lax.axis_index(axes)
+        return (position + k) % size
+    return position ^ k
+
+
+def send_round(value, axes, size):
     slots = [value]
     for k in range(1, size):
-        slots.append(lax.ppermute(value, axes, [(i, i ^ k) for i in range(size)]))
-    gathered = jnp.stack(slots)
-    for bit in range(size.bit_length() - 1):
-        pairs = gathered.reshape((-1, 2, 1 << bit) + value.shape)
-        pairs = jnp.where((position >> bit) % 2 == 1, pairs[:, ::-1], pairs)
-        gathered = pairs.reshape(gathered.shape)
-    return gathered
+        slots.append(lax.ppermute(value, axes, [(partner(i, k, size), i) for i in range(size)]))
+    return slots
+
+
+def place_kernel(place_ref, *refs):
+    slots, (basis_ref, state_ref) = refs[:-2], refs[-2:]
+    outer, _, far, near, _, _ = basis_ref.shape
+    half = state_ref.shape[-1]
+    across, along, core = place_ref[0], place_ref[1], place_ref[2]
+    for j, (own, other) in enumerate(zip(slots[::2], slots[1::2])):
+        there = partner(across, j, outer * near)
+        o, n = there // near, lax.rem(there, near)
+        for k in range(far):
+            f = partner(along, k, far)
+            for c, slot in ((core, own), (1 - core, other)):
+                basis_ref[o, c, f, n, :, :half] = slot[k, 0]
+                basis_ref[o, c, f, n, :, half:] = slot[k, 1]
+            for c in range(2):
+                state_ref[o, f, n, c] = own[k, 2 + c]
+
+
+def place_slots(place, slots, outer, near):
+    far, _, rows, half = slots[0].shape
+    basis = ((outer, 2, far, near, rows, 2 * half), BF16)
+    state = ((outer, far, near, 2, rows, half), BF16)
+    return local_call(place_kernel, "place_slots", 8, basis, state)(place, *slots)
 
 
 def deal_kernel(right_ref, out_ref, held, in_sems, out_sems):
-    pairs = held.shape[0]
-    loads = [pltpu.make_async_copy(right_ref.at[s], held.at[s], in_sems.at[s]) for s in range(pairs)]
+    pairs, devices = held.shape[:2]
+    count = in_sems.shape[1]
+    size = devices // count
+    places = [(s, g, pl.ds(g * size, size)) for s in range(pairs) for g in range(count)]
+    loads = [
+        pltpu.make_async_copy(right_ref.at[s, part], held.at[s, part], in_sems.at[s, g])
+        for s, g, part in places
+    ]
     stores = [
-        pltpu.make_async_copy(held.at[s], out_ref.at[:, s], out_sems.at[s]) for s in range(pairs)
+        pltpu.make_async_copy(held.at[s, part], out_ref.at[part, s], out_sems.at[s, g])
+        for s, g, part in places
     ]
     for load in loads:
         load.start()
@@ -72,6 +101,7 @@
     split = right_ops.reshape(pairs, devices, rows, states)
     if rows % 16:
         return split.transpose(1, 0, 2, 3)
+    count = 1
     return pl.pallas_call(
         deal_kernel,
         in_specs=[IN_HBM],
@@ -79,10 +109,10 @@
         out_shape=jax.ShapeDtypeStruct((devices, pairs, rows, states), BF16),
         scratch_shapes=[
             pltpu.VMEM(split.shape, BF16),
-            pltpu.SemaphoreType.DMA((pairs,)),
-            pltpu.SemaphoreType.DMA((pairs,)),
+            pltpu.SemaphoreType.DMA((pairs, count)),
+            pltpu.SemaphoreType.DMA((pairs, count)),
         ],
-        compiler_params=kernel_params(2),
+        compiler_params=kernel_params(61),
         name="deal_rows",
     )(split)
 
@@ -105,7 +135,7 @@
         ],
         out_specs=pl.BlockSpec((1, states, states), lambda s: (s, 0, 0)),
         out_shape=jax.ShapeDtypeStruct(left_ops.shape, BF16),
-        compiler_params=kernel_params(12),
+        compiler_params=kernel_params(60),
         cost_estimate=pl.CostEstimate(flops=0, bytes_accessed=0, transcendentals=0),
         name="build",
     )(basis, left_ops)
@@ -168,71 +198,114 @@
     )(mixing, right_rows)
 
 
-def fetch_kernel(core_ref, state_ref, own_hbm, other_ref, comp_ref, keep_ref, send_ref, applied_ref, own_ref, sem):
-    load = pltpu.make_async_copy(own_hbm, own_ref, sem)
-    load.start()
-    apply_kernel(core_ref, state_ref, own_ref, other_ref, comp_ref, keep_ref, send_ref, applied_ref, load)
-
-
-def apply_kernel(core_ref, state_ref, own_ref, other_ref, comp_ref, keep_ref, send_ref, applied_ref, load=None):
+def apply_kernel(state_ref, own_ref, other_ref, applied_ref):
     outer, narrow, _, rows, half = state_ref.shape
     pairs = own_ref.shape[0]
-    chips = outer * narrow
-    core = core_ref[0]
     state = jnp.concatenate(
         [state_ref[y, :, c].reshape(narrow * rows, half) for y in range(outer) for c in range(2)]
     )
-    for side, ref in ((1, other_ref), (0, own_ref)):
-        if side == 0 and load is not None:
-            load.wait()
+    for side, ref in enumerate((own_ref, other_ref)):
         for q in range(pairs):
             one = jnp.dot(ref[q], state, preferred_element_type=F32).astype(BF16)
             column = (side * pairs + q) * half
             applied_ref[:, column : column + half] = one
-    applied = applied_ref[...]
-    for out_ref, place in ((send_ref, 1 - core), (keep_ref, core)):
-        columns = []
-        for side in (core, 1 - core):
-            for q in range(pairs):
-                part = comp_ref[pl.ds(place * chips, chips), side * pairs + q]
-                columns.append(part.reshape(chips * rows, half))
-        joined = jnp.concatenate(columns, axis=1)
-        term = lax.dot_general(applied, joined, (((1,), (1,)), ((), ())), preferred_element_type=F32)
-        term = term.astype(out_ref.dtype).reshape(outer, 2, narrow, rows, half)
-        for c in range(2):
-            out_ref[:, :, c] = term[:, c]
-
-
-def apply_pairs(core, state, own, other, comp, fetch):
+
+
+def store_term(applied, joined, term_ref):
+    outer, narrow, _, rows, half = term_ref.shape
+    joined = joined.reshape(half, -1)
+    term = lax.dot_general(applied, joined, (((1,), (1,)), ((), ())), preferred_element_type=F32)
+    term = term.astype(term_ref.dtype).reshape(outer, 2, narrow, rows, half)
+    for c in range(2):
+        term_ref[:, :, c] = term[:, c]
+
+
+def join_kernel(core_ref, applied_ref, comp_ref, keep_ref, send_ref, joined_ref):
+    outer, narrow, _, rows, half = keep_ref.shape
+    pairs = comp_ref.shape[1] // 2
+    chips = outer * narrow
+    core = core_ref[0]
+    for k, (place, term_ref) in enumerate(((1 - core, send_ref), (core, keep_ref))):
+        for n in range(2 * pairs):
+            pair = n + pairs * (core if n < pairs else -core)
+            joined_ref[k, :, :, n * half : (n + 1) * half] = comp_ref[pl.ds(place * chips, chips), pair]
+        store_term(applied_ref[...], joined_ref[k], term_ref)
+
+
+def apply_term_kernel(state_ref, own_ref, other_ref, joined_ref, keep_ref, send_ref, applied_ref):
+    apply_kernel(state_ref, own_ref, other_ref, applied_ref)
+    for k, term_ref in enumerate((send_ref, keep_ref)):
+        store_term(applied_ref[...], joined_ref[k], term_ref)
+
+
+def local_call(kernel, name, mib, *out, scratch=(), flops=0):
+    def call(*operands):
+        specs = [
+            pl.BlockSpec(memory_space=pltpu.SMEM) if value.dtype == jnp.int32 else IN_VMEM
+            for value in operands
+        ]
+        return pl.pallas_call(
+            kernel,
+            in_specs=specs,
+            out_specs=[IN_VMEM] * len(out),
+            out_shape=[jax.ShapeDtypeStruct(*one) for one in out],
+            scratch_shapes=scratch,
+            compiler_params=kernel_params(mib),
+            cost_estimate=pl.CostEstimate(
+                flops=flops, bytes_accessed=sum(2 * value.size for value in operands if flops), transcendentals=0
+            ),
+            name=name,
+        )(*operands)
+
+    return call
+
+
+def apply_pairs(state, own, other):
     outer, narrow, _, rows, half = state.shape
     pairs, states, _ = own.shape
     if rows % 16:
         full = state.transpose(0, 2, 1, 3, 4).reshape(states, half)
         built = jnp.concatenate([own, other])
-        applied = jnp.einsum("sil,lk->sik", built, full, preferred_element_type=F32).astype(BF16)
-        joined = comp.transpose(1, 0, 2, 3).reshape(2, pairs, states, half)
-        joined = jnp.concatenate([joined[core[0]], joined[1 - core[0]]])
-        term = jnp.einsum("sik,sjk->ij", applied, joined, preferred_element_type=F32)
-        term = term.reshape(outer, 2, narrow, rows, 2, half).transpose(4, 0, 2, 1, 3, 5)
-        return term[core[0]], term[1 - core[0]].astype(BF16)
+        applied = jnp.einsum("sil,lk->isk", built, full, preferred_element_type=F32).astype(BF16)
+        return applied.reshape(states, 2 * pairs * half)
+    shape = (states, 2 * pairs * half)
+    return local_call(apply_kernel, "apply_pairs", 8, (shape, BF16))(state, own, other)[0]
+
+
+def join_terms(core, applied, comp, outer, narrow):
+    devices, both, rows, half = comp.shape
+    states = devices * rows
+    if rows % 16:
+        split = comp.reshape(2, devices // 2, 2, both // 2, rows, half)
+        split = jnp.stack([split[1 - core], split[core]])
+        split = jnp.concatenate([split[:, :, core], split[:, :, 1 - core]], axis=2)
+        joined = split.transpose(0, 1, 3, 2, 4).reshape(2, devices // 2, rows, both * half)
+        return *terms_of(applied, joined, outer, narrow), joined
+    shape = (outer, narrow, 2, rows, half)
+    out = (shape, F32), (shape, BF16), ((2, devices // 2, rows, both * half), BF16)
+    flops = 2 * states * applied.size
+    call = local_call(join_kernel, "join_terms", 12, *out, flops=flops)
+    return call(core.reshape(1), applied, comp)
+
+
+def terms_of(applied, joined, outer, narrow):
+    _, chips, rows, width = joined.shape
+    states = 2 * chips * rows
+    term = jnp.einsum("ix,kjx->kij", applied, joined.reshape(2, states // 2, width), preferred_element_type=F32)
+    term = term.reshape(2, outer, 2, narrow, rows, states // 2).transpose(0, 1, 3, 2, 4, 5)
+    return term[1], term[0].astype(BF16)
+
+
+def apply_and_terms(state, own, other, joined):
+    outer, narrow, _, rows, half = state.shape
+    pairs, states, _ = own.shape
+    if rows % 16:
+        return terms_of(apply_pairs(state, own, other), joined, outer, narrow)
     scratch = [pltpu.VMEM((states, 2 * pairs * half), BF16)]
-    if fetch:
-        scratch += [pltpu.VMEM(own.shape, BF16), pltpu.SemaphoreType.DMA]
-    return pl.pallas_call(
-        fetch_kernel if fetch else apply_kernel,
-        in_specs=[pl.BlockSpec(memory_space=pltpu.SMEM), IN_VMEM, IN_HBM if fetch else IN_VMEM, IN_VMEM, IN_VMEM],
-        out_specs=[IN_VMEM] * 2,
-        out_shape=[
-            jax.ShapeDtypeStruct(state.shape, F32),
-            jax.ShapeDtypeStruct(state.shape, BF16),
-        ],
-        scratch_shapes=scratch,
-        compiler_params=kernel_params(58 if fetch else 12),
-        cost_estimate=pl.CostEstimate(
-            flops=8 * pairs * states**2 * half, bytes_accessed=8 * pairs * states**2, transcendentals=0
-        ),
-        name="apply_pairs",
-    )(core, state, own, other, comp)
+    out = (state.shape, F32), (state.shape, BF16)
+    flops = 8 * pairs * states**2 * half
+    call = local_call(apply_term_kernel, "apply_terms", 12, *out, scratch=scratch, flops=flops)
+    return call(state, own, other, joined)
 
 
 def local(site_basis, left_ops, right_ops, integrals, wavefunction, pair_order, sector_sizes):
@@ -273,26 +346,31 @@
     piece = (piece.astype(F32) * local_mask).astype(BF16)
     summed = piece.astype(F32)
 
-    together = jnp.concatenate([site_basis.reshape(rows * 2, half), piece.reshape(2 * rows, half)])
+    halves = jnp.stack([site_basis[:, :half], site_basis[:, half:]])
+    packet = jnp.concatenate([halves, piece])
+    packet, local_mask, summed = lax.optimization_barrier((packet, local_mask, summed))
     mixed = mix(mixing, right_rows, wide, narrow, pairs * rows)
-    gathered, mixed = lax.optimization_barrier((gather_over(together, FAR, far), mixed))
-    gathered = gather_over(gathered, (OUTER, NEAR), outer * near)
-    gathered = gathered.reshape(outer, near, far, 4 * rows, half).transpose(0, 2, 1, 3, 4)
-    basis_rows = gathered[..., : 2 * rows, :].reshape(outer, narrow, rows, states)
-    state = gathered[..., 2 * rows :, :].reshape(outer, narrow, 2, rows, half)
-    basis = by_core(basis_rows, swap_cores(basis_rows))
-    basis = basis.transpose(1, 0, 2, 3, 4).reshape(states, states)
-    own_built = build(basis, left_ops)
+    packets, mixed = lax.optimization_barrier((jnp.stack(send_round(packet, FAR, far)), mixed))
+    slots = []
+    for slot in send_round(packets, (OUTER, NEAR), outer * near):
+        slots += [slot, swap_cores(slot[:, :2])]
+    place = [lax.axis_index((OUTER, NEAR)), lax.axis_index(FAR), own_core]
+    basis, state = place_slots(jnp.stack(place), slots, outer, near)
+    state = state.reshape(outer, narrow, 2, rows, half)
+    own_built = build(basis.reshape(states, states), left_ops)
     other_built = swap_cores(own_built)
+    applied = apply_pairs(state, own_built, other_built)
 
     mixed = mixed.reshape(devices, 2 * pairs * rows, half)
     comp = lax.all_to_all(mixed, ALL, split_axis=0, concat_axis=0, tiled=True)
     comp = comp.reshape(devices, 2 * pairs, rows, half)
 
     step_size = 2.0 / math.sqrt(pair_total)
-    core = own_core.reshape(1)
     for order_index in range(1, ORDER + 1):
-        keep, send = apply_pairs(core, state, own_built, other_built, comp, False)
+        if order_index == 1:
+            keep, send, joined = join_terms(own_core, applied, comp, outer, narrow)
+        else:
+            keep, send = apply_and_terms(state, own_built, other_built, joined)
         partial = (keep + swap_cores(send).astype(F32)).astype(BF16)
         partial = partial.reshape(chips, 2 * rows, half)
         arrived = lax.all_to_all(partial, CHIPS, split_axis=0, concat_axis=0, tiled=True)

time: 179 us -> 174 us (0.972)
  waiting for transfers between devices: 71.3 us -> 63.2 us
  Pallas kernels: 12.5 us -> 16.8 us
  local copies, waits for them, and re-layouts: 7.87 us -> 5.08 us
    all_to_all x1, waiting for transfers between devices: 26.3 us -> 0.04 us  [local(): comp = lax.all_to_all(mixed, ALL, split_axis=0, concat_axis=0, tiled=True)]
    ppermute x6, waiting for transfers between devices: 34.3 us -> 53.7 us  [send_round(): lax.ppermute(value, axes, [(partner(i, k, size), i) for i in range(size)])]
    pallas_call x1, Pallas kernels: 2.4 us -> 4.81 us  [build(): pl.pallas_call(build_kernel, grid=(pairs,), in_specs=[whole_block((states...]
    ppermute x7 -> x10, waiting for transfers between devices: 10.5 us -> 9.51 us  [swap_cores(): return lax.ppermute(value, CORE, [(0, 1), (1, 0)])]
    pallas_call x3 -> x5, Pallas kernels: 5.37 us -> 6.25 us  [call(): pl.pallas_call(kernel, in_specs=specs, out_specs=[IN_VMEM] * len(out), ou...]
  transfers between devices with their start and end apart: 15 -> 18, of which waited for: 11 -> 12; matrix products, arithmetic and copies ran while one was open for 3% -> 1% of each run, Pallas kernels for 1% -> 4%
where the time goes in v3:
time: 174 us
  blocking collectives  65.8 us (38%)
  waiting for transfers between devices  63.2 us (36%)
  starting transfers between devices  20.6 us (12%)
  Pallas kernels  16.8 us (10%)
  local copies, waits for them, and re-layouts  5.08 us (3%)
    ppermute x6, waiting for transfers between devices, send_round(): lax.ppermute(value, axes, [(partner(i, k, size), i) for i in range(size)])  53.7 us
    all_to_all x3, blocking collectives, local(): lax.all_to_all(partial, CHIPS, split_axis=0, concat_axis=0, tiled=True)  40.9 us
    all_to_all x2, blocking collectives, local(): lax.all_to_all(copies, CHIPS, split_axis=0, concat_axis=0, tiled=True)  25 us
    ppermute x10, waiting for transfers between devices, swap_cores(): return lax.ppermute(value, CORE, [(0, 1), (1, 0)])  9.51 us
    ppermute x6, starting transfers between devices, send_round(): lax.ppermute(value, axes, [(partner(i, k, size), i) for i in range(size)])  8.01 us
    all_to_all x1, starting transfers between devices, local(): lax.all_to_all(parts, ALL, split_axis=0, concat_axis=0, tiled=True)  7.3 us
    pallas_call x5, Pallas kernels, call(): pl.pallas_call(kernel, in_specs=specs, out_specs=[IN_VMEM] * len(out), ou...  6.25 us
    pallas_call x1, Pallas kernels, build(): pl.pallas_call(build_kernel, grid=(pairs,), in_specs=[whole_block((states...  4.81 us
  transfers between devices with their start and end apart: 18, of which 12 were waited for; matrix products, arithmetic and copies ran while one was open for 1% of the time, Pallas kernels for 4%

profile of v3, /device:TPU:0, one launch (start us, length us, event | category | flops | bytes accessed | tf_op | source)
XLA Modules:
  0.0 173.6 jit_solution(11455060923661437932)
XLA Ops:
  0.0 2.3 %deal_rows.1 = bf16[32,3,16,512]{3,2,1,0:T(8,128)(2,1)} custom-call(bf16[3,32,16,512]{3,2,1,0:T(8,128)(2,1)} %bitcast.49), custom_call_target="tpu_custom_call" | custom-call | tf_op jit(solution)/shard_map/deal_rows/pallas_call | solution.py:105
  2.4 7.3 %all-to-all-start = ((bf16[32,48,512]{2,1,0:T(8,128)(2,1)}), bf16[32,48,512]{2,1,0:T(8,128)(2,1)S(1)}, u32[]{:S(2)}, u32[]{:S(2)}) async-start(bf16[32,48,512]{2,1,0:T(8,128)(2,1)} %bitcast.48), calls=%async_computation | async-start | bytes 3145728 | tf_op jit(solution)/shard_map/all_to_all | solution.py:335
  9.7 0.3 collective-permute-start
  10.0 0.2 reduce-window.8
  10.4 0.7 gather_fusion
  11.1 0.1 copy.12
  11.3 0.7 gather_fusion.1
  12.0 0.1 copy.13
  12.2 3.6 %collective-permute-start.3 = (bf16[4,16,256]{2,1,0:T(8,128)(2,1)S(1)}, bf16[4,16,256]{2,1,0:T(8,128)(2,1)S(1)}, u32[]{:S(2)}, u32[]{:S(2)}) collective-permute-start(bf16[4,16,256]{2,1,0:T(8,128)(2,1)S(1)} %pad_maximum_fusion.1), channel_id=1, source_target_pairs={{6,0},{4,2},{2,4},{0,6},{7,1},{5,3},{3,5},{1,7},{14,8},{12,10},{10... | collective-permute-start | bytes 98312 | tf_op jit(solution)/shard_map/ppermute | solution.py:48
  15.8 0.9 collective-permute-start.1
  16.7 24.2 %collective-permute-done.3 = bf16[4,16,256]{2,1,0:T(8,128)(2,1)S(1)} collective-permute-done((bf16[4,16,256]{2,1,0:T(8,128)(2,1)S(1)}, bf16[4,16,256]{2,1,0:T(8,128)(2,1)S(1)}, u32[]{:S(2)}, u32[]{:S(2)}) %collective-permute-start.3) | collective-permute-done | bytes 32800 | tf_op jit(solution)/shard_map/ppermute | solution.py:48
  40.9 9.1 %collective-permute-done.2 = bf16[4,16,256]{2,1,0:T(8,128)(2,1)S(1)} collective-permute-done((bf16[4,16,256]{2,1,0:T(8,128)(2,1)S(1)}, bf16[4,16,256]{2,1,0:T(8,128)(2,1)S(1)}, u32[]{:S(2)}, u32[]{:S(2)}) %collective-permute-start.2) | collective-permute-done | bytes 32800 | tf_op jit(solution)/shard_map/ppermute | solution.py:48
  50.0 3.4 %mix.1 = bf16[2,2,8,2,48,256]{5,4,3,2,1,0:T(8,128)(2,1)} custom-call(bf16[96,96]{1,0:T(8,128)(2,1)S(1)} %select_bitcast_fusion.mixing_ref, bf16[1536,512]{1,0:T(8,128)(2,1)S(1)} %bitcast.42), custom_call_target="tpu_custom_call" | custom-call | flops 150994944 | bytes 3145728 | tf_op jit(solution)/shard_map/mix/pallas_call | solution.py:184
  53.4 3.6 %all-to-all-start.1 = ((bf16[32,96,256]{2,1,0:T(8,128)(2,1)}), bf16[32,96,256]{2,1,0:T(8,128)(2,1)S(1)}, u32[]{:S(2)}, u32[]{:S(2)}) async-start(bf16[32,96,256]{2,1,0:T(8,128)(2,1)} %bitcast.20), calls=%async_computation.1 | async-start | bytes 3145728 | tf_op jit(solution)/shard_map/all_to_all | solution.py:365
  57.0 2.7 %collective-permute-start.9 = (bf16[4,4,16,256]{3,2,1,0:T(8,128)(2,1)S(1)}, bf16[4,4,16,256]{3,2,1,0:T(8,128)(2,1)S(1)}, u32[]{:S(2)}, u32[]{:S(2)}) collective-permute-start(bf16[4,4,16,256]{3,2,1,0:T(8,128)(2,1)S(1)} %pad_maximum_fusion.refs_0_), channel_id=1, source_target_pairs={{17,0},{16,1},{1,16},{0,17},{19,2},{18,3},{3,18},{2,19},{21,4},{20... | collective-permute-start | bytes 393224 | tf_op jit(solution)/shard_map/ppermute | solution.py:48
  59.8 0.6 collective-permute-start.7
  60.3 0.3 collective-permute-start.5
  60.6 19.2 %collective-permute-done.9.refs_6_ = bf16[4,4,16,256]{3,2,1,0:T(8,128)(2,1)S(1)} collective-permute-done((bf16[4,4,16,256]{3,2,1,0:T(8,128)(2,1)S(1)}, bf16[4,4,16,256]{3,2,1,0:T(8,128)(2,1)S(1)}, u32[]{:S(2)}, u32[]{:S(2)}) %collective-permute-start.9) | collective-permute-done | bytes 131104 | tf_op jit(solution)/shard_map/ppermute | solution.py:48
  79.8 1.0 collective-permute-done.7.refs_4_
  80.9 0.2 collective-permute-done.5.refs_2_
  81.0 0.4 collective-permute-start.6
  81.5 0.6 collective-permute-done.8.refs_5_
  82.1 0.2 collective-permute-done.6.refs_3_
  82.4 0.7 place_slots.1
  83.0 0.8 copy-done.5
  83.8 4.8 %build.1.own_ref = bf16[3,512,512]{2,1,0:T(8,128)(2,1)} custom-call(bf16[512,512]{1,0:T(8,128)(2,1)} %bitcast.44, bf16[3,512,512]{2,1,0:T(8,128)(2,1)} %left_ref.1), custom_call_target="tpu_custom_call" | custom-call | tf_op jit(solution)/shard_map/build/pallas_call | solution.py:129
  88.6 0.4 collective-permute-start.11
  89.0 3.3 %collective-permute-done.11.other_ref = bf16[3,512,512]{2,1,0:T(8,128)(2,1)S(1)} collective-permute-done((bf16[3,512,512]{2,1,0:T(8,128)(2,1)}, bf16[3,512,512]{2,1,0:T(8,128)(2,1)S(1)}, u32[]{:S(2)}, u32[]{:S(2)}) %collective-permute-start.11) | collective-permute-done | bytes 1572896 | tf_op jit(solution)/shard_map/ppermute | solution.py:36
  92.3 1.4 copy-done.1
  93.7 1.0 apply_pairs.1.applied_ref
  94.7 1.2 copy-done.3
  95.8 1.0 join_terms.1
  96.9 0.4 collective-permute-start.12
  97.3 1.2 collective-permute-done.12
  98.5 0.1 add_convert_fusion.2
  98.6 14.2 %all_to_all.35 = bf16[16,32,256]{2,1,0:T(8,128)(2,1)S(1)} all-to-all(bf16[16,32,256]{2,1,0:T(8,128)(2,1)S(1)} %bitcast.50), channel_id=1, replica_groups=mesh['outer'=2,'core'=2,'far'=4,'near'=2] {'outer','far','near'}, dimensions={0} | all-to-all | bytes 524288 | tf_op jit(solution)/shard_map/all_to_all | solution.py:376
  112.9 12.5 %all_to_all.36 = bf16[16,32,256]{2,1,0:T(8,128)(2,1)S(1)} all-to-all(bf16[16,32,256]{2,1,0:T(8,128)(2,1)S(1)} %broadcast_in_dim.42), channel_id=1, replica_groups=mesh['outer'=2,'core'=2,'far'=4,'near'=2] {'outer','far','near'}, dimensions={0} | all-to-all | bytes 524288 | tf_op jit(solution)/shard_map/all_to_all | solution.py:382
  125.4 1.8 %apply_terms.2 = (f32[2,8,2,16,256]{4,3,2,1,0:T(8,128)S(1)}, bf16[2,8,2,16,256]{4,3,2,1,0:T(8,128)(2,1)S(1)}) custom-call(bf16[2,8,2,16,256]{4,3,2,1,0:T(8,128)(2,1)S(1)} %bitcast.47, bf16[3,512,512]{2,1,0:T(8,128)(2,1)S(1)} %copy-done.2, bf16[3,512,512]{2,1,0:T(8,128)(2,1)S(1)} %copy-done.4, bf16[2,16,16,1536]{3,2,1,0:T(8,128)(2,1)S(1)} %get-tuple-element.34.joined_ref), custom_call_target="tpu_custom_call" | custom-call | flops 1610612736 | bytes 4980736 | tf_op jit(solution)/shard_map/apply_terms/pallas_call | solution.py:247
  127.2 1.5 collective-permute-done.13
  128.8 0.1 add_convert_fusion.1
  128.8 13.3 %all_to_all.37 = bf16[16,32,256]{2,1,0:T(8,128)(2,1)S(1)} all-to-all(bf16[16,32,256]{2,1,0:T(8,128)(2,1)S(1)} %bitcast.51), channel_id=1, replica_groups=mesh['outer'=2,'core'=2,'far'=4,'near'=2] {'outer','far','near'}, dimensions={0} | all-to-all | bytes 524288 | tf_op jit(solution)/shard_map/all_to_all | solution.py:376
  142.3 12.5 %all_to_all.38 = bf16[16,32,256]{2,1,0:T(8,128)(2,1)S(1)} all-to-all(bf16[16,32,256]{2,1,0:T(8,128)(2,1)S(1)} %broadcast_in_dim.44), channel_id=1, replica_groups=mesh['outer'=2,'core'=2,'far'=4,'near'=2] {'outer','far','near'}, dimensions={0} | all-to-all | bytes 524288 | tf_op jit(solution)/shard_map/all_to_all | solution.py:382
  154.8 1.8 %apply_terms.3 = (f32[2,8,2,16,256]{4,3,2,1,0:T(8,128)S(1)}, bf16[2,8,2,16,256]{4,3,2,1,0:T(8,128)(2,1)S(1)}) custom-call(bf16[2,8,2,16,256]{4,3,2,1,0:T(8,128)(2,1)S(1)} %bitcast.46, bf16[3,512,512]{2,1,0:T(8,128)(2,1)S(1)} %copy-done.2, bf16[3,512,512]{2,1,0:T(8,128)(2,1)S(1)} %copy-done.4, bf16[2,16,16,1536]{3,2,1,0:T(8,128)(2,1)S(1)} %get-tuple-element.34.joined_ref), custom_call_target="tpu_custom_call" | custom-call | flops 1610612736 | bytes 4980736 | tf_op jit(solution)/shard_map/apply_terms/pallas_call | solution.py:247
  156.6 1.5 collective-permute-done.14
  158.2 0.1 add_convert_fusion
  158.3 13.3 %all_to_all.39 = bf16[16,32,256]{2,1,0:T(8,128)(2,1)S(1)} all-to-all(bf16[16,32,256]{2,1,0:T(8,128)(2,1)S(1)} %bitcast.52), channel_id=1, replica_groups=mesh['outer'=2,'core'=2,'far'=4,'near'=2] {'outer','far','near'}, dimensions={0} | all-to-all | bytes 524288 | tf_op jit(solution)/shard_map/all_to_all | solution.py:376
  171.8 1.2 collective-permute-done.15
  172.9 0.6 pad_maximum_fusion.2
  (62 shorter events, 1.0 us)
Async XLA Ops:
  0.0 10.4 %copy-start = (bf16[96,96]{1,0:T(8,128)(2,1)S(1)}, bf16[96,96]{1,0:T(8,128)(2,1)}, u32[]{:S(2)}) copy-start(bf16[96,96]{1,0:T(8,128)(2,1)} %param.10) | copy-start | bytes 55300
  2.3 7.4 %copy-start.6 = (bf16[16,512]{1,0:T(8,128)(2,1)S(1)}, bf16[16,512]{1,0:T(8,128)(2,1)}, u32[]{:S(2)}) copy-start(bf16[16,512]{1,0:T(8,128)(2,1)} %param.11) | copy-start | bytes 49156
  2.3 7.7 %copy-start.8 = (s32[8]{0:T(128)S(1)}, s32[8]{0:T(128)}, u32[]{:S(2)}) copy-start(s32[8]{0:T(128)} %param.13) | copy-start | bytes 100
  2.3 8.0 %copy-start.9 = (s32[96]{0:T(128)S(1)}, s32[96]{0:T(128)}, u32[]{:S(2)}) copy-start(s32[96]{0:T(128)} %param.12) | copy-start | bytes 1156
  2.3 9.0 %copy-start.7 = (bf16[16,512]{1,0:T(8,128)(2,1)S(1)}, bf16[16,512]{1,0:T(8,128)(2,1)}, u32[]{:S(2)}) copy-start(bf16[16,512]{1,0:T(8,128)(2,1)} %param.7) | copy-start | bytes 49156
  2.4 47.6 %all-to-all-start = ((bf16[32,48,512]{2,1,0:T(8,128)(2,1)}), bf16[32,48,512]{2,1,0:T(8,128)(2,1)S(1)}, u32[]{:S(2)}, u32[]{:S(2)}) async-start(bf16[32,48,512]{2,1,0:T(8,128)(2,1)} %bitcast.48), calls=%async_computation | async-start | bytes 3145728 | tf_op jit(solution)/shard_map/all_to_all | solution.py:335
  9.7 2.4 %collective-permute-start = (bf16[16,256]{1,0:T(8,128)(2,1)S(1)}, bf16[16,256]{1,0:T(8,128)(2,1)S(1)}, u32[]{:S(2)}, u32[]{:S(2)}) collective-permute-start(bf16[16,256]{1,0:T(8,128)(2,1)S(1)} %broadcast_select_fusion.2), channel_id=1, source_target_pairs={{0,8},{8,0},{1,9},{9,1},{2,10},{10,2},{3,11},{11,3},{4,12},{12,4},... | collective-permute-start | bytes 24584 | tf_op jit(solution)/shard_map/ppermute | solution.py:36
  12.2 28.6 %collective-permute-start.3 = (bf16[4,16,256]{2,1,0:T(8,128)(2,1)S(1)}, bf16[4,16,256]{2,1,0:T(8,128)(2,1)S(1)}, u32[]{:S(2)}, u32[]{:S(2)}) collective-permute-start(bf16[4,16,256]{2,1,0:T(8,128)(2,1)S(1)} %pad_maximum_fusion.1), channel_id=1, source_target_pairs={{6,0},{4,2},{2,4},{0,6},{7,1},{5,3},{3,5},{1,7},{14,8},{12,10},{10... | collective-permute-start | bytes 98312 | tf_op jit(solution)/shard_map/ppermute | solution.py:48
  15.8 34.1 %collective-permute-start.2 = (bf16[4,16,256]{2,1,0:T(8,128)(2,1)S(1)}, bf16[4,16,256]{2,1,0:T(8,128)(2,1)S(1)}, u32[]{:S(2)}, u32[]{:S(2)}) collective-permute-start(bf16[4,16,256]{2,1,0:T(8,128)(2,1)S(1)} %pad_maximum_fusion.1), channel_id=1, source_target_pairs={{4,0},{6,2},{0,4},{2,6},{5,1},{7,3},{1,5},{3,7},{12,8},{14,10},{8,... | collective-permute-start | bytes 98312 | tf_op jit(solution)/shard_map/ppermute | solution.py:48
  15.8 34.1 %collective-permute-start.1 = (bf16[4,16,256]{2,1,0:T(8,128)(2,1)S(1)}, bf16[4,16,256]{2,1,0:T(8,128)(2,1)S(1)}, u32[]{:S(2)}, u32[]{:S(2)}) collective-permute-start(bf16[4,16,256]{2,1,0:T(8,128)(2,1)S(1)} %pad_maximum_fusion.1), channel_id=1, source_target_pairs={{2,0},{0,2},{6,4},{4,6},{3,1},{1,3},{7,5},{5,7},{10,8},{8,10},{14,... | collective-permute-start | bytes 98312 | tf_op jit(solution)/shard_map/ppermute | solution.py:48
  53.4 42.5 %all-to-all-start.1 = ((bf16[32,96,256]{2,1,0:T(8,128)(2,1)}), bf16[32,96,256]{2,1,0:T(8,128)(2,1)S(1)}, u32[]{:S(2)}, u32[]{:S(2)}) async-start(bf16[32,96,256]{2,1,0:T(8,128)(2,1)} %bitcast.20), calls=%async_computation.1 | async-start | bytes 3145728 | tf_op jit(solution)/shard_map/all_to_all | solution.py:365
  57.0 22.8 %collective-permute-start.9 = (bf16[4,4,16,256]{3,2,1,0:T(8,128)(2,1)S(1)}, bf16[4,4,16,256]{3,2,1,0:T(8,128)(2,1)S(1)}, u32[]{:S(2)}, u32[]{:S(2)}) collective-permute-start(bf16[4,4,16,256]{3,2,1,0:T(8,128)(2,1)S(1)} %pad_maximum_fusion.refs_0_), channel_id=1, source_target_pairs={{17,0},{16,1},{1,16},{0,17},{19,2},{18,3},{3,18},{2,19},{21,4},{20... | collective-permute-start | bytes 393224 | tf_op jit(solution)/shard_map/ppermute | solution.py:48
  59.8 21.1 %collective-permute-start.7 = (bf16[4,4,16,256]{3,2,1,0:T(8,128)(2,1)S(1)}, bf16[4,4,16,256]{3,2,1,0:T(8,128)(2,1)S(1)}, u32[]{:S(2)}, u32[]{:S(2)}) collective-permute-start(bf16[4,4,16,256]{3,2,1,0:T(8,128)(2,1)S(1)} %pad_maximum_fusion.refs_0_), channel_id=1, source_target_pairs={{16,0},{17,1},{0,16},{1,17},{18,2},{19,3},{2,18},{3,19},{20,4},{21... | collective-permute-start | bytes 393224 | tf_op jit(solution)/shard_map/ppermute | solution.py:48
  60.3 20.7 %collective-permute-start.5 = (bf16[4,4,16,256]{3,2,1,0:T(8,128)(2,1)S(1)}, bf16[4,4,16,256]{3,2,1,0:T(8,128)(2,1)S(1)}, u32[]{:S(2)}, u32[]{:S(2)}) collective-permute-start(bf16[4,4,16,256]{3,2,1,0:T(8,128)(2,1)S(1)} %pad_maximum_fusion.refs_0_), channel_id=1, source_target_pairs={{1,0},{0,1},{17,16},{16,17},{3,2},{2,3},{19,18},{18,19},{5,4},{4,5... | collective-permute-start | bytes 393224 | tf_op jit(solution)/shard_map/ppermute | solution.py:48
  60.6 20.9 %collective-permute-start.4 = (bf16[4,2,16,256]{3,2,1,0:T(8,128)(2,1)S(1)}, bf16[4,2,16,256]{3,2,1,0:T(8,128)(2,1)S(1)}, u32[]{:S(2)}, u32[]{:S(2)}) collective-permute-start(bf16[4,2,16,256]{3,2,1,0:T(8,128)(2,1)S(1)} %slice.46), channel_id=1, source_target_pairs={{0,8},{8,0},{1,9},{9,1},{2,10},{10,2},{3,11},{11,3},{4,12},{12,4},... | collective-permute-start | bytes 196616 | tf_op jit(solution)/shard_map/ppermute | solution.py:36
  79.8 1.7 collective-permute-start.10
  80.9 1.3 collective-permute-start.8
  81.0 1.3 collective-permute-start.6
  83.0 0.8 copy-start.5
  88.6 3.6 %collective-permute-start.11 = (bf16[3,512,512]{2,1,0:T(8,128)(2,1)}, bf16[3,512,512]{2,1,0:T(8,128)(2,1)S(1)}, u32[]{:S(2)}, u32[]{:S(2)}) collective-permute-start(bf16[3,512,512]{2,1,0:T(8,128)(2,1)} %build.1.own_ref), channel_id=1, source_target_pairs={{0,8},{8,0},{1,9},{9,1},{2,10},{10,2},{3,11},{11,3},{4,12},{12,4},... | collective-permute-start | bytes 4718600 | tf_op jit(solution)/shard_map/ppermute | solution.py:36
  92.3 1.4 copy-start.1
  94.6 1.2 copy-start.3
  95.8 29.5 %copy-start.4 = (bf16[3,512,512]{2,1,0:T(8,128)(2,1)S(1)}, bf16[3,512,512]{2,1,0:T(8,128)(2,1)}, u32[]{:S(2)}) copy-start(bf16[3,512,512]{2,1,0:T(8,128)(2,1)} %copy-done.3) | copy-start | bytes 4718596
  96.9 28.5 %copy-start.2 = (bf16[3,512,512]{2,1,0:T(8,128)(2,1)S(1)}, bf16[3,512,512]{2,1,0:T(8,128)(2,1)}, u32[]{:S(2)}) copy-start(bf16[3,512,512]{2,1,0:T(8,128)(2,1)} %build.1.own_ref) | copy-start | bytes 4718596
  96.9 1.6 collective-permute-start.12
  127.1 1.6 collective-permute-start.13
  156.6 1.6 collective-permute-start.14
  171.7 1.2 collective-permute-start.15

commit v4 on v3

--- a/solution.py
+++ b/solution.py
@@ -1,4 +1,5 @@
 import functools
+import itertools
 import math
 
 import jax
@@ -9,9 +10,10 @@
 from jax.sharding import Mesh, PartitionSpec as P
 
 ORDER = 3
-OUTER, CORE, FAR, NEAR = "outer", "core", "far", "near"
-ALL = (OUTER, CORE, FAR, NEAR)
-CHIPS = (OUTER, FAR, NEAR)
+OUTER, CORE, HIGH, LOW, NEAR = "outer", "core", "high", "low", "near"
+ALL = (OUTER, CORE, HIGH, LOW, NEAR)
+CHIPS = (OUTER, HIGH, LOW, NEAR)
+CUBE = (OUTER, LOW, NEAR)
 MIB = 1024 * 1024
 LANES = 128
 IN_HBM, IN_VMEM = pl.BlockSpec(memory_space=pltpu.HBM), pl.BlockSpec(memory_space=pltpu.VMEM)
@@ -34,6 +36,14 @@
 
 def swap_cores(value):
     return lax.ppermute(value, CORE, [(0, 1), (1, 0)])
+
+
+def add_high(value):
+    if lax.axis_size(HIGH) == 1:
+        return value
+    rounded = value.astype(BF16)
+    other = lax.ppermute(rounded, HIGH, [(0, 1), (1, 0)])
+    return rounded.astype(F32) + other.astype(F32)
 
 
 def partner(position, k, size):
@@ -52,6 +62,7 @@
 def place_kernel(place_ref, *refs):
     slots, (basis_ref, state_ref) = refs[:-2], refs[-2:]
     outer, _, far, near, _, _ = basis_ref.shape
+    low = state_ref.shape[1] // near
     half = state_ref.shape[-1]
     across, along, core = place_ref[0], place_ref[1], place_ref[2]
     for j, (own, other) in enumerate(zip(slots[::2], slots[1::2])):
@@ -63,13 +74,13 @@
                 basis_ref[o, c, f, n, :, :half] = slot[k, 0]
                 basis_ref[o, c, f, n, :, half:] = slot[k, 1]
             for c in range(2):
-                state_ref[o, f, n, c] = own[k, 2 + c]
-
-
-def place_slots(place, slots, outer, near):
+                state_ref[o, lax.rem(f, low) * near + n, f // low, c] = own[k, 2 + c]
+
+
+def place_slots(place, slots, outer, high, near):
     far, _, rows, half = slots[0].shape
     basis = ((outer, 2, far, near, rows, 2 * half), BF16)
-    state = ((outer, far, near, 2, rows, half), BF16)
+    state = ((outer, far // high * near, high, 2, rows, half), BF16)
     return local_call(place_kernel, "place_slots", 8, basis, state)(place, *slots)
 
 
@@ -199,10 +210,11 @@
 
 
 def apply_kernel(state_ref, own_ref, other_ref, applied_ref):
-    outer, narrow, _, rows, half = state_ref.shape
+    outer, cube, high, _, rows, half = state_ref.shape
     pairs = own_ref.shape[0]
+    places = itertools.product(range(outer), range(2), range(high))
     state = jnp.concatenate(
-        [state_ref[y, :, c].reshape(narrow * rows, half) for y in range(outer) for c in range(2)]
+        [state_ref[o, :, h, c].reshape(cube * rows, half) for o, c, h in places]
     )
     for side, ref in enumerate((own_ref, other_ref)):
         for q in range(pairs):
@@ -211,31 +223,41 @@
             applied_ref[:, column : column + half] = one
 
 
-def store_term(applied, joined, term_ref):
-    outer, narrow, _, rows, half = term_ref.shape
+def term_shape(state_shape, last):
+    outer, cube, high, _, rows, half = state_shape
+    return (outer, high, cube, 2, rows, half) if last else state_shape
+
+
+def store_term(last, applied, joined, term_ref):
+    outer, cube, high, _, rows, half = term_ref.shape
+    if last:
+        high, cube = cube, high
     joined = joined.reshape(half, -1)
     term = lax.dot_general(applied, joined, (((1,), (1,)), ((), ())), preferred_element_type=F32)
-    term = term.astype(term_ref.dtype).reshape(outer, 2, narrow, rows, half)
+    term = term.astype(term_ref.dtype).reshape(outer, 2, high, cube, rows, half)
     for c in range(2):
-        term_ref[:, :, c] = term[:, c]
+        for h in range(high):
+            if last:
+                term_ref[:, h, :, c] = term[:, c, h]
+            else:
+                term_ref[:, :, h, c] = term[:, c, h]
 
 
 def join_kernel(core_ref, applied_ref, comp_ref, keep_ref, send_ref, joined_ref):
-    outer, narrow, _, rows, half = keep_ref.shape
-    pairs = comp_ref.shape[1] // 2
-    chips = outer * narrow
+    half = keep_ref.shape[-1]
+    chips, pairs = comp_ref.shape[0] // 2, comp_ref.shape[1] // 2
     core = core_ref[0]
     for k, (place, term_ref) in enumerate(((1 - core, send_ref), (core, keep_ref))):
         for n in range(2 * pairs):
             pair = n + pairs * (core if n < pairs else -core)
             joined_ref[k, :, :, n * half : (n + 1) * half] = comp_ref[pl.ds(place * chips, chips), pair]
-        store_term(applied_ref[...], joined_ref[k], term_ref)
-
-
-def apply_term_kernel(state_ref, own_ref, other_ref, joined_ref, keep_ref, send_ref, applied_ref):
+        store_term(False, applied_ref[...], joined_ref[k], term_ref)
+
+
+def apply_term_kernel(last, state_ref, own_ref, other_ref, joined_ref, keep_ref, send_ref, applied_ref):
     apply_kernel(state_ref, own_ref, other_ref, applied_ref)
     for k, term_ref in enumerate((send_ref, keep_ref)):
-        store_term(applied_ref[...], joined_ref[k], term_ref)
+        store_term(last, applied_ref[...], joined_ref[k], term_ref)
 
 
 def local_call(kernel, name, mib, *out, scratch=(), flops=0):
@@ -261,10 +283,10 @@
 
 
 def apply_pairs(state, own, other):
-    outer, narrow, _, rows, half = state.shape
     pairs, states, _ = own.shape
-    if rows % 16:
-        full = state.transpose(0, 2, 1, 3, 4).reshape(states, half)
+    half = state.shape[-1]
+    if state.shape[-2] % 16:
+        full = state.transpose(0, 3, 2, 1, 4, 5).reshape(states, half)
         built = jnp.concatenate([own, other])
         applied = jnp.einsum("sil,lk->isk", built, full, preferred_element_type=F32).astype(BF16)
         return applied.reshape(states, 2 * pairs * half)
@@ -272,45 +294,45 @@
     return local_call(apply_kernel, "apply_pairs", 8, (shape, BF16))(state, own, other)[0]
 
 
-def join_terms(core, applied, comp, outer, narrow):
+def join_terms(core, applied, comp, shape):
     devices, both, rows, half = comp.shape
-    states = devices * rows
     if rows % 16:
         split = comp.reshape(2, devices // 2, 2, both // 2, rows, half)
         split = jnp.stack([split[1 - core], split[core]])
         split = jnp.concatenate([split[:, :, core], split[:, :, 1 - core]], axis=2)
         joined = split.transpose(0, 1, 3, 2, 4).reshape(2, devices // 2, rows, both * half)
-        return *terms_of(applied, joined, outer, narrow), joined
-    shape = (outer, narrow, 2, rows, half)
+        return *terms_of(applied, joined, shape, False), joined
     out = (shape, F32), (shape, BF16), ((2, devices // 2, rows, both * half), BF16)
-    flops = 2 * states * applied.size
+    flops = 2 * devices * rows * applied.size
     call = local_call(join_kernel, "join_terms", 12, *out, flops=flops)
     return call(core.reshape(1), applied, comp)
 
 
-def terms_of(applied, joined, outer, narrow):
-    _, chips, rows, width = joined.shape
-    states = 2 * chips * rows
-    term = jnp.einsum("ix,kjx->kij", applied, joined.reshape(2, states // 2, width), preferred_element_type=F32)
-    term = term.reshape(2, outer, 2, narrow, rows, states // 2).transpose(0, 1, 3, 2, 4, 5)
+def terms_of(applied, joined, shape, last):
+    outer, cube, high, _, rows, half = shape
+    joined = joined.reshape(2, half, -1)
+    term = jnp.einsum("ix,kjx->kij", applied, joined, preferred_element_type=F32)
+    term = term.reshape(2, outer, 2, high, cube, rows, half)
+    term = term.transpose((0, 1, 3, 4, 2, 5, 6) if last else (0, 1, 4, 3, 2, 5, 6))
     return term[1], term[0].astype(BF16)
 
 
-def apply_and_terms(state, own, other, joined):
-    outer, narrow, _, rows, half = state.shape
+def apply_and_terms(state, own, other, joined, last):
     pairs, states, _ = own.shape
-    if rows % 16:
-        return terms_of(apply_pairs(state, own, other), joined, outer, narrow)
+    half = state.shape[-1]
+    if state.shape[-2] % 16:
+        return terms_of(apply_pairs(state, own, other), joined, state.shape, last)
     scratch = [pltpu.VMEM((states, 2 * pairs * half), BF16)]
-    out = (state.shape, F32), (state.shape, BF16)
+    shape = term_shape(state.shape, last)
     flops = 8 * pairs * states**2 * half
-    call = local_call(apply_term_kernel, "apply_terms", 12, *out, scratch=scratch, flops=flops)
+    kernel = functools.partial(apply_term_kernel, last)
+    call = local_call(kernel, "apply_terms", 12, (shape, F32), (shape, BF16), scratch=scratch, flops=flops)
     return call(state, own, other, joined)
 
 
 def local(site_basis, left_ops, right_ops, integrals, wavefunction, pair_order, sector_sizes):
-    outer, far, near = (lax.axis_size(name) for name in CHIPS)
-    narrow = far * near
+    outer, high, low, near = (lax.axis_size(name) for name in CHIPS)
+    narrow = high * low * near
     wide = 2 * outer
     devices = wide * narrow
     rows, states = wavefunction.shape
@@ -318,7 +340,7 @@
     pairs = left_ops.shape[0]
     pair_total = integrals.shape[0]
     chips = outer * narrow
-    own_outer, own_core, own_narrow = (lax.axis_index(name) for name in (OUTER, CORE, (FAR, NEAR)))
+    own_core, own_high = lax.axis_index(CORE), lax.axis_index(HIGH)
     is_high = own_core == 1
 
     def own_half(value):
@@ -337,10 +359,13 @@
     mixing = jnp.take(jnp.take(integrals, pair_order, axis=0), pair_order, axis=1)
 
     blocks = block_ids(sector_sizes, states).astype(F32)
-    by_device = blocks.reshape(outer, 2, narrow, rows)
-    chip_rows = lax.dynamic_slice(by_device, (own_outer, 0, own_narrow, 0), (1, 2, 1, rows)).reshape(2, rows)
+    by_device = blocks.reshape(outer, 2, high, low, near, rows)
+    first = (lax.axis_index(OUTER), 0, 0, lax.axis_index(LOW), lax.axis_index(NEAR), 0)
+    cube_rows = lax.dynamic_slice(by_device, first, (1, 2, high, 1, 1, rows))
+    cube_rows = cube_rows.reshape(2, high, rows).transpose(1, 0, 2)
     own_columns = own_half(blocks)
-    local_mask = (jnp.abs(chip_rows[:, :, None] - own_columns[None, None, :]) <= 2.0).astype(F32)
+    cube_mask = (jnp.abs(cube_rows[..., None] - own_columns) <= 2.0).astype(F32)
+    local_mask = lax.dynamic_index_in_dim(cube_mask, own_high, 0, keepdims=False)
 
     piece = by_core(own_half(wavefunction), swap_cores(other_half(wavefunction)))
     piece = (piece.astype(F32) * local_mask).astype(BF16)
@@ -348,15 +373,16 @@
 
     halves = jnp.stack([site_basis[:, :half], site_basis[:, half:]])
     packet = jnp.concatenate([halves, piece])
-    packet, local_mask, summed = lax.optimization_barrier((packet, local_mask, summed))
+    packet, local_mask, cube_mask, summed = lax.optimization_barrier(
+        (packet, local_mask, cube_mask, summed)
+    )
     mixed = mix(mixing, right_rows, wide, narrow, pairs * rows)
-    packets, mixed = lax.optimization_barrier((jnp.stack(send_round(packet, FAR, far)), mixed))
+    packets, mixed = lax.optimization_barrier((jnp.stack(send_round(packet, (HIGH, LOW), high * low)), mixed))
     slots = []
     for slot in send_round(packets, (OUTER, NEAR), outer * near):
         slots += [slot, swap_cores(slot[:, :2])]
-    place = [lax.axis_index((OUTER, NEAR)), lax.axis_index(FAR), own_core]
-    basis, state = place_slots(jnp.stack(place), slots, outer, near)
-    state = state.reshape(outer, narrow, 2, rows, half)
+    place = [lax.axis_index((OUTER, NEAR)), lax.axis_index((HIGH, LOW)), own_core]
+    basis, state = place_slots(jnp.stack(place), slots, outer, high, near)
     own_built = build(basis.reshape(states, states), left_ops)
     other_built = swap_cores(own_built)
     applied = apply_pairs(state, own_built, other_built)
@@ -367,20 +393,29 @@
 
     step_size = 2.0 / math.sqrt(pair_total)
     for order_index in range(1, ORDER + 1):
+        last = order_index == ORDER
         if order_index == 1:
-            keep, send, joined = join_terms(own_core, applied, comp, outer, narrow)
+            keep, send, joined = join_terms(own_core, applied, comp, state.shape)
         else:
-            keep, send = apply_and_terms(state, own_built, other_built, joined)
+            keep, send = apply_and_terms(state, own_built, other_built, joined, last)
         partial = (keep + swap_cores(send).astype(F32)).astype(BF16)
-        partial = partial.reshape(chips, 2 * rows, half)
-        arrived = lax.all_to_all(partial, CHIPS, split_axis=0, concat_axis=0, tiled=True)
-        term = jnp.sum(arrived.astype(F32), axis=0).reshape(2, rows, half)
-        piece = (-(step_size / order_index) * local_mask * term).astype(BF16)
+        factor = -(step_size / order_index)
+        if last:
+            partial = partial.reshape(chips, 2 * rows, half)
+            arrived = lax.all_to_all(partial, CHIPS, split_axis=0, concat_axis=0, tiled=True)
+            term = jnp.sum(arrived.astype(F32), axis=0).reshape(2, rows, half)
+            piece = (factor * local_mask * term).astype(BF16)
+        else:
+            partial = partial.reshape(chips // high, high * 2 * rows, half)
+            arrived = lax.all_to_all(partial, CUBE, split_axis=0, concat_axis=0, tiled=True)
+            term = jnp.sum(arrived.astype(F32), axis=0).reshape(cube_mask.shape)
+            term = add_high(cube_mask * term)
+            pieces = (factor * cube_mask * term).astype(BF16)
+            piece = lax.dynamic_index_in_dim(pieces, own_high, 0, keepdims=False)
+            copies = jnp.broadcast_to(pieces.reshape(partial.shape[1:]), partial.shape)
+            state = lax.all_to_all(copies, CUBE, split_axis=0, concat_axis=0, tiled=True)
+            state = state.reshape(outer, low * near, high, 2, rows, half)
         summed = summed + piece.astype(F32)
-        if order_index < ORDER:
-            copies = jnp.broadcast_to(piece.reshape(1, 2 * rows, half), (chips, 2 * rows, half))
-            state = lax.all_to_all(copies, CHIPS, split_axis=0, concat_axis=0, tiled=True)
-            state = state.reshape(outer, narrow, 2, rows, half)
 
     mine = jnp.where(is_high, summed[1], summed[0])
     theirs = jnp.where(is_high, summed[0], summed[1])
@@ -391,7 +426,8 @@
 def solution(mesh):
     wide, narrow = mesh.shape["wide"], mesh.shape["narrow"]
     near = math.gcd(narrow, 2)
-    finer = Mesh(mesh.devices.reshape(wide // 2, 2, narrow // near, near), ALL)
+    high = math.gcd(narrow // near, 2)
+    finer = Mesh(mesh.devices.reshape(wide // 2, 2, high, narrow // near // high, near), ALL)
     placed = (
         P(ALL, None),
         P(ALL, None, None),

time: 174 us -> 170 us (0.977)
  blocking collectives: 65.8 us -> 51.9 us
  waiting for transfers between devices: 63.2 us -> 69.6 us
  starting transfers between devices: 20.6 us -> 24 us
    all_to_all x3 -> x1, blocking collectives: 40.9 us -> 13 us  [local(): lax.all_to_all(partial, CHIPS, split_axis=0, concat_axis=0, tiled=True)]
    all_to_all x2 -> x4, blocking collectives: 25 us -> 38.9 us  [the longest x2 20.1 us: local(): lax.all_to_all(partial, CUBE, split_axis=0, concat_axis=0, tiled=True)]
    ppermute x0 -> x2, waiting for transfers between devices: none -> 6.41 us  [add_high(): other = lax.ppermute(rounded, HIGH, [(0, 1), (1, 0)])]
    ppermute x0 -> x2, starting transfers between devices: none -> 3.35 us  [add_high(): other = lax.ppermute(rounded, HIGH, [(0, 1), (1, 0)])]
  transfers between devices with their start and end apart: 18 -> 20, of which waited for: 12 -> 14; matrix products, arithmetic and copies ran while one was open for 1% -> 1% of each run, Pallas kernels for 4% -> 4%
where the time goes in v4:
time: 170 us; the launch traced here: 169 us
  waiting for transfers between devices  69.6 us (41%)
  blocking collectives  51.9 us (31%)
  starting transfers between devices  24 us (14%)
  Pallas kernels  16.8 us (10%)
  local copies, waits for them, and re-layouts  5.11 us (3%)
    ppermute x6, waiting for transfers between devices, send_round(): lax.ppermute(value, axes, [(partner(i, k, size), i) for i in range(size)])  53.6 us
    all_to_all x2, blocking collectives, local(): lax.all_to_all(partial, CUBE, split_axis=0, concat_axis=0, tiled=True)  20.1 us
    all_to_all x2, blocking collectives, local(): lax.all_to_all(copies, CUBE, split_axis=0, concat_axis=0, tiled=True)  18.8 us
    all_to_all x1, blocking collectives, local(): lax.all_to_all(partial, CHIPS, split_axis=0, concat_axis=0, tiled=True)  13 us
    ppermute x10, waiting for transfers between devices, swap_cores(): return lax.ppermute(value, CORE, [(0, 1), (1, 0)])  9.5 us
    ppermute x6, starting transfers between devices, send_round(): lax.ppermute(value, axes, [(partner(i, k, size), i) for i in range(size)])  8.01 us
    all_to_all x1, starting transfers between devices, local(): lax.all_to_all(parts, ALL, split_axis=0, concat_axis=0, tiled=True)  7.3 us
    ppermute x2, waiting for transfers between devices, add_high(): other = lax.ppermute(rounded, HIGH, [(0, 1), (1, 0)])  6.41 us
  transfers between devices with their start and end apart: 20, of which 14 were waited for; matrix products, arithmetic and copies ran while one was open for 1% of the time, Pallas kernels for 4%

profile of v4, /device:TPU:0, one launch (start us, length us, event | category | flops | bytes accessed | tf_op | source)
XLA Modules:
  0.0 169.4 jit_solution(15940070830734406334)
XLA Ops:
  0.0 2.3 %deal_rows.1 = bf16[32,3,16,512]{3,2,1,0:T(8,128)(2,1)} custom-call(bf16[3,32,16,512]{3,2,1,0:T(8,128)(2,1)} %bitcast.58), custom_call_target="tpu_custom_call" | custom-call | tf_op jit(solution)/shard_map/deal_rows/pallas_call | solution.py:116
  2.3 7.3 %all-to-all-start = ((bf16[32,48,512]{2,1,0:T(8,128)(2,1)}), bf16[32,48,512]{2,1,0:T(8,128)(2,1)S(1)}, u32[]{:S(2)}, u32[]{:S(2)}) async-start(bf16[32,48,512]{2,1,0:T(8,128)(2,1)} %bitcast.57), calls=%async_computation | async-start | bytes 3145728 | tf_op jit(solution)/shard_map/all_to_all | solution.py:357
  9.7 0.3 collective-permute-start
  10.0 0.2 reduce-window.8
  10.4 0.7 gather_fusion
  11.1 0.1 copy.15
  11.4 0.7 gather_fusion.1
  12.2 3.6 %collective-permute-start.3 = (bf16[4,16,256]{2,1,0:T(8,128)(2,1)S(1)}, bf16[4,16,256]{2,1,0:T(8,128)(2,1)S(1)}, u32[]{:S(2)}, u32[]{:S(2)}) collective-permute-start(bf16[4,16,256]{2,1,0:T(8,128)(2,1)S(1)} %pad_maximum_fusion.1), channel_id=1, source_target_pairs={{6,0},{4,2},{2,4},{0,6},{7,1},{5,3},{3,5},{1,7},{14,8},{12,10},{10... | collective-permute-start | bytes 98312 | tf_op jit(solution)/shard_map/ppermute | solution.py:58
  15.8 0.9 collective-permute-start.1
  16.7 24.2 %collective-permute-done.3 = bf16[4,16,256]{2,1,0:T(8,128)(2,1)S(1)} collective-permute-done((bf16[4,16,256]{2,1,0:T(8,128)(2,1)S(1)}, bf16[4,16,256]{2,1,0:T(8,128)(2,1)S(1)}, u32[]{:S(2)}, u32[]{:S(2)}) %collective-permute-start.3) | collective-permute-done | bytes 32800 | tf_op jit(solution)/shard_map/ppermute | solution.py:58
  40.8 9.1 %collective-permute-done.2 = bf16[4,16,256]{2,1,0:T(8,128)(2,1)S(1)} collective-permute-done((bf16[4,16,256]{2,1,0:T(8,128)(2,1)S(1)}, bf16[4,16,256]{2,1,0:T(8,128)(2,1)S(1)}, u32[]{:S(2)}, u32[]{:S(2)}) %collective-permute-start.2) | collective-permute-done | bytes 32800 | tf_op jit(solution)/shard_map/ppermute | solution.py:58
  50.0 3.4 %mix.1 = bf16[2,2,8,2,48,256]{5,4,3,2,1,0:T(8,128)(2,1)} custom-call(bf16[96,96]{1,0:T(8,128)(2,1)S(1)} %select_bitcast_fusion.mixing_ref, bf16[1536,512]{1,0:T(8,128)(2,1)S(1)} %bitcast.52), custom_call_target="tpu_custom_call" | custom-call | flops 150994944 | bytes 3145728 | tf_op jit(solution)/shard_map/mix/pallas_call | solution.py:195
  53.4 3.6 %all-to-all-start.1 = ((bf16[32,96,256]{2,1,0:T(8,128)(2,1)}), bf16[32,96,256]{2,1,0:T(8,128)(2,1)S(1)}, u32[]{:S(2)}, u32[]{:S(2)}) async-start(bf16[32,96,256]{2,1,0:T(8,128)(2,1)} %bitcast.21), calls=%async_computation.1 | async-start | bytes 3145728 | tf_op jit(solution)/shard_map/all_to_all | solution.py:391
  57.0 2.7 %collective-permute-start.9 = (bf16[4,4,16,256]{3,2,1,0:T(8,128)(2,1)S(1)}, bf16[4,4,16,256]{3,2,1,0:T(8,128)(2,1)S(1)}, u32[]{:S(2)}, u32[]{:S(2)}) collective-permute-start(bf16[4,4,16,256]{3,2,1,0:T(8,128)(2,1)S(1)} %pad_maximum_fusion.refs_0_), channel_id=1, source_target_pairs={{17,0},{16,1},{1,16},{0,17},{19,2},{18,3},{3,18},{2,19},{21,4},{20... | collective-permute-start | bytes 393224 | tf_op jit(solution)/shard_map/ppermute | solution.py:58
  59.7 0.6 collective-permute-start.7
  60.3 0.3 collective-permute-start.5
  60.6 19.2 %collective-permute-done.9.refs_6_ = bf16[4,4,16,256]{3,2,1,0:T(8,128)(2,1)S(1)} collective-permute-done((bf16[4,4,16,256]{3,2,1,0:T(8,128)(2,1)S(1)}, bf16[4,4,16,256]{3,2,1,0:T(8,128)(2,1)S(1)}, u32[]{:S(2)}, u32[]{:S(2)}) %collective-permute-start.9) | collective-permute-done | bytes 131104 | tf_op jit(solution)/shard_map/ppermute | solution.py:58
  79.8 1.0 collective-permute-done.7.refs_4_
  80.9 0.2 collective-permute-done.5.refs_2_
  81.0 0.4 collective-permute-start.6
  81.5 0.6 collective-permute-done.8.refs_5_
  82.1 0.2 collective-permute-done.6.refs_3_
  82.3 0.7 place_slots.1
  83.0 0.8 copy-done.5
  83.8 4.8 %build.1.own_ref = bf16[3,512,512]{2,1,0:T(8,128)(2,1)} custom-call(bf16[512,512]{1,0:T(8,128)(2,1)} %bitcast.54, bf16[3,512,512]{2,1,0:T(8,128)(2,1)} %left_ref.1), custom_call_target="tpu_custom_call" | custom-call | tf_op jit(solution)/shard_map/build/pallas_call | solution.py:140
  88.6 0.4 collective-permute-start.11
  89.0 3.3 %collective-permute-done.11.other_ref = bf16[3,512,512]{2,1,0:T(8,128)(2,1)S(1)} collective-permute-done((bf16[3,512,512]{2,1,0:T(8,128)(2,1)}, bf16[3,512,512]{2,1,0:T(8,128)(2,1)S(1)}, u32[]{:S(2)}, u32[]{:S(2)}) %collective-permute-start.11) | collective-permute-done | bytes 1572896 | tf_op jit(solution)/shard_map/ppermute | solution.py:38
  92.3 1.4 copy-done.1
  93.7 1.0 apply_pairs.1.applied_ref
  94.7 1.2 copy-done.3
  95.8 1.0 join_terms.1
  96.9 0.4 collective-permute-start.12
  97.3 1.2 collective-permute-done.12
  98.6 10.2 %all_to_all.35 = bf16[8,64,256]{2,1,0:T(8,128)(2,1)S(1)} all-to-all(bf16[8,64,256]{2,1,0:T(8,128)(2,1)S(1)} %bitcast.59), channel_id=1, replica_groups=mesh['outer'=2,'core'=2,'high'=2,'low'=2,'near'=2] {'outer','low','near'}, dimensions={0} | all-to-all | bytes 524288 | tf_op jit(solution)/shard_map/all_to_all | solution.py:410
  108.8 1.7 collective-permute-start.13
  110.5 3.2 %collective-permute-done.13 = bf16[2,2,16,256]{3,2,1,0:T(8,128)(2,1)S(1)} collective-permute-done((bf16[2,2,16,256]{3,2,1,0:T(8,128)(2,1)S(1)}, bf16[2,2,16,256]{3,2,1,0:T(8,128)(2,1)S(1)}, u32[]{:S(2)}, u32[]{:S(2)}) %collective-permute-start.13) | collective-permute-done | bytes 32800 | tf_op jit(solution)/shard_map/ppermute | solution.py:45
  113.7 9.4 %all_to_all.36 = bf16[8,64,256]{2,1,0:T(8,128)(2,1)S(1)} all-to-all(bf16[8,64,256]{2,1,0:T(8,128)(2,1)S(1)} %broadcast_in_dim.34), channel_id=1, replica_groups=mesh['outer'=2,'core'=2,'high'=2,'low'=2,'near'=2] {'outer','low','near'}, dimensions={0} | all-to-all | bytes 524288 | tf_op jit(solution)/shard_map/all_to_all | solution.py:416
  123.1 1.8 %apply_terms.2 = (f32[2,4,2,2,16,256]{5,4,3,2,1,0:T(8,128)S(1)}, bf16[2,4,2,2,16,256]{5,4,3,2,1,0:T(8,128)(2,1)S(1)}) custom-call(bf16[2,4,2,2,16,256]{5,4,3,2,1,0:T(8,128)(2,1)S(1)} %bitcast.56, bf16[3,512,512]{2,1,0:T(8,128)(2,1)S(1)} %copy-done.2, bf16[3,512,512]{2,1,0:T(8,128)(2,1)S(1)} %copy-done.4, ...), custom_call_target="tpu_custom_call" | custom-call | flops 1610612736 | bytes 4980736 | tf_op jit(solution)/shard_map/apply_terms/pallas_call | solution.py:269
  125.0 1.5 collective-permute-done.14
  126.6 10.0 %all_to_all.37 = bf16[8,64,256]{2,1,0:T(8,128)(2,1)S(1)} all-to-all(bf16[8,64,256]{2,1,0:T(8,128)(2,1)S(1)} %bitcast.60), channel_id=1, replica_groups=mesh['outer'=2,'core'=2,'high'=2,'low'=2,'near'=2] {'outer','low','near'}, dimensions={0} | all-to-all | bytes 524288 | tf_op jit(solution)/shard_map/all_to_all | solution.py:410
  136.6 1.7 collective-permute-start.15
  138.3 3.2 %collective-permute-done.15 = bf16[2,2,16,256]{3,2,1,0:T(8,128)(2,1)S(1)} collective-permute-done((bf16[2,2,16,256]{3,2,1,0:T(8,128)(2,1)S(1)}, bf16[2,2,16,256]{3,2,1,0:T(8,128)(2,1)S(1)}, u32[]{:S(2)}, u32[]{:S(2)}) %collective-permute-start.15) | collective-permute-done | bytes 32800 | tf_op jit(solution)/shard_map/ppermute | solution.py:45
  141.5 9.4 %all_to_all.38 = bf16[8,64,256]{2,1,0:T(8,128)(2,1)S(1)} all-to-all(bf16[8,64,256]{2,1,0:T(8,128)(2,1)S(1)} %broadcast_in_dim.35), channel_id=1, replica_groups=mesh['outer'=2,'core'=2,'high'=2,'low'=2,'near'=2] {'outer','low','near'}, dimensions={0} | all-to-all | bytes 524288 | tf_op jit(solution)/shard_map/all_to_all | solution.py:416
  150.9 1.8 %apply_terms.3 = (f32[2,2,4,2,16,256]{5,4,3,2,1,0:T(8,128)S(1)}, bf16[2,2,4,2,16,256]{5,4,3,2,1,0:T(8,128)(2,1)S(1)}) custom-call(bf16[2,4,2,2,16,256]{5,4,3,2,1,0:T(8,128)(2,1)S(1)} %bitcast.55, bf16[3,512,512]{2,1,0:T(8,128)(2,1)S(1)} %copy-done.2, bf16[3,512,512]{2,1,0:T(8,128)(2,1)S(1)} %copy-done.4, ...), custom_call_target="tpu_custom_call" | custom-call | flops 1610612736 | bytes 4980736 | tf_op jit(solution)/shard_map/apply_terms/pallas_call | solution.py:269
  152.8 1.5 collective-permute-done.16
  154.4 13.0 %all_to_all.39 = bf16[16,32,256]{2,1,0:T(8,128)(2,1)S(1)} all-to-all(bf16[16,32,256]{2,1,0:T(8,128)(2,1)S(1)} %bitcast.61), channel_id=1, replica_groups=mesh['outer'=2,'core'=2,'high'=2,'low'=2,'near'=2] {'outer','high','low'..., dimensions={0} | all-to-all | bytes 524288 | tf_op jit(solution)/shard_map/all_to_all | solution.py:405
  167.6 1.2 collective-permute-done.17
  168.8 0.6 pad_maximum_fusion.2
  (69 shorter events, 1.4 us)
Async XLA Ops:
  0.0 10.4 %copy-start = (bf16[96,96]{1,0:T(8,128)(2,1)S(1)}, bf16[96,96]{1,0:T(8,128)(2,1)}, u32[]{:S(2)}) copy-start(bf16[96,96]{1,0:T(8,128)(2,1)} %param.10) | copy-start | bytes 55300
  2.3 7.4 %copy-start.6 = (bf16[16,512]{1,0:T(8,128)(2,1)S(1)}, bf16[16,512]{1,0:T(8,128)(2,1)}, u32[]{:S(2)}) copy-start(bf16[16,512]{1,0:T(8,128)(2,1)} %param.11) | copy-start | bytes 49156
  2.3 7.7 %copy-start.8 = (s32[8]{0:T(128)S(1)}, s32[8]{0:T(128)}, u32[]{:S(2)}) copy-start(s32[8]{0:T(128)} %param.13) | copy-start | bytes 100
  2.3 8.1 %copy-start.9 = (s32[96]{0:T(128)S(1)}, s32[96]{0:T(128)}, u32[]{:S(2)}) copy-start(s32[96]{0:T(128)} %param.12) | copy-start | bytes 1156
  2.3 9.0 %copy-start.7 = (bf16[16,512]{1,0:T(8,128)(2,1)S(1)}, bf16[16,512]{1,0:T(8,128)(2,1)}, u32[]{:S(2)}) copy-start(bf16[16,512]{1,0:T(8,128)(2,1)} %param.7) | copy-start | bytes 49156
  2.3 47.6 %all-to-all-start = ((bf16[32,48,512]{2,1,0:T(8,128)(2,1)}), bf16[32,48,512]{2,1,0:T(8,128)(2,1)S(1)}, u32[]{:S(2)}, u32[]{:S(2)}) async-start(bf16[32,48,512]{2,1,0:T(8,128)(2,1)} %bitcast.57), calls=%async_computation | async-start | bytes 3145728 | tf_op jit(solution)/shard_map/all_to_all | solution.py:357
  9.7 2.5 %collective-permute-start = (bf16[16,256]{1,0:T(8,128)(2,1)S(1)}, bf16[16,256]{1,0:T(8,128)(2,1)S(1)}, u32[]{:S(2)}, u32[]{:S(2)}) collective-permute-start(bf16[16,256]{1,0:T(8,128)(2,1)S(1)} %broadcast_select_fusion.2), channel_id=1, source_target_pairs={{0,8},{8,0},{1,9},{9,1},{2,10},{10,2},{3,11},{11,3},{4,12},{12,4},... | collective-permute-start | bytes 24584 | tf_op jit(solution)/shard_map/ppermute | solution.py:38
  12.2 28.6 %collective-permute-start.3 = (bf16[4,16,256]{2,1,0:T(8,128)(2,1)S(1)}, bf16[4,16,256]{2,1,0:T(8,128)(2,1)S(1)}, u32[]{:S(2)}, u32[]{:S(2)}) collective-permute-start(bf16[4,16,256]{2,1,0:T(8,128)(2,1)S(1)} %pad_maximum_fusion.1), channel_id=1, source_target_pairs={{6,0},{4,2},{2,4},{0,6},{7,1},{5,3},{3,5},{1,7},{14,8},{12,10},{10... | collective-permute-start | bytes 98312 | tf_op jit(solution)/shard_map/ppermute | solution.py:58
  15.8 34.1 %collective-permute-start.2 = (bf16[4,16,256]{2,1,0:T(8,128)(2,1)S(1)}, bf16[4,16,256]{2,1,0:T(8,128)(2,1)S(1)}, u32[]{:S(2)}, u32[]{:S(2)}) collective-permute-start(bf16[4,16,256]{2,1,0:T(8,128)(2,1)S(1)} %pad_maximum_fusion.1), channel_id=1, source_target_pairs={{4,0},{6,2},{0,4},{2,6},{5,1},{7,3},{1,5},{3,7},{12,8},{14,10},{8,... | collective-permute-start | bytes 98312 | tf_op jit(solution)/shard_map/ppermute | solution.py:58
  15.8 34.1 %collective-permute-start.1 = (bf16[4,16,256]{2,1,0:T(8,128)(2,1)S(1)}, bf16[4,16,256]{2,1,0:T(8,128)(2,1)S(1)}, u32[]{:S(2)}, u32[]{:S(2)}) collective-permute-start(bf16[4,16,256]{2,1,0:T(8,128)(2,1)S(1)} %pad_maximum_fusion.1), channel_id=1, source_target_pairs={{2,0},{0,2},{6,4},{4,6},{3,1},{1,3},{7,5},{5,7},{10,8},{8,10},{14,... | collective-permute-start | bytes 98312 | tf_op jit(solution)/shard_map/ppermute | solution.py:58
  53.4 42.5 %all-to-all-start.1 = ((bf16[32,96,256]{2,1,0:T(8,128)(2,1)}), bf16[32,96,256]{2,1,0:T(8,128)(2,1)S(1)}, u32[]{:S(2)}, u32[]{:S(2)}) async-start(bf16[32,96,256]{2,1,0:T(8,128)(2,1)} %bitcast.21), calls=%async_computation.1 | async-start | bytes 3145728 | tf_op jit(solution)/shard_map/all_to_all | solution.py:391
  57.0 22.8 %collective-permute-start.9 = (bf16[4,4,16,256]{3,2,1,0:T(8,128)(2,1)S(1)}, bf16[4,4,16,256]{3,2,1,0:T(8,128)(2,1)S(1)}, u32[]{:S(2)}, u32[]{:S(2)}) collective-permute-start(bf16[4,4,16,256]{3,2,1,0:T(8,128)(2,1)S(1)} %pad_maximum_fusion.refs_0_), channel_id=1, source_target_pairs={{17,0},{16,1},{1,16},{0,17},{19,2},{18,3},{3,18},{2,19},{21,4},{20... | collective-permute-start | bytes 393224 | tf_op jit(solution)/shard_map/ppermute | solution.py:58
  59.7 21.1 %collective-permute-start.7 = (bf16[4,4,16,256]{3,2,1,0:T(8,128)(2,1)S(1)}, bf16[4,4,16,256]{3,2,1,0:T(8,128)(2,1)S(1)}, u32[]{:S(2)}, u32[]{:S(2)}) collective-permute-start(bf16[4,4,16,256]{3,2,1,0:T(8,128)(2,1)S(1)} %pad_maximum_fusion.refs_0_), channel_id=1, source_target_pairs={{16,0},{17,1},{0,16},{1,17},{18,2},{19,3},{2,18},{3,19},{20,4},{21... | collective-permute-start | bytes 393224 | tf_op jit(solution)/shard_map/ppermute | solution.py:58
  60.3 20.7 %collective-permute-start.5 = (bf16[4,4,16,256]{3,2,1,0:T(8,128)(2,1)S(1)}, bf16[4,4,16,256]{3,2,1,0:T(8,128)(2,1)S(1)}, u32[]{:S(2)}, u32[]{:S(2)}) collective-permute-start(bf16[4,4,16,256]{3,2,1,0:T(8,128)(2,1)S(1)} %pad_maximum_fusion.refs_0_), channel_id=1, source_target_pairs={{1,0},{0,1},{17,16},{16,17},{3,2},{2,3},{19,18},{18,19},{5,4},{4,5... | collective-permute-start | bytes 393224 | tf_op jit(solution)/shard_map/ppermute | solution.py:58
  60.6 20.9 %collective-permute-start.4 = (bf16[4,2,16,256]{3,2,1,0:T(8,128)(2,1)S(1)}, bf16[4,2,16,256]{3,2,1,0:T(8,128)(2,1)S(1)}, u32[]{:S(2)}, u32[]{:S(2)}) collective-permute-start(bf16[4,2,16,256]{3,2,1,0:T(8,128)(2,1)S(1)} %slice.46), channel_id=1, source_target_pairs={{0,8},{8,0},{1,9},{9,1},{2,10},{10,2},{3,11},{11,3},{4,12},{12,4},... | collective-permute-start | bytes 196616 | tf_op jit(solution)/shard_map/ppermute | solution.py:38
  79.8 1.7 %collective-permute-start.10 = (bf16[4,2,16,256]{3,2,1,0:T(8,128)(2,1)S(1)}, bf16[4,2,16,256]{3,2,1,0:T(8,128)(2,1)S(1)}, u32[]{:S(2)}, u32[]{:S(2)}) collective-permute-start(bf16[4,2,16,256]{3,2,1,0:T(8,128)(2,1)S(1)} %slice.58), channel_id=1, source_target_pairs={{0,8},{8,0},{1,9},{9,1},{2,10},{10,2},{3,11},{11,3},{4,12},{12,4},... | collective-permute-start | bytes 196616 | tf_op jit(solution)/shard_map/ppermute | solution.py:38
  80.8 1.3 collective-permute-start.8
  81.0 1.3 collective-permute-start.6
  83.0 0.8 copy-start.5
  88.6 3.6 %collective-permute-start.11 = (bf16[3,512,512]{2,1,0:T(8,128)(2,1)}, bf16[3,512,512]{2,1,0:T(8,128)(2,1)S(1)}, u32[]{:S(2)}, u32[]{:S(2)}) collective-permute-start(bf16[3,512,512]{2,1,0:T(8,128)(2,1)} %build.1.own_ref), channel_id=1, source_target_pairs={{0,8},{8,0},{1,9},{9,1},{2,10},{10,2},{3,11},{11,3},{4,12},{12,4},... | collective-permute-start | bytes 4718600 | tf_op jit(solution)/shard_map/ppermute | solution.py:38
  92.3 1.4 copy-start.1
  94.7 1.2 copy-start.3
  95.8 27.3 %copy-start.4 = (bf16[3,512,512]{2,1,0:T(8,128)(2,1)S(1)}, bf16[3,512,512]{2,1,0:T(8,128)(2,1)}, u32[]{:S(2)}) copy-start(bf16[3,512,512]{2,1,0:T(8,128)(2,1)} %copy-done.3) | copy-start | bytes 4718596
  96.9 26.3 %copy-start.2 = (bf16[3,512,512]{2,1,0:T(8,128)(2,1)S(1)}, bf16[3,512,512]{2,1,0:T(8,128)(2,1)}, u32[]{:S(2)}) copy-start(bf16[3,512,512]{2,1,0:T(8,128)(2,1)} %build.1.own_ref) | copy-start | bytes 4718596
  96.9 1.6 collective-permute-start.12
  108.8 4.9 %collective-permute-start.13 = (bf16[2,2,16,256]{3,2,1,0:T(8,128)(2,1)S(1)}, bf16[2,2,16,256]{3,2,1,0:T(8,128)(2,1)S(1)}, u32[]{:S(2)}, u32[]{:S(2)}) collective-permute-start(bf16[2,2,16,256]{3,2,1,0:T(8,128)(2,1)S(1)} %multiply_convert_fusion.3), channel_id=1, source_target_pairs={{0,4},{4,0},{1,5},{5,1},{2,6},{6,2},{3,7},{7,3},{8,12},{12,8},{9,1... | collective-permute-start | bytes 98312 | tf_op jit(solution)/shard_map/ppermute | solution.py:45
  124.9 1.6 collective-permute-start.14
  136.6 4.9 %collective-permute-start.15 = (bf16[2,2,16,256]{3,2,1,0:T(8,128)(2,1)S(1)}, bf16[2,2,16,256]{3,2,1,0:T(8,128)(2,1)S(1)}, u32[]{:S(2)}, u32[]{:S(2)}) collective-permute-start(bf16[2,2,16,256]{3,2,1,0:T(8,128)(2,1)S(1)} %multiply_convert_fusion.1), channel_id=1, source_target_pairs={{0,4},{4,0},{1,5},{5,1},{2,6},{6,2},{3,7},{7,3},{8,12},{12,8},{9,1... | collective-permute-start | bytes 98312 | tf_op jit(solution)/shard_map/ppermute | solution.py:45
  152.7 1.6 collective-permute-start.16
  167.6 1.2 collective-permute-start.17

commit v5 on v4

--- a/solution.py
+++ b/solution.py
@@ -157,6 +157,7 @@
     wide, narrow, block, half = mixed.shape[1:]
     rows = right_ref.shape[0] // total
     lanes = half // LANES
+    pitch = taken.shape[2]
     mixing = mixing_ref[...]
     stores = [
         pltpu.make_async_copy(mixed.at[h, w], out_ref.at[w // 2, h, :, w % 2], sems.at[h, w])
@@ -166,15 +167,18 @@
     for h in range(2):
         places = range(h * lanes, (h + 1) * lanes)
         for place in places:
-            taken[place] = right_ref[:, place * LANES : (place + 1) * LANES].astype(F32)
+            part = right_ref[:, place * LANES : (place + 1) * LANES].astype(F32)
+            taken[place, :, :rows] = part.reshape(total, rows, LANES)
+        flat_in = [taken.at[place].reshape(total * pitch, LANES) for place in places]
+        flat_out = [given.at[place].reshape(total * pitch, LANES) for place in places]
         for row in range(rows):
-            every = pl.ds(row, total, stride=rows)
-            one = jnp.concatenate([taken[place, every] for place in places], axis=1).astype(BF16)
+            every = pl.ds(row, total, stride=pitch)
+            one = jnp.concatenate([ref[every] for ref in flat_in], axis=1).astype(BF16)
             one = jnp.dot(mixing, one, preferred_element_type=F32)
-            for lane, place in enumerate(places):
-                given[place, every] = one[:, lane * LANES : (lane + 1) * LANES]
+            for lane, ref in enumerate(flat_out):
+                ref[every] = one[:, lane * LANES : (lane + 1) * LANES]
         for lane, place in enumerate(places):
-            done = given[place].astype(BF16).reshape(wide, narrow, block, LANES)
+            done = given[place, :, :rows].astype(BF16).reshape(wide, narrow, block, LANES)
             mixed[h, :, :, :, lane * LANES : (lane + 1) * LANES] = done
         for w in range(wide):
             stores[h * wide + w].start()
@@ -198,8 +202,8 @@
         out_specs=IN_HBM,
         out_shape=jax.ShapeDtypeStruct((wide // 2, 2, narrow, 2, block, half), BF16),
         scratch_shapes=[
-            pltpu.VMEM((states // LANES, size, LANES), F32),
-            pltpu.VMEM((states // LANES, size, LANES), F32),
+            pltpu.VMEM((states // LANES, total, size // total + 8, LANES), F32),
+            pltpu.VMEM((states // LANES, total, size // total + 8, LANES), F32),
             pltpu.VMEM((2, wide, narrow, block, half), BF16),
             pltpu.SemaphoreType.DMA((2, wide)),
         ],
@@ -223,24 +227,14 @@
             applied_ref[:, column : column + half] = one
 
 
-def term_shape(state_shape, last):
-    outer, cube, high, _, rows, half = state_shape
-    return (outer, high, cube, 2, rows, half) if last else state_shape
-
-
-def store_term(last, applied, joined, term_ref):
+def store_term(applied, joined, term_ref):
     outer, cube, high, _, rows, half = term_ref.shape
-    if last:
-        high, cube = cube, high
     joined = joined.reshape(half, -1)
     term = lax.dot_general(applied, joined, (((1,), (1,)), ((), ())), preferred_element_type=F32)
     term = term.astype(term_ref.dtype).reshape(outer, 2, high, cube, rows, half)
     for c in range(2):
         for h in range(high):
-            if last:
-                term_ref[:, h, :, c] = term[:, c, h]
-            else:
-                term_ref[:, :, h, c] = term[:, c, h]
+            term_ref[:, :, h, c] = term[:, c, h]
 
 
 def join_kernel(core_ref, applied_ref, comp_ref, keep_ref, send_ref, joined_ref):
@@ -251,13 +245,30 @@
         for n in range(2 * pairs):
             pair = n + pairs * (core if n < pairs else -core)
             joined_ref[k, :, :, n * half : (n + 1) * half] = comp_ref[pl.ds(place * chips, chips), pair]
-        store_term(False, applied_ref[...], joined_ref[k], term_ref)
-
-
-def apply_term_kernel(last, state_ref, own_ref, other_ref, joined_ref, keep_ref, send_ref, applied_ref):
+        store_term(applied_ref[...], joined_ref[k], term_ref)
+
+
+def apply_term_kernel(state_ref, own_ref, other_ref, joined_ref, keep_ref, send_ref, applied_ref):
     apply_kernel(state_ref, own_ref, other_ref, applied_ref)
     for k, term_ref in enumerate((send_ref, keep_ref)):
-        store_term(last, applied_ref[...], joined_ref[k], term_ref)
+        store_term(applied_ref[...], joined_ref[k], term_ref)
+
+
+def last_term_kernel(
+    core_ref, state_ref, own_ref, other_ref, joined_ref, keep_ref, send_ref, applied_ref
+):
+    apply_kernel(state_ref, own_ref, other_ref, applied_ref)
+    outer, narrow, _, rows, half = keep_ref.shape
+    count = narrow * rows
+    core = core_ref[0]
+    for c, term_ref in ((1 - core, send_ref), (core, keep_ref)):
+        starts = [pl.multiple_of((2 * o + c) * count, count) for o in range(outer)]
+        applied = jnp.concatenate([applied_ref[pl.ds(start, count)] for start in starts])
+        for k, place in enumerate((1 - core, core)):
+            joined = joined_ref[k].reshape(half, -1)
+            term = lax.dot_general(applied, joined, (((1,), (1,)), ((), ())), preferred_element_type=F32)
+            term = term.astype(term_ref.dtype).reshape(outer, narrow, rows, half)
+            term_ref[:, :, place] = term
 
 
 def local_call(kernel, name, mib, *out, scratch=(), flops=0):
@@ -301,33 +312,50 @@
         split = jnp.stack([split[1 - core], split[core]])
         split = jnp.concatenate([split[:, :, core], split[:, :, 1 - core]], axis=2)
         joined = split.transpose(0, 1, 3, 2, 4).reshape(2, devices // 2, rows, both * half)
-        return *terms_of(applied, joined, shape, False), joined
+        return *terms_of(applied, joined, shape), joined
     out = (shape, F32), (shape, BF16), ((2, devices // 2, rows, both * half), BF16)
     flops = 2 * devices * rows * applied.size
     call = local_call(join_kernel, "join_terms", 12, *out, flops=flops)
     return call(core.reshape(1), applied, comp)
 
 
-def terms_of(applied, joined, shape, last):
+def all_terms(applied, joined, shape):
     outer, cube, high, _, rows, half = shape
     joined = joined.reshape(2, half, -1)
     term = jnp.einsum("ix,kjx->kij", applied, joined, preferred_element_type=F32)
-    term = term.reshape(2, outer, 2, high, cube, rows, half)
-    term = term.transpose((0, 1, 3, 4, 2, 5, 6) if last else (0, 1, 4, 3, 2, 5, 6))
+    return term.reshape(2, outer, 2, high, cube, rows, half)
+
+
+def terms_of(applied, joined, shape):
+    term = all_terms(applied, joined, shape).transpose(0, 1, 4, 3, 2, 5, 6)
     return term[1], term[0].astype(BF16)
 
 
-def apply_and_terms(state, own, other, joined, last):
+def apply_and_terms(state, own, other, joined):
     pairs, states, _ = own.shape
     half = state.shape[-1]
     if state.shape[-2] % 16:
-        return terms_of(apply_pairs(state, own, other), joined, state.shape, last)
+        return terms_of(apply_pairs(state, own, other), joined, state.shape)
     scratch = [pltpu.VMEM((states, 2 * pairs * half), BF16)]
-    shape = term_shape(state.shape, last)
+    out = (state.shape, F32), (state.shape, BF16)
     flops = 8 * pairs * states**2 * half
-    kernel = functools.partial(apply_term_kernel, last)
-    call = local_call(kernel, "apply_terms", 12, (shape, F32), (shape, BF16), scratch=scratch, flops=flops)
+    call = local_call(apply_term_kernel, "apply_terms", 12, *out, scratch=scratch, flops=flops)
     return call(state, own, other, joined)
+
+
+def apply_and_last_terms(core, state, own, other, joined):
+    outer, cube, high, _, rows, half = state.shape
+    pairs, states, _ = own.shape
+    shape = (outer, high * cube, 2, rows, half)
+    if rows % 16:
+        term = all_terms(apply_pairs(state, own, other), joined, state.shape)
+        term = term.reshape(2, outer, 2, high * cube, rows, half)
+        term = jnp.where(core == 1, term, term[::-1]).transpose(2, 1, 3, 0, 4, 5)
+        return term[core], term[1 - core].astype(BF16)
+    scratch = [pltpu.VMEM((states, 2 * pairs * half), BF16)]
+    flops = 8 * pairs * states**2 * half
+    call = local_call(last_term_kernel, "last_terms", 12, (shape, F32), (shape, BF16), scratch=scratch, flops=flops)
+    return call(core.reshape(1), state, own, other, joined)
 
 
 def local(site_basis, left_ops, right_ops, integrals, wavefunction, pair_order, sector_sizes):
@@ -366,6 +394,9 @@
     own_columns = own_half(blocks)
     cube_mask = (jnp.abs(cube_rows[..., None] - own_columns) <= 2.0).astype(F32)
     local_mask = lax.dynamic_index_in_dim(cube_mask, own_high, 0, keepdims=False)
+    own_row = lax.axis_index(ALL) * rows
+    own_rows = lax.dynamic_slice_in_dim(blocks, own_row, rows, 0)
+    row_mask = (jnp.abs(own_rows[:, None] - blocks.reshape(2, 1, half)) <= 2.0).astype(F32)
 
     piece = by_core(own_half(wavefunction), swap_cores(other_half(wavefunction)))
     piece = (piece.astype(F32) * local_mask).astype(BF16)
@@ -373,8 +404,8 @@
 
     halves = jnp.stack([site_basis[:, :half], site_basis[:, half:]])
     packet = jnp.concatenate([halves, piece])
-    packet, local_mask, cube_mask, summed = lax.optimization_barrier(
-        (packet, local_mask, cube_mask, summed)
+    packet, cube_mask, row_mask, summed = lax.optimization_barrier(
+        (packet, cube_mask, row_mask, summed)
     )
     mixed = mix(mixing, right_rows, wide, narrow, pairs * rows)
     packets, mixed = lax.optimization_barrier((jnp.stack(send_round(packet, (HIGH, LOW), high * low)), mixed))
@@ -392,35 +423,37 @@
     comp = comp.reshape(devices, 2 * pairs, rows, half)
 
     step_size = 2.0 / math.sqrt(pair_total)
-    for order_index in range(1, ORDER + 1):
-        last = order_index == ORDER
+    for order_index in range(1, ORDER):
         if order_index == 1:
             keep, send, joined = join_terms(own_core, applied, comp, state.shape)
         else:
-            keep, send = apply_and_terms(state, own_built, other_built, joined, last)
+            keep, send = apply_and_terms(state, own_built, other_built, joined)
         partial = (keep + swap_cores(send).astype(F32)).astype(BF16)
-        factor = -(step_size / order_index)
-        if last:
-            partial = partial.reshape(chips, 2 * rows, half)
-            arrived = lax.all_to_all(partial, CHIPS, split_axis=0, concat_axis=0, tiled=True)
-            term = jnp.sum(arrived.astype(F32), axis=0).reshape(2, rows, half)
-            piece = (factor * local_mask * term).astype(BF16)
-        else:
-            partial = partial.reshape(chips // high, high * 2 * rows, half)
-            arrived = lax.all_to_all(partial, CUBE, split_axis=0, concat_axis=0, tiled=True)
-            term = jnp.sum(arrived.astype(F32), axis=0).reshape(cube_mask.shape)
-            term = add_high(cube_mask * term)
-            pieces = (factor * cube_mask * term).astype(BF16)
-            piece = lax.dynamic_index_in_dim(pieces, own_high, 0, keepdims=False)
-            copies = jnp.broadcast_to(pieces.reshape(partial.shape[1:]), partial.shape)
-            state = lax.all_to_all(copies, CUBE, split_axis=0, concat_axis=0, tiled=True)
-            state = state.reshape(outer, low * near, high, 2, rows, half)
+        partial = partial.reshape(chips // high, high * 2 * rows, half)
+        arrived = lax.all_to_all(partial, CUBE, split_axis=0, concat_axis=0, tiled=True)
+        term = jnp.sum(arrived.astype(F32), axis=0).reshape(cube_mask.shape)
+        term = add_high(cube_mask * term)
+        pieces = (-(step_size / order_index) * cube_mask * term).astype(BF16)
+        piece = lax.dynamic_index_in_dim(pieces, own_high, 0, keepdims=False)
         summed = summed + piece.astype(F32)
-
-    mine = jnp.where(is_high, summed[1], summed[0])
-    theirs = jnp.where(is_high, summed[0], summed[1])
-    left, right = by_core(mine, swap_cores(theirs))
-    return jnp.concatenate([left, right], axis=1)
+        copies = jnp.broadcast_to(pieces.reshape(partial.shape[1:]), partial.shape)
+        mine = jnp.where(is_high, summed[1], summed[0])
+        theirs = jnp.where(is_high, summed[0], summed[1])
+        copies, summed, mine, theirs = lax.optimization_barrier((copies, summed, mine, theirs))
+        state = lax.all_to_all(copies, CUBE, split_axis=0, concat_axis=0, tiled=True)
+        state = state.reshape(outer, low * near, high, 2, rows, half)
+
+    keep, send = apply_and_last_terms(own_core, state, own_built, other_built, joined)
+    theirs, send = lax.optimization_barrier((theirs, send))
+    theirs, send = lax.optimization_barrier((swap_cores(theirs), swap_cores(send)))
+    summed = by_core(mine, theirs)
+    partial = (keep + send.astype(F32)).astype(BF16).reshape(chips, 2 * rows, half)
+    partial, summed = lax.optimization_barrier((partial, summed))
+    arrived = lax.all_to_all(partial, CHIPS, split_axis=0, concat_axis=0, tiled=True)
+    term = jnp.sum(arrived.astype(F32), axis=0).reshape(2, rows, half)
+    piece = (-(step_size / ORDER) * row_mask * term).astype(BF16)
+    summed = summed + piece.astype(F32)
+    return jnp.concatenate([summed[0], summed[1]], axis=1)
 
 
 def solution(mesh):

time: 170 us -> 168 us (0.988)
  waiting for transfers between devices: 69.6 us -> 67.8 us
  transfers between devices with their start and end apart: 20 -> 20, of which waited for: 14 -> 13; matrix products, arithmetic and copies ran while one was open for 1% -> 1% of each run, Pallas kernels for 4% -> 4%
where the time goes in v5:
time: 168 us
  waiting for transfers between devices  67.8 us (40%)
  blocking collectives  51.9 us (31%)
  starting transfers between devices  24.4 us (15%)
  Pallas kernels  16 us (10%)
  local copies, waits for them, and re-layouts  5.22 us (3%)
  other arithmetic  1.73 us (1%)
    ppermute x6, waiting for transfers between devices, send_round(): lax.ppermute(value, axes, [(partner(i, k, size), i) for i in range(size)])  53.5 us
    all_to_all x2, blocking collectives, local(): lax.all_to_all(partial, CUBE, split_axis=0, concat_axis=0, tiled=True)  20.1 us
    all_to_all x2, blocking collectives, local(): lax.all_to_all(copies, CUBE, split_axis=0, concat_axis=0, tiled=True)  18.8 us
    all_to_all x1, blocking collectives, local(): lax.all_to_all(partial, CHIPS, split_axis=0, concat_axis=0, tiled=True)  13 us
    ppermute x6, starting transfers between devices, send_round(): lax.ppermute(value, axes, [(partner(i, k, size), i) for i in range(size)])  8.01 us
    ppermute x10, waiting for transfers between devices, swap_cores(): return lax.ppermute(value, CORE, [(0, 1), (1, 0)])  7.84 us
    all_to_all x1, starting transfers between devices, local(): lax.all_to_all(parts, ALL, split_axis=0, concat_axis=0, tiled=True)  7.3 us
    ppermute x2, waiting for transfers between devices, add_high(): other = lax.ppermute(rounded, HIGH, [(0, 1), (1, 0)])  6.44 us
  transfers between devices with their start and end apart: 20, of which 13 were waited for; matrix products, arithmetic and copies ran while one was open for 1% of the time, Pallas kernels for 4%

profile of v5, /device:TPU:0, one launch (start us, length us, event | category | flops | bytes accessed | tf_op | source)
XLA Modules:
  0.0 167.5 jit_solution(7105789973223300922)
XLA Ops:
  0.0 2.3 %deal_rows.1 = bf16[32,3,16,512]{3,2,1,0:T(8,128)(2,1)} custom-call(bf16[3,32,16,512]{3,2,1,0:T(8,128)(2,1)} %bitcast.67), custom_call_target="tpu_custom_call" | custom-call | tf_op jit(solution)/shard_map/deal_rows/pallas_call | solution.py:116
  2.3 7.3 %all-to-all-start = ((bf16[32,48,512]{2,1,0:T(8,128)(2,1)}), bf16[32,48,512]{2,1,0:T(8,128)(2,1)S(1)}, u32[]{:S(2)}, u32[]{:S(2)}) async-start(bf16[32,48,512]{2,1,0:T(8,128)(2,1)} %bitcast.66), calls=%async_computation | async-start | bytes 3145728 | tf_op jit(solution)/shard_map/all_to_all | solution.py:385
  9.7 0.3 collective-permute-start
  10.0 0.2 reduce-window.8
  10.5 0.7 gather_fusion
  11.2 0.1 copy.15
  11.5 0.7 gather_fusion.1
  12.4 3.6 %collective-permute-start.3 = (bf16[4,16,256]{2,1,0:T(8,128)(2,1)S(1)}, bf16[4,16,256]{2,1,0:T(8,128)(2,1)S(1)}, u32[]{:S(2)}, u32[]{:S(2)}) collective-permute-start(bf16[4,16,256]{2,1,0:T(8,128)(2,1)S(1)} %pad_maximum_fusion.1), channel_id=1, source_target_pairs={{6,0},{4,2},{2,4},{0,6},{7,1},{5,3},{3,5},{1,7},{14,8},{12,10},{10... | collective-permute-start | bytes 98312 | tf_op jit(solution)/shard_map/ppermute | solution.py:58
  16.0 0.9 collective-permute-start.1
  16.8 24.0 %collective-permute-done.3 = bf16[4,16,256]{2,1,0:T(8,128)(2,1)S(1)} collective-permute-done((bf16[4,16,256]{2,1,0:T(8,128)(2,1)S(1)}, bf16[4,16,256]{2,1,0:T(8,128)(2,1)S(1)}, u32[]{:S(2)}, u32[]{:S(2)}) %collective-permute-start.3) | collective-permute-done | bytes 32800 | tf_op jit(solution)/shard_map/ppermute | solution.py:58
  40.8 9.1 %collective-permute-done.2 = bf16[4,16,256]{2,1,0:T(8,128)(2,1)S(1)} collective-permute-done((bf16[4,16,256]{2,1,0:T(8,128)(2,1)S(1)}, bf16[4,16,256]{2,1,0:T(8,128)(2,1)S(1)}, u32[]{:S(2)}, u32[]{:S(2)}) %collective-permute-start.2) | collective-permute-done | bytes 32800 | tf_op jit(solution)/shard_map/ppermute | solution.py:58
  50.0 2.5 %mix.1 = bf16[2,2,8,2,48,256]{5,4,3,2,1,0:T(8,128)(2,1)} custom-call(bf16[96,96]{1,0:T(8,128)(2,1)S(1)} %select_bitcast_fusion.mixing_ref, bf16[1536,512]{1,0:T(8,128)(2,1)S(1)} %bitcast.61), custom_call_target="tpu_custom_call" | custom-call | flops 150994944 | bytes 3145728 | tf_op jit(solution)/shard_map/mix/pallas_call | solution.py:199
  52.4 3.6 %all-to-all-start.1 = ((bf16[32,96,256]{2,1,0:T(8,128)(2,1)}), bf16[32,96,256]{2,1,0:T(8,128)(2,1)S(1)}, u32[]{:S(2)}, u32[]{:S(2)}) async-start(bf16[32,96,256]{2,1,0:T(8,128)(2,1)} %bitcast.21), calls=%async_computation.1 | async-start | bytes 3145728 | tf_op jit(solution)/shard_map/all_to_all | solution.py:422
  56.1 2.7 %collective-permute-start.9 = (bf16[4,4,16,256]{3,2,1,0:T(8,128)(2,1)S(1)}, bf16[4,4,16,256]{3,2,1,0:T(8,128)(2,1)S(1)}, u32[]{:S(2)}, u32[]{:S(2)}) collective-permute-start(bf16[4,4,16,256]{3,2,1,0:T(8,128)(2,1)S(1)} %pad_maximum_fusion.refs_0_), channel_id=1, source_target_pairs={{17,0},{16,1},{1,16},{0,17},{19,2},{18,3},{3,18},{2,19},{21,4},{20... | collective-permute-start | bytes 393224 | tf_op jit(solution)/shard_map/ppermute | solution.py:58
  58.8 0.6 collective-permute-start.7
  59.4 0.3 collective-permute-start.5
  59.6 19.2 %collective-permute-done.9.refs_6_ = bf16[4,4,16,256]{3,2,1,0:T(8,128)(2,1)S(1)} collective-permute-done((bf16[4,4,16,256]{3,2,1,0:T(8,128)(2,1)S(1)}, bf16[4,4,16,256]{3,2,1,0:T(8,128)(2,1)S(1)}, u32[]{:S(2)}, u32[]{:S(2)}) %collective-permute-start.9) | collective-permute-done | bytes 131104 | tf_op jit(solution)/shard_map/ppermute | solution.py:58
  78.9 1.0 collective-permute-done.7.refs_4_
  79.9 0.2 collective-permute-done.5.refs_2_
  80.1 0.4 collective-permute-start.6
  80.6 0.6 collective-permute-done.8.refs_5_
  81.2 0.2 collective-permute-done.6.refs_3_
  81.4 0.7 place_slots.1
  82.1 0.8 copy-done.5
  82.9 4.8 %build.1.own_ref = bf16[3,512,512]{2,1,0:T(8,128)(2,1)} custom-call(bf16[512,512]{1,0:T(8,128)(2,1)} %bitcast.63, bf16[3,512,512]{2,1,0:T(8,128)(2,1)} %left_ref.1), custom_call_target="tpu_custom_call" | custom-call | tf_op jit(solution)/shard_map/build/pallas_call | solution.py:140
  87.7 0.4 collective-permute-start.11
  88.1 3.3 %collective-permute-done.11.other_ref = bf16[3,512,512]{2,1,0:T(8,128)(2,1)S(1)} collective-permute-done((bf16[3,512,512]{2,1,0:T(8,128)(2,1)}, bf16[3,512,512]{2,1,0:T(8,128)(2,1)S(1)}, u32[]{:S(2)}, u32[]{:S(2)}) %collective-permute-start.11) | collective-permute-done | bytes 1572896 | tf_op jit(solution)/shard_map/ppermute | solution.py:38
  91.3 1.4 copy-done.1
  92.7 1.0 apply_pairs.1.applied_ref
  93.7 1.2 copy-done.3
  94.9 1.0 join_terms.1
  95.9 0.4 collective-permute-start.12
  96.4 1.2 collective-permute-done.12
  97.6 10.2 %all_to_all.35 = bf16[8,64,256]{2,1,0:T(8,128)(2,1)S(1)} all-to-all(bf16[8,64,256]{2,1,0:T(8,128)(2,1)S(1)} %bitcast.69), channel_id=1, replica_groups=mesh['outer'=2,'core'=2,'high'=2,'low'=2,'near'=2] {'outer','low','near'}, dimensions={0} | all-to-all | bytes 524288 | tf_op jit(solution)/shard_map/all_to_all | solution.py:433
  107.9 1.7 collective-permute-start.13
  109.5 3.2 %collective-permute-done.13 = bf16[2,2,16,256]{3,2,1,0:T(8,128)(2,1)S(1)} collective-permute-done((bf16[2,2,16,256]{3,2,1,0:T(8,128)(2,1)S(1)}, bf16[2,2,16,256]{3,2,1,0:T(8,128)(2,1)S(1)}, u32[]{:S(2)}, u32[]{:S(2)}) %collective-permute-start.13) | collective-permute-done | bytes 32800 | tf_op jit(solution)/shard_map/ppermute | solution.py:45
  112.8 9.4 %all_to_all.36 = bf16[8,64,256]{2,1,0:T(8,128)(2,1)S(1)} all-to-all(bf16[8,64,256]{2,1,0:T(8,128)(2,1)S(1)} %broadcast_in_dim.34), channel_id=1, replica_groups=mesh['outer'=2,'core'=2,'high'=2,'low'=2,'near'=2] {'outer','low','near'}, dimensions={0} | all-to-all | bytes 524288 | tf_op jit(solution)/shard_map/all_to_all | solution.py:443
  122.2 1.8 %apply_terms.1 = (f32[2,4,2,2,16,256]{5,4,3,2,1,0:T(8,128)S(1)}, bf16[2,4,2,2,16,256]{5,4,3,2,1,0:T(8,128)(2,1)S(1)}) custom-call(bf16[2,4,2,2,16,256]{5,4,3,2,1,0:T(8,128)(2,1)S(1)} %bitcast.65, bf16[3,512,512]{2,1,0:T(8,128)(2,1)S(1)} %copy-done.2, bf16[3,512,512]{2,1,0:T(8,128)(2,1)S(1)} %copy-done.4, ...), custom_call_target="tpu_custom_call" | custom-call | flops 1610612736 | bytes 4980736 | tf_op jit(solution)/shard_map/apply_terms/pallas_call | solution.py:280
  124.1 1.5 collective-permute-done.14
  125.7 10.0 %all_to_all.37 = bf16[8,64,256]{2,1,0:T(8,128)(2,1)S(1)} all-to-all(bf16[8,64,256]{2,1,0:T(8,128)(2,1)S(1)} %bitcast.70), channel_id=1, replica_groups=mesh['outer'=2,'core'=2,'high'=2,'low'=2,'near'=2] {'outer','low','near'}, dimensions={0} | all-to-all | bytes 524288 | tf_op jit(solution)/shard_map/all_to_all | solution.py:433
  135.7 1.7 collective-permute-start.15
  137.4 3.2 %collective-permute-done.15 = bf16[2,2,16,256]{3,2,1,0:T(8,128)(2,1)S(1)} collective-permute-done((bf16[2,2,16,256]{3,2,1,0:T(8,128)(2,1)S(1)}, bf16[2,2,16,256]{3,2,1,0:T(8,128)(2,1)S(1)}, u32[]{:S(2)}, u32[]{:S(2)}) %collective-permute-start.15) | collective-permute-done | bytes 32800 | tf_op jit(solution)/shard_map/ppermute | solution.py:45
  140.7 9.4 %all_to_all.38 = bf16[8,64,256]{2,1,0:T(8,128)(2,1)S(1)} all-to-all(bf16[8,64,256]{2,1,0:T(8,128)(2,1)S(1)} %broadcast_in_dim.35), channel_id=1, replica_groups=mesh['outer'=2,'core'=2,'high'=2,'low'=2,'near'=2] {'outer','low','near'}, dimensions={0} | all-to-all | bytes 524288 | tf_op jit(solution)/shard_map/all_to_all | solution.py:443
  150.1 2.0 %last_terms.1 = (f32[2,8,2,16,256]{4,3,2,1,0:T(8,128)S(1)}, bf16[2,8,2,16,256]{4,3,2,1,0:T(8,128)(2,1)S(1)}) custom-call(s32[1]{0:T(128)} %bitcast.core_ref, bf16[2,4,2,2,16,256]{5,4,3,2,1,0:T(8,128)(2,1)S(1)} %bitcast.64, bf16[3,512,512]{2,1,0:T(8,128)(2,1)S(1)} %copy-done.2, bf16[3,512,512]{2,1,0:T(8,128)(2,1)S(1)} %copy-done.4, ...), custom_call_target="tpu_custom_call" | custom-call | flops 1610612736 | bytes 4980738 | tf_op jit(solution)/shard_map/last_terms/pallas_call | solution.py:280
  152.1 0.5 collective-permute-start.16
  152.6 1.0 collective-permute-done.16
  153.8 13.0 %all_to_all.39 = bf16[16,32,256]{2,1,0:T(8,128)(2,1)S(1)} all-to-all(bf16[16,32,256]{2,1,0:T(8,128)(2,1)S(1)} %bitcast.68), channel_id=1, replica_groups=mesh['outer'=2,'core'=2,'high'=2,'low'=2,'near'=2] {'outer','high','low'..., dimensions={0} | all-to-all | bytes 524288 | tf_op jit(solution)/shard_map/all_to_all | solution.py:452
  166.9 0.6 pad_maximum_fusion.3
  (76 shorter events, 1.5 us)
Async XLA Ops:
  0.0 10.5 %copy-start = (bf16[96,96]{1,0:T(8,128)(2,1)S(1)}, bf16[96,96]{1,0:T(8,128)(2,1)}, u32[]{:S(2)}) copy-start(bf16[96,96]{1,0:T(8,128)(2,1)} %param.10) | copy-start | bytes 55300
  2.3 7.4 %copy-start.6 = (bf16[16,512]{1,0:T(8,128)(2,1)S(1)}, bf16[16,512]{1,0:T(8,128)(2,1)}, u32[]{:S(2)}) copy-start(bf16[16,512]{1,0:T(8,128)(2,1)} %param.11) | copy-start | bytes 49156
  2.3 7.7 %copy-start.8 = (s32[8]{0:T(128)S(1)}, s32[8]{0:T(128)}, u32[]{:S(2)}) copy-start(s32[8]{0:T(128)} %param.13) | copy-start | bytes 100
  2.3 8.2 %copy-start.9 = (s32[96]{0:T(128)S(1)}, s32[96]{0:T(128)}, u32[]{:S(2)}) copy-start(s32[96]{0:T(128)} %param.12) | copy-start | bytes 1156
  2.3 9.2 %copy-start.7 = (bf16[16,512]{1,0:T(8,128)(2,1)S(1)}, bf16[16,512]{1,0:T(8,128)(2,1)}, u32[]{:S(2)}) copy-start(bf16[16,512]{1,0:T(8,128)(2,1)} %param.7) | copy-start | bytes 49156
  2.3 47.6 %all-to-all-start = ((bf16[32,48,512]{2,1,0:T(8,128)(2,1)}), bf16[32,48,512]{2,1,0:T(8,128)(2,1)S(1)}, u32[]{:S(2)}, u32[]{:S(2)}) async-start(bf16[32,48,512]{2,1,0:T(8,128)(2,1)} %bitcast.66), calls=%async_computation | async-start | bytes 3145728 | tf_op jit(solution)/shard_map/all_to_all | solution.py:385
  9.7 2.6 %collective-permute-start = (bf16[16,256]{1,0:T(8,128)(2,1)S(1)}, bf16[16,256]{1,0:T(8,128)(2,1)S(1)}, u32[]{:S(2)}, u32[]{:S(2)}) collective-permute-start(bf16[16,256]{1,0:T(8,128)(2,1)S(1)} %broadcast_select_fusion.2), channel_id=1, source_target_pairs={{0,8},{8,0},{1,9},{9,1},{2,10},{10,2},{3,11},{11,3},{4,12},{12,4},... | collective-permute-start | bytes 24584 | tf_op jit(solution)/shard_map/ppermute | solution.py:38
  12.4 28.5 %collective-permute-start.3 = (bf16[4,16,256]{2,1,0:T(8,128)(2,1)S(1)}, bf16[4,16,256]{2,1,0:T(8,128)(2,1)S(1)}, u32[]{:S(2)}, u32[]{:S(2)}) collective-permute-start(bf16[4,16,256]{2,1,0:T(8,128)(2,1)S(1)} %pad_maximum_fusion.1), channel_id=1, source_target_pairs={{6,0},{4,2},{2,4},{0,6},{7,1},{5,3},{3,5},{1,7},{14,8},{12,10},{10... | collective-permute-start | bytes 98312 | tf_op jit(solution)/shard_map/ppermute | solution.py:58
  16.0 33.9 %collective-permute-start.2 = (bf16[4,16,256]{2,1,0:T(8,128)(2,1)S(1)}, bf16[4,16,256]{2,1,0:T(8,128)(2,1)S(1)}, u32[]{:S(2)}, u32[]{:S(2)}) collective-permute-start(bf16[4,16,256]{2,1,0:T(8,128)(2,1)S(1)} %pad_maximum_fusion.1), channel_id=1, source_target_pairs={{4,0},{6,2},{0,4},{2,6},{5,1},{7,3},{1,5},{3,7},{12,8},{14,10},{8,... | collective-permute-start | bytes 98312 | tf_op jit(solution)/shard_map/ppermute | solution.py:58
  16.0 33.9 %collective-permute-start.1 = (bf16[4,16,256]{2,1,0:T(8,128)(2,1)S(1)}, bf16[4,16,256]{2,1,0:T(8,128)(2,1)S(1)}, u32[]{:S(2)}, u32[]{:S(2)}) collective-permute-start(bf16[4,16,256]{2,1,0:T(8,128)(2,1)S(1)} %pad_maximum_fusion.1), channel_id=1, source_target_pairs={{2,0},{0,2},{6,4},{4,6},{3,1},{1,3},{7,5},{5,7},{10,8},{8,10},{14,... | collective-permute-start | bytes 98312 | tf_op jit(solution)/shard_map/ppermute | solution.py:58
  52.4 42.5 %all-to-all-start.1 = ((bf16[32,96,256]{2,1,0:T(8,128)(2,1)}), bf16[32,96,256]{2,1,0:T(8,128)(2,1)S(1)}, u32[]{:S(2)}, u32[]{:S(2)}) async-start(bf16[32,96,256]{2,1,0:T(8,128)(2,1)} %bitcast.21), calls=%async_computation.1 | async-start | bytes 3145728 | tf_op jit(solution)/shard_map/all_to_all | solution.py:422
  56.1 22.8 %collective-permute-start.9 = (bf16[4,4,16,256]{3,2,1,0:T(8,128)(2,1)S(1)}, bf16[4,4,16,256]{3,2,1,0:T(8,128)(2,1)S(1)}, u32[]{:S(2)}, u32[]{:S(2)}) collective-permute-start(bf16[4,4,16,256]{3,2,1,0:T(8,128)(2,1)S(1)} %pad_maximum_fusion.refs_0_), channel_id=1, source_target_pairs={{17,0},{16,1},{1,16},{0,17},{19,2},{18,3},{3,18},{2,19},{21,4},{20... | collective-permute-start | bytes 393224 | tf_op jit(solution)/shard_map/ppermute | solution.py:58
  58.8 21.1 %collective-permute-start.7 = (bf16[4,4,16,256]{3,2,1,0:T(8,128)(2,1)S(1)}, bf16[4,4,16,256]{3,2,1,0:T(8,128)(2,1)S(1)}, u32[]{:S(2)}, u32[]{:S(2)}) collective-permute-start(bf16[4,4,16,256]{3,2,1,0:T(8,128)(2,1)S(1)} %pad_maximum_fusion.refs_0_), channel_id=1, source_target_pairs={{16,0},{17,1},{0,16},{1,17},{18,2},{19,3},{2,18},{3,19},{20,4},{21... | collective-permute-start | bytes 393224 | tf_op jit(solution)/shard_map/ppermute | solution.py:58
  59.4 20.7 %collective-permute-start.5 = (bf16[4,4,16,256]{3,2,1,0:T(8,128)(2,1)S(1)}, bf16[4,4,16,256]{3,2,1,0:T(8,128)(2,1)S(1)}, u32[]{:S(2)}, u32[]{:S(2)}) collective-permute-start(bf16[4,4,16,256]{3,2,1,0:T(8,128)(2,1)S(1)} %pad_maximum_fusion.refs_0_), channel_id=1, source_target_pairs={{1,0},{0,1},{17,16},{16,17},{3,2},{2,3},{19,18},{18,19},{5,4},{4,5... | collective-permute-start | bytes 393224 | tf_op jit(solution)/shard_map/ppermute | solution.py:58
  59.6 20.9 %collective-permute-start.4 = (bf16[4,2,16,256]{3,2,1,0:T(8,128)(2,1)S(1)}, bf16[4,2,16,256]{3,2,1,0:T(8,128)(2,1)S(1)}, u32[]{:S(2)}, u32[]{:S(2)}) collective-permute-start(bf16[4,2,16,256]{3,2,1,0:T(8,128)(2,1)S(1)} %slice.56), channel_id=1, source_target_pairs={{0,8},{8,0},{1,9},{9,1},{2,10},{10,2},{3,11},{11,3},{4,12},{12,4},... | collective-permute-start | bytes 196616 | tf_op jit(solution)/shard_map/ppermute | solution.py:38
  78.8 1.7 %collective-permute-start.10 = (bf16[4,2,16,256]{3,2,1,0:T(8,128)(2,1)S(1)}, bf16[4,2,16,256]{3,2,1,0:T(8,128)(2,1)S(1)}, u32[]{:S(2)}, u32[]{:S(2)}) collective-permute-start(bf16[4,2,16,256]{3,2,1,0:T(8,128)(2,1)S(1)} %slice.70), channel_id=1, source_target_pairs={{0,8},{8,0},{1,9},{9,1},{2,10},{10,2},{3,11},{11,3},{4,12},{12,4},... | collective-permute-start | bytes 196616 | tf_op jit(solution)/shard_map/ppermute | solution.py:38
  79.9 1.3 collective-permute-start.8
  80.1 1.3 collective-permute-start.6
  82.1 0.8 copy-start.5
  87.7 3.6 %collective-permute-start.11 = (bf16[3,512,512]{2,1,0:T(8,128)(2,1)}, bf16[3,512,512]{2,1,0:T(8,128)(2,1)S(1)}, u32[]{:S(2)}, u32[]{:S(2)}) collective-permute-start(bf16[3,512,512]{2,1,0:T(8,128)(2,1)} %build.1.own_ref), channel_id=1, source_target_pairs={{0,8},{8,0},{1,9},{9,1},{2,10},{10,2},{3,11},{11,3},{4,12},{12,4},... | collective-permute-start | bytes 4718600 | tf_op jit(solution)/shard_map/ppermute | solution.py:38
  91.3 1.4 copy-start.1
  93.7 1.2 copy-start.3
  94.9 27.3 %copy-start.4 = (bf16[3,512,512]{2,1,0:T(8,128)(2,1)S(1)}, bf16[3,512,512]{2,1,0:T(8,128)(2,1)}, u32[]{:S(2)}) copy-start(bf16[3,512,512]{2,1,0:T(8,128)(2,1)} %copy-done.3) | copy-start | bytes 4718596
  95.9 26.3 %copy-start.2 = (bf16[3,512,512]{2,1,0:T(8,128)(2,1)S(1)}, bf16[3,512,512]{2,1,0:T(8,128)(2,1)}, u32[]{:S(2)}) copy-start(bf16[3,512,512]{2,1,0:T(8,128)(2,1)} %build.1.own_ref) | copy-start | bytes 4718596
  95.9 1.6 collective-permute-start.12
  107.9 4.9 %collective-permute-start.13 = (bf16[2,2,16,256]{3,2,1,0:T(8,128)(2,1)S(1)}, bf16[2,2,16,256]{3,2,1,0:T(8,128)(2,1)S(1)}, u32[]{:S(2)}, u32[]{:S(2)}) collective-permute-start(bf16[2,2,16,256]{3,2,1,0:T(8,128)(2,1)S(1)} %multiply_convert_fusion.3), channel_id=1, source_target_pairs={{0,4},{4,0},{1,5},{5,1},{2,6},{6,2},{3,7},{7,3},{8,12},{12,8},{9,1... | collective-permute-start | bytes 98312 | tf_op jit(solution)/shard_map/ppermute | solution.py:45
  124.0 1.6 collective-permute-start.14
  135.7 4.9 %collective-permute-start.15 = (bf16[2,2,16,256]{3,2,1,0:T(8,128)(2,1)S(1)}, bf16[2,2,16,256]{3,2,1,0:T(8,128)(2,1)S(1)}, u32[]{:S(2)}, u32[]{:S(2)}) collective-permute-start(bf16[2,2,16,256]{3,2,1,0:T(8,128)(2,1)S(1)} %multiply_convert_fusion.1), channel_id=1, source_target_pairs={{0,4},{4,0},{1,5},{5,1},{2,6},{6,2},{3,7},{7,3},{8,12},{12,8},{9,1... | collective-permute-start | bytes 98312 | tf_op jit(solution)/shard_map/ppermute | solution.py:45
  152.0 1.6 collective-permute-start.17
  152.1 1.5 collective-permute-start.16

commit v6 on v5

--- a/solution.py
+++ b/solution.py
@@ -168,9 +168,9 @@
         places = range(h * lanes, (h + 1) * lanes)
         for place in places:
             part = right_ref[:, place * LANES : (place + 1) * LANES].astype(F32)
-            taken[place, :, :rows] = part.reshape(total, rows, LANES)
-        flat_in = [taken.at[place].reshape(total * pitch, LANES) for place in places]
-        flat_out = [given.at[place].reshape(total * pitch, LANES) for place in places]
+            taken[place, :total, :rows] = part.reshape(total, rows, LANES)
+        flat_in = [taken.at[place].reshape((total + 1) * pitch, LANES) for place in places]
+        flat_out = [given.at[place].reshape((total + 1) * pitch, LANES) for place in places]
         for row in range(rows):
             every = pl.ds(row, total, stride=pitch)
             one = jnp.concatenate([ref[every] for ref in flat_in], axis=1).astype(BF16)
@@ -178,7 +178,7 @@
             for lane, ref in enumerate(flat_out):
                 ref[every] = one[:, lane * LANES : (lane + 1) * LANES]
         for lane, place in enumerate(places):
-            done = given[place, :, :rows].astype(BF16).reshape(wide, narrow, block, LANES)
+            done = given[place, :total, :rows].astype(BF16).reshape(wide, narrow, block, LANES)
             mixed[h, :, :, :, lane * LANES : (lane + 1) * LANES] = done
         for w in range(wide):
             stores[h * wide + w].start()
@@ -202,8 +202,8 @@
         out_specs=IN_HBM,
         out_shape=jax.ShapeDtypeStruct((wide // 2, 2, narrow, 2, block, half), BF16),
         scratch_shapes=[
-            pltpu.VMEM((states // LANES, total, size // total + 8, LANES), F32),
-            pltpu.VMEM((states // LANES, total, size // total + 8, LANES), F32),
+            pltpu.VMEM((states // LANES, total + 1, size // total + 8, LANES), F32),
+            pltpu.VMEM((states // LANES, total + 1, size // total + 8, LANES), F32),
             pltpu.VMEM((2, wide, narrow, block, half), BF16),
             pltpu.SemaphoreType.DMA((2, wide)),
         ],

time: 168 us -> 168 us (level)
  no operation moved by 1% of the time
where the time goes in v6:
time: 168 us
  waiting for transfers between devices  67.8 us (40%)
  blocking collectives  51.9 us (31%)
  starting transfers between devices  24.4 us (15%)
  Pallas kernels  16 us (10%)
  local copies, waits for them, and re-layouts  5.22 us (3%)
  other arithmetic  1.73 us (1%)
    ppermute x6, waiting for transfers between devices, send_round(): lax.ppermute(value, axes, [(partner(i, k, size), i) for i in range(size)])  53.5 us
    all_to_all x2, blocking collectives, local(): lax.all_to_all(partial, CUBE, split_axis=0, concat_axis=0, tiled=True)  20.1 us
    all_to_all x2, blocking collectives, local(): lax.all_to_all(copies, CUBE, split_axis=0, concat_axis=0, tiled=True)  18.8 us
    all_to_all x1, blocking collectives, local(): lax.all_to_all(partial, CHIPS, split_axis=0, concat_axis=0, tiled=True)  13 us
    ppermute x6, starting transfers between devices, send_round(): lax.ppermute(value, axes, [(partner(i, k, size), i) for i in range(size)])  8.01 us
    ppermute x10, waiting for transfers between devices, swap_cores(): return lax.ppermute(value, CORE, [(0, 1), (1, 0)])  7.87 us
    all_to_all x1, starting transfers between devices, local(): lax.all_to_all(parts, ALL, split_axis=0, concat_axis=0, tiled=True)  7.3 us
    pallas_call x5, Pallas kernels, call(): pl.pallas_call(kernel, in_specs=specs, out_specs=[IN_VMEM] * len(out), ou...  6.44 us
  transfers between devices with their start and end apart: 20, of which 13 were waited for; matrix products, arithmetic and copies ran while one was open for 1% of the time, Pallas kernels for 4%

profile of v6, /device:TPU:0, one launch (start us, length us, event | category | flops | bytes accessed | tf_op | source)
XLA Modules:
  0.0 167.5 jit_solution(10671013026965848148)
XLA Ops:
  0.0 2.3 %deal_rows.1 = bf16[32,3,16,512]{3,2,1,0:T(8,128)(2,1)} custom-call(bf16[3,32,16,512]{3,2,1,0:T(8,128)(2,1)} %bitcast.67), custom_call_target="tpu_custom_call" | custom-call | tf_op jit(solution)/shard_map/deal_rows/pallas_call | solution.py:116
  2.3 7.3 %all-to-all-start = ((bf16[32,48,512]{2,1,0:T(8,128)(2,1)}), bf16[32,48,512]{2,1,0:T(8,128)(2,1)S(1)}, u32[]{:S(2)}, u32[]{:S(2)}) async-start(bf16[32,48,512]{2,1,0:T(8,128)(2,1)} %bitcast.66), calls=%async_computation | async-start | bytes 3145728 | tf_op jit(solution)/shard_map/all_to_all | solution.py:385
  9.7 0.3 collective-permute-start
  10.0 0.2 reduce-window.8
  10.5 0.7 gather_fusion
  11.2 0.1 copy.15
  11.5 0.7 gather_fusion.1
  12.4 3.6 %collective-permute-start.3 = (bf16[4,16,256]{2,1,0:T(8,128)(2,1)S(1)}, bf16[4,16,256]{2,1,0:T(8,128)(2,1)S(1)}, u32[]{:S(2)}, u32[]{:S(2)}) collective-permute-start(bf16[4,16,256]{2,1,0:T(8,128)(2,1)S(1)} %pad_maximum_fusion.1), channel_id=1, source_target_pairs={{6,0},{4,2},{2,4},{0,6},{7,1},{5,3},{3,5},{1,7},{14,8},{12,10},{10... | collective-permute-start | bytes 98312 | tf_op jit(solution)/shard_map/ppermute | solution.py:58
  16.0 0.9 collective-permute-start.1
  16.8 24.0 %collective-permute-done.3 = bf16[4,16,256]{2,1,0:T(8,128)(2,1)S(1)} collective-permute-done((bf16[4,16,256]{2,1,0:T(8,128)(2,1)S(1)}, bf16[4,16,256]{2,1,0:T(8,128)(2,1)S(1)}, u32[]{:S(2)}, u32[]{:S(2)}) %collective-permute-start.3) | collective-permute-done | bytes 32800 | tf_op jit(solution)/shard_map/ppermute | solution.py:58
  40.8 9.1 %collective-permute-done.2 = bf16[4,16,256]{2,1,0:T(8,128)(2,1)S(1)} collective-permute-done((bf16[4,16,256]{2,1,0:T(8,128)(2,1)S(1)}, bf16[4,16,256]{2,1,0:T(8,128)(2,1)S(1)}, u32[]{:S(2)}, u32[]{:S(2)}) %collective-permute-start.2) | collective-permute-done | bytes 32800 | tf_op jit(solution)/shard_map/ppermute | solution.py:58
  50.0 2.5 %mix.1 = bf16[2,2,8,2,48,256]{5,4,3,2,1,0:T(8,128)(2,1)} custom-call(bf16[96,96]{1,0:T(8,128)(2,1)S(1)} %select_bitcast_fusion.mixing_ref, bf16[1536,512]{1,0:T(8,128)(2,1)S(1)} %bitcast.61), custom_call_target="tpu_custom_call" | custom-call | flops 150994944 | bytes 3145728 | tf_op jit(solution)/shard_map/mix/pallas_call | solution.py:199
  52.4 3.6 %all-to-all-start.1 = ((bf16[32,96,256]{2,1,0:T(8,128)(2,1)}), bf16[32,96,256]{2,1,0:T(8,128)(2,1)S(1)}, u32[]{:S(2)}, u32[]{:S(2)}) async-start(bf16[32,96,256]{2,1,0:T(8,128)(2,1)} %bitcast.21), calls=%async_computation.1 | async-start | bytes 3145728 | tf_op jit(solution)/shard_map/all_to_all | solution.py:422
  56.1 2.7 %collective-permute-start.9 = (bf16[4,4,16,256]{3,2,1,0:T(8,128)(2,1)S(1)}, bf16[4,4,16,256]{3,2,1,0:T(8,128)(2,1)S(1)}, u32[]{:S(2)}, u32[]{:S(2)}) collective-permute-start(bf16[4,4,16,256]{3,2,1,0:T(8,128)(2,1)S(1)} %pad_maximum_fusion.refs_0_), channel_id=1, source_target_pairs={{17,0},{16,1},{1,16},{0,17},{19,2},{18,3},{3,18},{2,19},{21,4},{20... | collective-permute-start | bytes 393224 | tf_op jit(solution)/shard_map/ppermute | solution.py:58
  58.8 0.6 collective-permute-start.7
  59.4 0.3 collective-permute-start.5
  59.6 19.2 %collective-permute-done.9.refs_6_ = bf16[4,4,16,256]{3,2,1,0:T(8,128)(2,1)S(1)} collective-permute-done((bf16[4,4,16,256]{3,2,1,0:T(8,128)(2,1)S(1)}, bf16[4,4,16,256]{3,2,1,0:T(8,128)(2,1)S(1)}, u32[]{:S(2)}, u32[]{:S(2)}) %collective-permute-start.9) | collective-permute-done | bytes 131104 | tf_op jit(solution)/shard_map/ppermute | solution.py:58
  78.9 1.0 collective-permute-done.7.refs_4_
  79.9 0.2 collective-permute-done.5.refs_2_
  80.1 0.4 collective-permute-start.6
  80.6 0.6 collective-permute-done.8.refs_5_
  81.2 0.2 collective-permute-done.6.refs_3_
  81.4 0.7 place_slots.1
  82.1 0.8 copy-done.5
  82.9 4.8 %build.1.own_ref = bf16[3,512,512]{2,1,0:T(8,128)(2,1)} custom-call(bf16[512,512]{1,0:T(8,128)(2,1)} %bitcast.63, bf16[3,512,512]{2,1,0:T(8,128)(2,1)} %left_ref.1), custom_call_target="tpu_custom_call" | custom-call | tf_op jit(solution)/shard_map/build/pallas_call | solution.py:140
  87.7 0.3 collective-permute-start.11
  88.1 3.3 %collective-permute-done.11.other_ref = bf16[3,512,512]{2,1,0:T(8,128)(2,1)S(1)} collective-permute-done((bf16[3,512,512]{2,1,0:T(8,128)(2,1)}, bf16[3,512,512]{2,1,0:T(8,128)(2,1)S(1)}, u32[]{:S(2)}, u32[]{:S(2)}) %collective-permute-start.11) | collective-permute-done | bytes 1572896 | tf_op jit(solution)/shard_map/ppermute | solution.py:38
  91.3 1.4 copy-done.1
  92.7 1.0 apply_pairs.1.applied_ref
  93.7 1.2 copy-done.3
  94.9 1.0 join_terms.1
  95.9 0.4 collective-permute-start.12
  96.3 1.2 collective-permute-done.12
  97.6 10.2 %all_to_all.35 = bf16[8,64,256]{2,1,0:T(8,128)(2,1)S(1)} all-to-all(bf16[8,64,256]{2,1,0:T(8,128)(2,1)S(1)} %bitcast.69), channel_id=1, replica_groups=mesh['outer'=2,'core'=2,'high'=2,'low'=2,'near'=2] {'outer','low','near'}, dimensions={0} | all-to-all | bytes 524288 | tf_op jit(solution)/shard_map/all_to_all | solution.py:433
  107.9 1.7 collective-permute-start.13
  109.5 3.2 %collective-permute-done.13 = bf16[2,2,16,256]{3,2,1,0:T(8,128)(2,1)S(1)} collective-permute-done((bf16[2,2,16,256]{3,2,1,0:T(8,128)(2,1)S(1)}, bf16[2,2,16,256]{3,2,1,0:T(8,128)(2,1)S(1)}, u32[]{:S(2)}, u32[]{:S(2)}) %collective-permute-start.13) | collective-permute-done | bytes 32800 | tf_op jit(solution)/shard_map/ppermute | solution.py:45
  112.8 9.4 %all_to_all.36 = bf16[8,64,256]{2,1,0:T(8,128)(2,1)S(1)} all-to-all(bf16[8,64,256]{2,1,0:T(8,128)(2,1)S(1)} %broadcast_in_dim.34), channel_id=1, replica_groups=mesh['outer'=2,'core'=2,'high'=2,'low'=2,'near'=2] {'outer','low','near'}, dimensions={0} | all-to-all | bytes 524288 | tf_op jit(solution)/shard_map/all_to_all | solution.py:443
  122.2 1.8 %apply_terms.1 = (f32[2,4,2,2,16,256]{5,4,3,2,1,0:T(8,128)S(1)}, bf16[2,4,2,2,16,256]{5,4,3,2,1,0:T(8,128)(2,1)S(1)}) custom-call(bf16[2,4,2,2,16,256]{5,4,3,2,1,0:T(8,128)(2,1)S(1)} %bitcast.65, bf16[3,512,512]{2,1,0:T(8,128)(2,1)S(1)} %copy-done.2, bf16[3,512,512]{2,1,0:T(8,128)(2,1)S(1)} %copy-done.4, ...), custom_call_target="tpu_custom_call" | custom-call | flops 1610612736 | bytes 4980736 | tf_op jit(solution)/shard_map/apply_terms/pallas_call | solution.py:280
  124.1 1.5 collective-permute-done.14
  125.7 10.0 %all_to_all.37 = bf16[8,64,256]{2,1,0:T(8,128)(2,1)S(1)} all-to-all(bf16[8,64,256]{2,1,0:T(8,128)(2,1)S(1)} %bitcast.70), channel_id=1, replica_groups=mesh['outer'=2,'core'=2,'high'=2,'low'=2,'near'=2] {'outer','low','near'}, dimensions={0} | all-to-all | bytes 524288 | tf_op jit(solution)/shard_map/all_to_all | solution.py:433
  135.7 1.7 collective-permute-start.15
  137.4 3.2 %collective-permute-done.15 = bf16[2,2,16,256]{3,2,1,0:T(8,128)(2,1)S(1)} collective-permute-done((bf16[2,2,16,256]{3,2,1,0:T(8,128)(2,1)S(1)}, bf16[2,2,16,256]{3,2,1,0:T(8,128)(2,1)S(1)}, u32[]{:S(2)}, u32[]{:S(2)}) %collective-permute-start.15) | collective-permute-done | bytes 32800 | tf_op jit(solution)/shard_map/ppermute | solution.py:45
  140.7 9.4 %all_to_all.38 = bf16[8,64,256]{2,1,0:T(8,128)(2,1)S(1)} all-to-all(bf16[8,64,256]{2,1,0:T(8,128)(2,1)S(1)} %broadcast_in_dim.35), channel_id=1, replica_groups=mesh['outer'=2,'core'=2,'high'=2,'low'=2,'near'=2] {'outer','low','near'}, dimensions={0} | all-to-all | bytes 524288 | tf_op jit(solution)/shard_map/all_to_all | solution.py:443
  150.1 2.0 %last_terms.1 = (f32[2,8,2,16,256]{4,3,2,1,0:T(8,128)S(1)}, bf16[2,8,2,16,256]{4,3,2,1,0:T(8,128)(2,1)S(1)}) custom-call(s32[1]{0:T(128)} %bitcast.core_ref, bf16[2,4,2,2,16,256]{5,4,3,2,1,0:T(8,128)(2,1)S(1)} %bitcast.64, bf16[3,512,512]{2,1,0:T(8,128)(2,1)S(1)} %copy-done.2, bf16[3,512,512]{2,1,0:T(8,128)(2,1)S(1)} %copy-done.4, ...), custom_call_target="tpu_custom_call" | custom-call | flops 1610612736 | bytes 4980738 | tf_op jit(solution)/shard_map/last_terms/pallas_call | solution.py:280
  152.1 0.5 collective-permute-start.16
  152.6 1.0 collective-permute-done.16
  153.8 13.0 %all_to_all.39 = bf16[16,32,256]{2,1,0:T(8,128)(2,1)S(1)} all-to-all(bf16[16,32,256]{2,1,0:T(8,128)(2,1)S(1)} %bitcast.68), channel_id=1, replica_groups=mesh['outer'=2,'core'=2,'high'=2,'low'=2,'near'=2] {'outer','high','low'..., dimensions={0} | all-to-all | bytes 524288 | tf_op jit(solution)/shard_map/all_to_all | solution.py:452
  166.9 0.6 pad_maximum_fusion.3
  (76 shorter events, 1.5 us)
Async XLA Ops:
  0.0 10.5 %copy-start = (bf16[96,96]{1,0:T(8,128)(2,1)S(1)}, bf16[96,96]{1,0:T(8,128)(2,1)}, u32[]{:S(2)}) copy-start(bf16[96,96]{1,0:T(8,128)(2,1)} %param.10) | copy-start | bytes 55300
  2.3 7.4 %copy-start.6 = (bf16[16,512]{1,0:T(8,128)(2,1)S(1)}, bf16[16,512]{1,0:T(8,128)(2,1)}, u32[]{:S(2)}) copy-start(bf16[16,512]{1,0:T(8,128)(2,1)} %param.11) | copy-start | bytes 49156
  2.3 7.7 %copy-start.8 = (s32[8]{0:T(128)S(1)}, s32[8]{0:T(128)}, u32[]{:S(2)}) copy-start(s32[8]{0:T(128)} %param.13) | copy-start | bytes 100
  2.3 8.2 %copy-start.9 = (s32[96]{0:T(128)S(1)}, s32[96]{0:T(128)}, u32[]{:S(2)}) copy-start(s32[96]{0:T(128)} %param.12) | copy-start | bytes 1156
  2.3 9.2 %copy-start.7 = (bf16[16,512]{1,0:T(8,128)(2,1)S(1)}, bf16[16,512]{1,0:T(8,128)(2,1)}, u32[]{:S(2)}) copy-start(bf16[16,512]{1,0:T(8,128)(2,1)} %param.7) | copy-start | bytes 49156
  2.3 47.6 %all-to-all-start = ((bf16[32,48,512]{2,1,0:T(8,128)(2,1)}), bf16[32,48,512]{2,1,0:T(8,128)(2,1)S(1)}, u32[]{:S(2)}, u32[]{:S(2)}) async-start(bf16[32,48,512]{2,1,0:T(8,128)(2,1)} %bitcast.66), calls=%async_computation | async-start | bytes 3145728 | tf_op jit(solution)/shard_map/all_to_all | solution.py:385
  9.7 2.6 %collective-permute-start = (bf16[16,256]{1,0:T(8,128)(2,1)S(1)}, bf16[16,256]{1,0:T(8,128)(2,1)S(1)}, u32[]{:S(2)}, u32[]{:S(2)}) collective-permute-start(bf16[16,256]{1,0:T(8,128)(2,1)S(1)} %broadcast_select_fusion.2), channel_id=1, source_target_pairs={{0,8},{8,0},{1,9},{9,1},{2,10},{10,2},{3,11},{11,3},{4,12},{12,4},... | collective-permute-start | bytes 24584 | tf_op jit(solution)/shard_map/ppermute | solution.py:38
  12.4 28.5 %collective-permute-start.3 = (bf16[4,16,256]{2,1,0:T(8,128)(2,1)S(1)}, bf16[4,16,256]{2,1,0:T(8,128)(2,1)S(1)}, u32[]{:S(2)}, u32[]{:S(2)}) collective-permute-start(bf16[4,16,256]{2,1,0:T(8,128)(2,1)S(1)} %pad_maximum_fusion.1), channel_id=1, source_target_pairs={{6,0},{4,2},{2,4},{0,6},{7,1},{5,3},{3,5},{1,7},{14,8},{12,10},{10... | collective-permute-start | bytes 98312 | tf_op jit(solution)/shard_map/ppermute | solution.py:58
  16.0 34.0 %collective-permute-start.2 = (bf16[4,16,256]{2,1,0:T(8,128)(2,1)S(1)}, bf16[4,16,256]{2,1,0:T(8,128)(2,1)S(1)}, u32[]{:S(2)}, u32[]{:S(2)}) collective-permute-start(bf16[4,16,256]{2,1,0:T(8,128)(2,1)S(1)} %pad_maximum_fusion.1), channel_id=1, source_target_pairs={{4,0},{6,2},{0,4},{2,6},{5,1},{7,3},{1,5},{3,7},{12,8},{14,10},{8,... | collective-permute-start | bytes 98312 | tf_op jit(solution)/shard_map/ppermute | solution.py:58
  16.0 34.0 %collective-permute-start.1 = (bf16[4,16,256]{2,1,0:T(8,128)(2,1)S(1)}, bf16[4,16,256]{2,1,0:T(8,128)(2,1)S(1)}, u32[]{:S(2)}, u32[]{:S(2)}) collective-permute-start(bf16[4,16,256]{2,1,0:T(8,128)(2,1)S(1)} %pad_maximum_fusion.1), channel_id=1, source_target_pairs={{2,0},{0,2},{6,4},{4,6},{3,1},{1,3},{7,5},{5,7},{10,8},{8,10},{14,... | collective-permute-start | bytes 98312 | tf_op jit(solution)/shard_map/ppermute | solution.py:58
  52.4 42.5 %all-to-all-start.1 = ((bf16[32,96,256]{2,1,0:T(8,128)(2,1)}), bf16[32,96,256]{2,1,0:T(8,128)(2,1)S(1)}, u32[]{:S(2)}, u32[]{:S(2)}) async-start(bf16[32,96,256]{2,1,0:T(8,128)(2,1)} %bitcast.21), calls=%async_computation.1 | async-start | bytes 3145728 | tf_op jit(solution)/shard_map/all_to_all | solution.py:422
  56.1 22.8 %collective-permute-start.9 = (bf16[4,4,16,256]{3,2,1,0:T(8,128)(2,1)S(1)}, bf16[4,4,16,256]{3,2,1,0:T(8,128)(2,1)S(1)}, u32[]{:S(2)}, u32[]{:S(2)}) collective-permute-start(bf16[4,4,16,256]{3,2,1,0:T(8,128)(2,1)S(1)} %pad_maximum_fusion.refs_0_), channel_id=1, source_target_pairs={{17,0},{16,1},{1,16},{0,17},{19,2},{18,3},{3,18},{2,19},{21,4},{20... | collective-permute-start | bytes 393224 | tf_op jit(solution)/shard_map/ppermute | solution.py:58
  58.8 21.1 %collective-permute-start.7 = (bf16[4,4,16,256]{3,2,1,0:T(8,128)(2,1)S(1)}, bf16[4,4,16,256]{3,2,1,0:T(8,128)(2,1)S(1)}, u32[]{:S(2)}, u32[]{:S(2)}) collective-permute-start(bf16[4,4,16,256]{3,2,1,0:T(8,128)(2,1)S(1)} %pad_maximum_fusion.refs_0_), channel_id=1, source_target_pairs={{16,0},{17,1},{0,16},{1,17},{18,2},{19,3},{2,18},{3,19},{20,4},{21... | collective-permute-start | bytes 393224 | tf_op jit(solution)/shard_map/ppermute | solution.py:58
  59.4 20.7 %collective-permute-start.5 = (bf16[4,4,16,256]{3,2,1,0:T(8,128)(2,1)S(1)}, bf16[4,4,16,256]{3,2,1,0:T(8,128)(2,1)S(1)}, u32[]{:S(2)}, u32[]{:S(2)}) collective-permute-start(bf16[4,4,16,256]{3,2,1,0:T(8,128)(2,1)S(1)} %pad_maximum_fusion.refs_0_), channel_id=1, source_target_pairs={{1,0},{0,1},{17,16},{16,17},{3,2},{2,3},{19,18},{18,19},{5,4},{4,5... | collective-permute-start | bytes 393224 | tf_op jit(solution)/shard_map/ppermute | solution.py:58
  59.6 20.9 %collective-permute-start.4 = (bf16[4,2,16,256]{3,2,1,0:T(8,128)(2,1)S(1)}, bf16[4,2,16,256]{3,2,1,0:T(8,128)(2,1)S(1)}, u32[]{:S(2)}, u32[]{:S(2)}) collective-permute-start(bf16[4,2,16,256]{3,2,1,0:T(8,128)(2,1)S(1)} %slice.56), channel_id=1, source_target_pairs={{0,8},{8,0},{1,9},{9,1},{2,10},{10,2},{3,11},{11,3},{4,12},{12,4},... | collective-permute-start | bytes 196616 | tf_op jit(solution)/shard_map/ppermute | solution.py:38
  78.8 1.7 %collective-permute-start.10 = (bf16[4,2,16,256]{3,2,1,0:T(8,128)(2,1)S(1)}, bf16[4,2,16,256]{3,2,1,0:T(8,128)(2,1)S(1)}, u32[]{:S(2)}, u32[]{:S(2)}) collective-permute-start(bf16[4,2,16,256]{3,2,1,0:T(8,128)(2,1)S(1)} %slice.70), channel_id=1, source_target_pairs={{0,8},{8,0},{1,9},{9,1},{2,10},{10,2},{3,11},{11,3},{4,12},{12,4},... | collective-permute-start | bytes 196616 | tf_op jit(solution)/shard_map/ppermute | solution.py:38
  79.9 1.3 collective-permute-start.8
  80.1 1.3 collective-permute-start.6
  82.1 0.8 copy-start.5
  87.7 3.6 %collective-permute-start.11 = (bf16[3,512,512]{2,1,0:T(8,128)(2,1)}, bf16[3,512,512]{2,1,0:T(8,128)(2,1)S(1)}, u32[]{:S(2)}, u32[]{:S(2)}) collective-permute-start(bf16[3,512,512]{2,1,0:T(8,128)(2,1)} %build.1.own_ref), channel_id=1, source_target_pairs={{0,8},{8,0},{1,9},{9,1},{2,10},{10,2},{3,11},{11,3},{4,12},{12,4},... | collective-permute-start | bytes 4718600 | tf_op jit(solution)/shard_map/ppermute | solution.py:38
  91.3 1.4 copy-start.1
  93.7 1.2 copy-start.3
  94.9 27.3 %copy-start.4 = (bf16[3,512,512]{2,1,0:T(8,128)(2,1)S(1)}, bf16[3,512,512]{2,1,0:T(8,128)(2,1)}, u32[]{:S(2)}) copy-start(bf16[3,512,512]{2,1,0:T(8,128)(2,1)} %copy-done.3) | copy-start | bytes 4718596
  95.9 26.3 %copy-start.2 = (bf16[3,512,512]{2,1,0:T(8,128)(2,1)S(1)}, bf16[3,512,512]{2,1,0:T(8,128)(2,1)}, u32[]{:S(2)}) copy-start(bf16[3,512,512]{2,1,0:T(8,128)(2,1)} %build.1.own_ref) | copy-start | bytes 4718596
  95.9 1.6 collective-permute-start.12
  107.9 4.9 %collective-permute-start.13 = (bf16[2,2,16,256]{3,2,1,0:T(8,128)(2,1)S(1)}, bf16[2,2,16,256]{3,2,1,0:T(8,128)(2,1)S(1)}, u32[]{:S(2)}, u32[]{:S(2)}) collective-permute-start(bf16[2,2,16,256]{3,2,1,0:T(8,128)(2,1)S(1)} %multiply_convert_fusion.3), channel_id=1, source_target_pairs={{0,4},{4,0},{1,5},{5,1},{2,6},{6,2},{3,7},{7,3},{8,12},{12,8},{9,1... | collective-permute-start | bytes 98312 | tf_op jit(solution)/shard_map/ppermute | solution.py:45
  124.0 1.6 collective-permute-start.14
  135.7 4.9 %collective-permute-start.15 = (bf16[2,2,16,256]{3,2,1,0:T(8,128)(2,1)S(1)}, bf16[2,2,16,256]{3,2,1,0:T(8,128)(2,1)S(1)}, u32[]{:S(2)}, u32[]{:S(2)}) collective-permute-start(bf16[2,2,16,256]{3,2,1,0:T(8,128)(2,1)S(1)} %multiply_convert_fusion.1), channel_id=1, source_target_pairs={{0,4},{4,0},{1,5},{5,1},{2,6},{6,2},{3,7},{7,3},{8,12},{12,8},{9,1... | collective-permute-start | bytes 98312 | tf_op jit(solution)/shard_map/ppermute | solution.py:45
  152.0 1.6 collective-permute-start.17
  152.1 1.5 collective-permute-start.16

commit v7 on v6

--- a/solution.py
+++ b/solution.py
@@ -128,28 +128,35 @@
     )(split)
 
 
-def build_kernel(basis_ref, left_ref, built_ref):
+def build_kernel(basis_ref, own_ref, other_ref, built_ref):
     basis = basis_ref[...]
-    rotated = jnp.dot(left_ref[0], basis, preferred_element_type=F32).astype(BF16)
-    built = lax.dot_general(basis, rotated, (((0,), (0,)), ((), ())), preferred_element_type=F32)
-    built_ref[0] = built.astype(BF16)
-
-
-def build(basis, left_ops):
-    pairs, states, _ = left_ops.shape
+    pairs = pl.num_programs(0) // 2
+
+    def build_from(left_ref):
+        rotated = jnp.dot(left_ref[0], basis, preferred_element_type=F32).astype(BF16)
+        built = lax.dot_general(basis, rotated, (((0,), (0,)), ((), ())), preferred_element_type=F32)
+        built_ref[0] = built.astype(BF16)
+
+    pl.when(pl.program_id(0) < pairs)(lambda: build_from(own_ref))
+    pl.when(pl.program_id(0) >= pairs)(lambda: build_from(other_ref))
+
+
+def build(basis, own_left, other_left):
+    pairs, states, _ = own_left.shape
     return pl.pallas_call(
         build_kernel,
-        grid=(pairs,),
+        grid=(2 * pairs,),
         in_specs=[
             whole_block((states, states)),
-            pl.BlockSpec((1, states, states), lambda s: (s, 0, 0)),
+            pl.BlockSpec((1, states, states), lambda s: (jnp.minimum(s, pairs - 1), 0, 0)),
+            pl.BlockSpec((1, states, states), lambda s: (jnp.maximum(s - pairs, 0), 0, 0)),
         ],
         out_specs=pl.BlockSpec((1, states, states), lambda s: (s, 0, 0)),
-        out_shape=jax.ShapeDtypeStruct(left_ops.shape, BF16),
-        compiler_params=kernel_params(60),
+        out_shape=jax.ShapeDtypeStruct((2 * pairs, states, states), BF16),
+        compiler_params=kernel_params(57),
         cost_estimate=pl.CostEstimate(flops=0, bytes_accessed=0, transcendentals=0),
         name="build",
-    )(basis, left_ops)
+    )(basis, own_left, other_left)
 
 
 def mix_kernel(mixing_ref, right_ref, out_ref, taken, given, mixed, sems):
@@ -213,18 +220,15 @@
     )(mixing, right_rows)
 
 
-def apply_kernel(state_ref, own_ref, other_ref, applied_ref):
+def apply_kernel(state_ref, built_ref, applied_ref):
     outer, cube, high, _, rows, half = state_ref.shape
-    pairs = own_ref.shape[0]
     places = itertools.product(range(outer), range(2), range(high))
     state = jnp.concatenate(
         [state_ref[o, :, h, c].reshape(cube * rows, half) for o, c, h in places]
     )
-    for side, ref in enumerate((own_ref, other_ref)):
-        for q in range(pairs):
-            one = jnp.dot(ref[q], state, preferred_element_type=F32).astype(BF16)
-            column = (side * pairs + q) * half
-            applied_ref[:, column : column + half] = one
+    for s in range(built_ref.shape[0]):
+        one = jnp.dot(built_ref[s], state, preferred_element_type=F32).astype(BF16)
+        applied_ref[:, s * half : (s + 1) * half] = one
 
 
 def store_term(applied, joined, term_ref):
@@ -248,16 +252,16 @@
         store_term(applied_ref[...], joined_ref[k], term_ref)
 
 
-def apply_term_kernel(state_ref, own_ref, other_ref, joined_ref, keep_ref, send_ref, applied_ref):
-    apply_kernel(state_ref, own_ref, other_ref, applied_ref)
+def apply_term_kernel(state_ref, built_ref, joined_ref, keep_ref, send_ref, applied_ref):
+    apply_kernel(state_ref, built_ref, applied_ref)
     for k, term_ref in enumerate((send_ref, keep_ref)):
         store_term(applied_ref[...], joined_ref[k], term_ref)
 
 
 def last_term_kernel(
-    core_ref, state_ref, own_ref, other_ref, joined_ref, keep_ref, send_ref, applied_ref
+    core_ref, state_ref, built_ref, joined_ref, keep_ref, send_ref, applied_ref
 ):
-    apply_kernel(state_ref, own_ref, other_ref, applied_ref)
+    apply_kernel(state_ref, built_ref, applied_ref)
     outer, narrow, _, rows, half = keep_ref.shape
     count = narrow * rows
     core = core_ref[0]
@@ -293,16 +297,15 @@
     return call
 
 
-def apply_pairs(state, own, other):
-    pairs, states, _ = own.shape
+def apply_pairs(state, built):
+    both, states, _ = built.shape
     half = state.shape[-1]
     if state.shape[-2] % 16:
         full = state.transpose(0, 3, 2, 1, 4, 5).reshape(states, half)
-        built = jnp.concatenate([own, other])
         applied = jnp.einsum("sil,lk->isk", built, full, preferred_element_type=F32).astype(BF16)
-        return applied.reshape(states, 2 * pairs * half)
-    shape = (states, 2 * pairs * half)
-    return local_call(apply_kernel, "apply_pairs", 8, (shape, BF16))(state, own, other)[0]
+        return applied.reshape(states, both * half)
+    shape = (states, both * half)
+    return local_call(apply_kernel, "apply_pairs", 8, (shape, BF16))(state, built)[0]
 
 
 def join_terms(core, applied, comp, shape):
@@ -331,31 +334,31 @@
     return term[1], term[0].astype(BF16)
 
 
-def apply_and_terms(state, own, other, joined):
-    pairs, states, _ = own.shape
+def apply_and_terms(state, built, joined):
+    both, states, _ = built.shape
     half = state.shape[-1]
     if state.shape[-2] % 16:
-        return terms_of(apply_pairs(state, own, other), joined, state.shape)
-    scratch = [pltpu.VMEM((states, 2 * pairs * half), BF16)]
+        return terms_of(apply_pairs(state, built), joined, state.shape)
+    scratch = [pltpu.VMEM((states, both * half), BF16)]
     out = (state.shape, F32), (state.shape, BF16)
-    flops = 8 * pairs * states**2 * half
+    flops = 4 * both * states**2 * half
     call = local_call(apply_term_kernel, "apply_terms", 12, *out, scratch=scratch, flops=flops)
-    return call(state, own, other, joined)
-
-
-def apply_and_last_terms(core, state, own, other, joined):
+    return call(state, built, joined)
+
+
+def apply_and_last_terms(core, state, built, joined):
     outer, cube, high, _, rows, half = state.shape
-    pairs, states, _ = own.shape
+    both, states, _ = built.shape
     shape = (outer, high * cube, 2, rows, half)
     if rows % 16:
-        term = all_terms(apply_pairs(state, own, other), joined, state.shape)
+        term = all_terms(apply_pairs(state, built), joined, state.shape)
         term = term.reshape(2, outer, 2, high * cube, rows, half)
         term = jnp.where(core == 1, term, term[::-1]).transpose(2, 1, 3, 0, 4, 5)
         return term[core], term[1 - core].astype(BF16)
-    scratch = [pltpu.VMEM((states, 2 * pairs * half), BF16)]
-    flops = 8 * pairs * states**2 * half
+    scratch = [pltpu.VMEM((states, both * half), BF16)]
+    flops = 4 * both * states**2 * half
     call = local_call(last_term_kernel, "last_terms", 12, (shape, F32), (shape, BF16), scratch=scratch, flops=flops)
-    return call(core.reshape(1), state, own, other, joined)
+    return call(core.reshape(1), state, built, joined)
 
 
 def local(site_basis, left_ops, right_ops, integrals, wavefunction, pair_order, sector_sizes):
@@ -408,15 +411,15 @@
         (packet, cube_mask, row_mask, summed)
     )
     mixed = mix(mixing, right_rows, wide, narrow, pairs * rows)
-    packets, mixed = lax.optimization_barrier((jnp.stack(send_round(packet, (HIGH, LOW), high * low)), mixed))
+    packets = jnp.stack(send_round(packet, (HIGH, LOW), high * low))
+    packets, mixed, other_left = lax.optimization_barrier((packets, mixed, swap_cores(left_ops)))
     slots = []
     for slot in send_round(packets, (OUTER, NEAR), outer * near):
         slots += [slot, swap_cores(slot[:, :2])]
     place = [lax.axis_index((OUTER, NEAR)), lax.axis_index((HIGH, LOW)), own_core]
     basis, state = place_slots(jnp.stack(place), slots, outer, high, near)
-    own_built = build(basis.reshape(states, states), left_ops)
-    other_built = swap_cores(own_built)
-    applied = apply_pairs(state, own_built, other_built)
+    built = build(basis.reshape(states, states), left_ops, other_left)
+    applied = apply_pairs(state, built)
 
     mixed = mixed.reshape(devices, 2 * pairs * rows, half)
     comp = lax.all_to_all(mixed, ALL, split_axis=0, concat_axis=0, tiled=True)
@@ -427,7 +430,7 @@
         if order_index == 1:
             keep, send, joined = join_terms(own_core, applied, comp, state.shape)
         else:
-            keep, send = apply_and_terms(state, own_built, other_built, joined)
+            keep, send = apply_and_terms(state, built, joined)
         partial = (keep + swap_cores(send).astype(F32)).astype(BF16)
         partial = partial.reshape(chips // high, high * 2 * rows, half)
         arrived = lax.all_to_all(partial, CUBE, split_axis=0, concat_axis=0, tiled=True)
@@ -443,7 +446,7 @@
         state = lax.all_to_all(copies, CUBE, split_axis=0, concat_axis=0, tiled=True)
         state = state.reshape(outer, low * near, high, 2, rows, half)
 
-    keep, send = apply_and_last_terms(own_core, state, own_built, other_built, joined)
+    keep, send = apply_and_last_terms(own_core, state, built, joined)
     theirs, send = lax.optimization_barrier((theirs, send))
     theirs, send = lax.optimization_barrier((swap_cores(theirs), swap_cores(send)))
     summed = by_core(mine, theirs)

time: 168 us -> 168 us (level)
  Pallas kernels: 16 us -> 19.2 us
    pallas_call x1, Pallas kernels: 4.83 us -> 8.05 us  [build(): pl.pallas_call(build_kernel, grid=(2 * pairs,), in_specs=[whole_block((st...]
    ppermute x10, waiting for transfers between devices: 7.87 us -> 4.92 us  [swap_cores(): return lax.ppermute(value, CORE, [(0, 1), (1, 0)])]
    unnamed x20 -> x16, local copies, waits for them, and re-layouts: 3.4 us -> 2.72 us
  transfers between devices with their start and end apart: 20 -> 20, of which waited for: 13 -> 13; matrix products, arithmetic and copies ran while one was open for 1% -> 1% of each run, Pallas kernels for 4% -> 7%
where the time goes in v7:
time: 168 us; the launch traced here: 167 us
  waiting for transfers between devices  66.6 us (40%)
  blocking collectives  51.7 us (31%)
  starting transfers between devices  23 us (14%)
  Pallas kernels  19.2 us (11%)
  local copies, waits for them, and re-layouts  4.54 us (3%)
  other arithmetic  1.74 us (1%)
    ppermute x6, waiting for transfers between devices, send_round(): lax.ppermute(value, axes, [(partner(i, k, size), i) for i in range(size)])  53.2 us
    all_to_all x2, blocking collectives, local(): lax.all_to_all(partial, CUBE, split_axis=0, concat_axis=0, tiled=True)  19.9 us
    all_to_all x2, blocking collectives, local(): lax.all_to_all(copies, CUBE, split_axis=0, concat_axis=0, tiled=True)  18.8 us
    all_to_all x1, blocking collectives, local(): lax.all_to_all(partial, CHIPS, split_axis=0, concat_axis=0, tiled=True)  13 us
    pallas_call x1, Pallas kernels, build(): pl.pallas_call(build_kernel, grid=(2 * pairs,), in_specs=[whole_block((st...  8.05 us
    ppermute x6, starting transfers between devices, send_round(): lax.ppermute(value, axes, [(partner(i, k, size), i) for i in range(size)])  8.01 us
    ppermute x2, waiting for transfers between devices, add_high(): other = lax.ppermute(rounded, HIGH, [(0, 1), (1, 0)])  7.35 us
    all_to_all x1, starting transfers between devices, local(): lax.all_to_all(parts, ALL, split_axis=0, concat_axis=0, tiled=True)  7.3 us
  transfers between devices with their start and end apart: 20, of which 13 were waited for; matrix products, arithmetic and copies ran while one was open for 1% of the time, Pallas kernels for 7%

profile of v7, /device:TPU:0, one launch (start us, length us, event | category | flops | bytes accessed | tf_op | source)
XLA Modules:
  0.0 167.3 jit_solution(3251411839726618140)
XLA Ops:
  0.0 2.3 %deal_rows.1 = bf16[32,3,16,512]{3,2,1,0:T(8,128)(2,1)} custom-call(bf16[3,32,16,512]{3,2,1,0:T(8,128)(2,1)} %bitcast.67), custom_call_target="tpu_custom_call" | custom-call | tf_op jit(solution)/shard_map/deal_rows/pallas_call | solution.py:116
  2.3 7.3 %all-to-all-start = ((bf16[32,48,512]{2,1,0:T(8,128)(2,1)}), bf16[32,48,512]{2,1,0:T(8,128)(2,1)S(1)}, u32[]{:S(2)}, u32[]{:S(2)}) async-start(bf16[32,48,512]{2,1,0:T(8,128)(2,1)} %bitcast.66), calls=%async_computation | async-start | bytes 3145728 | tf_op jit(solution)/shard_map/all_to_all | solution.py:388
  9.7 0.3 collective-permute-start
  10.0 0.3 collective-permute-start.4
  10.2 0.2 reduce-window.8
  10.9 0.7 gather_fusion
  11.6 0.1 copy.15
  11.8 0.7 gather_fusion.1
  12.5 0.1 copy.16
  12.6 3.7 %collective-permute-start.3 = (bf16[4,16,256]{2,1,0:T(8,128)(2,1)S(1)}, bf16[4,16,256]{2,1,0:T(8,128)(2,1)S(1)}, u32[]{:S(2)}, u32[]{:S(2)}) collective-permute-start(bf16[4,16,256]{2,1,0:T(8,128)(2,1)S(1)} %pad_maximum_fusion.1), channel_id=1, source_target_pairs={{6,0},{4,2},{2,4},{0,6},{7,1},{5,3},{3,5},{1,7},{14,8},{12,10},{10... | collective-permute-start | bytes 98312 | tf_op jit(solution)/shard_map/ppermute | solution.py:58
  16.3 0.8 collective-permute-start.1
  17.1 23.8 %collective-permute-done.3 = bf16[4,16,256]{2,1,0:T(8,128)(2,1)S(1)} collective-permute-done((bf16[4,16,256]{2,1,0:T(8,128)(2,1)S(1)}, bf16[4,16,256]{2,1,0:T(8,128)(2,1)S(1)}, u32[]{:S(2)}, u32[]{:S(2)}) %collective-permute-start.3) | collective-permute-done | bytes 32800 | tf_op jit(solution)/shard_map/ppermute | solution.py:58
  40.8 9.1 %collective-permute-done.2 = bf16[4,16,256]{2,1,0:T(8,128)(2,1)S(1)} collective-permute-done((bf16[4,16,256]{2,1,0:T(8,128)(2,1)S(1)}, bf16[4,16,256]{2,1,0:T(8,128)(2,1)S(1)}, u32[]{:S(2)}, u32[]{:S(2)}) %collective-permute-start.2) | collective-permute-done | bytes 32800 | tf_op jit(solution)/shard_map/ppermute | solution.py:58
  50.0 2.5 %mix.1 = bf16[2,2,8,2,48,256]{5,4,3,2,1,0:T(8,128)(2,1)} custom-call(bf16[96,96]{1,0:T(8,128)(2,1)S(1)} %select_bitcast_fusion.mixing_ref, bf16[1536,512]{1,0:T(8,128)(2,1)S(1)} %bitcast.61), custom_call_target="tpu_custom_call" | custom-call | flops 150994944 | bytes 3145728 | tf_op jit(solution)/shard_map/mix/pallas_call | solution.py:206
  52.4 3.6 %all-to-all-start.1 = ((bf16[32,96,256]{2,1,0:T(8,128)(2,1)}), bf16[32,96,256]{2,1,0:T(8,128)(2,1)S(1)}, u32[]{:S(2)}, u32[]{:S(2)}) async-start(bf16[32,96,256]{2,1,0:T(8,128)(2,1)} %bitcast.21), calls=%async_computation.1 | async-start | bytes 3145728 | tf_op jit(solution)/shard_map/all_to_all | solution.py:425
  56.1 2.7 %collective-permute-start.10 = (bf16[4,4,16,256]{3,2,1,0:T(8,128)(2,1)S(1)}, bf16[4,4,16,256]{3,2,1,0:T(8,128)(2,1)S(1)}, u32[]{:S(2)}, u32[]{:S(2)}) collective-permute-start(bf16[4,4,16,256]{3,2,1,0:T(8,128)(2,1)S(1)} %pad_maximum_fusion.refs_0_), channel_id=1, source_target_pairs={{17,0},{16,1},{1,16},{0,17},{19,2},{18,3},{3,18},{2,19},{21,4},{20... | collective-permute-start | bytes 393224 | tf_op jit(solution)/shard_map/ppermute | solution.py:58
  58.8 0.6 collective-permute-start.8
  59.4 0.3 collective-permute-start.6
  59.6 19.2 %collective-permute-done.10.refs_6_ = bf16[4,4,16,256]{3,2,1,0:T(8,128)(2,1)S(1)} collective-permute-done((bf16[4,4,16,256]{3,2,1,0:T(8,128)(2,1)S(1)}, bf16[4,4,16,256]{3,2,1,0:T(8,128)(2,1)S(1)}, u32[]{:S(2)}, u32[]{:S(2)}) %collective-permute-start.10) | collective-permute-done | bytes 131104 | tf_op jit(solution)/shard_map/ppermute | solution.py:58
  78.9 1.0 collective-permute-done.8.refs_4_
  79.9 0.2 collective-permute-done.6.refs_2_
  80.1 0.4 collective-permute-start.7
  80.6 0.6 collective-permute-done.9.refs_5_
  81.2 0.2 collective-permute-done.7.refs_3_
  81.4 0.7 place_slots.1
  82.1 0.8 copy-done.3
  82.9 8.0 %build.1.built_ref = bf16[6,512,512]{2,1,0:T(8,128)(2,1)} custom-call(bf16[512,512]{1,0:T(8,128)(2,1)} %bitcast.63, bf16[3,512,512]{2,1,0:T(8,128)(2,1)} %own_ref.1, bf16[3,512,512]{2,1,0:T(8,128)(2,1)} %collective-permute-done.4.other_ref), custom_call_target="tpu_custom_call" | custom-call | tf_op jit(solution)/shard_map/build/pallas_call | solution.py:146
  91.0 1.9 %copy-done.1 = bf16[6,512,512]{2,1,0:T(8,128)(2,1)S(1)} copy-done((bf16[6,512,512]{2,1,0:T(8,128)(2,1)S(1)}, bf16[6,512,512]{2,1,0:T(8,128)(2,1)}, u32[]{:S(2)}) %copy-start.1) | copy-done | bytes 3145752
  92.8 1.0 apply_pairs.1.applied_ref
  93.8 1.1 all-to-all-done.1
  94.9 1.0 join_terms.1
  96.0 1.5 collective-permute-done.12
  97.5 0.1 add_convert_fusion.2
  97.6 10.0 %all_to_all.35 = bf16[8,64,256]{2,1,0:T(8,128)(2,1)S(1)} all-to-all(bf16[8,64,256]{2,1,0:T(8,128)(2,1)S(1)} %bitcast.69), channel_id=1, replica_groups=mesh['outer'=2,'core'=2,'high'=2,'low'=2,'near'=2] {'outer','low','near'}, dimensions={0} | all-to-all | bytes 524288 | tf_op jit(solution)/shard_map/all_to_all | solution.py:436
  107.6 1.2 collective-permute-start.13
  108.8 3.7 %collective-permute-done.13 = bf16[2,2,16,256]{3,2,1,0:T(8,128)(2,1)S(1)} collective-permute-done((bf16[2,2,16,256]{3,2,1,0:T(8,128)(2,1)S(1)}, bf16[2,2,16,256]{3,2,1,0:T(8,128)(2,1)S(1)}, u32[]{:S(2)}, u32[]{:S(2)}) %collective-permute-start.13) | collective-permute-done | bytes 32800 | tf_op jit(solution)/shard_map/ppermute | solution.py:45
  112.6 9.4 %all_to_all.36 = bf16[8,64,256]{2,1,0:T(8,128)(2,1)S(1)} all-to-all(bf16[8,64,256]{2,1,0:T(8,128)(2,1)S(1)} %broadcast_in_dim.34), channel_id=1, replica_groups=mesh['outer'=2,'core'=2,'high'=2,'low'=2,'near'=2] {'outer','low','near'}, dimensions={0} | all-to-all | bytes 524288 | tf_op jit(solution)/shard_map/all_to_all | solution.py:446
  122.0 1.8 %apply_terms.1 = (f32[2,4,2,2,16,256]{5,4,3,2,1,0:T(8,128)S(1)}, bf16[2,4,2,2,16,256]{5,4,3,2,1,0:T(8,128)(2,1)S(1)}) custom-call(bf16[2,4,2,2,16,256]{5,4,3,2,1,0:T(8,128)(2,1)S(1)} %bitcast.65, bf16[6,512,512]{2,1,0:T(8,128)(2,1)S(1)} %copy-done.2, bf16[2,16,16,1536]{3,2,1,0:T(8,128)(2,1)S(1)} %get-tuple-element.49.joined_ref), custom_call_target="tpu_custom_call" | custom-call | flops 1610612736 | bytes 4980736 | tf_op jit(solution)/shard_map/apply_terms/pallas_call | solution.py:284
  123.8 1.5 collective-permute-done.14
  125.5 10.0 %all_to_all.37 = bf16[8,64,256]{2,1,0:T(8,128)(2,1)S(1)} all-to-all(bf16[8,64,256]{2,1,0:T(8,128)(2,1)S(1)} %bitcast.70), channel_id=1, replica_groups=mesh['outer'=2,'core'=2,'high'=2,'low'=2,'near'=2] {'outer','low','near'}, dimensions={0} | all-to-all | bytes 524288 | tf_op jit(solution)/shard_map/all_to_all | solution.py:436
  135.5 1.2 collective-permute-start.15
  136.7 3.7 %collective-permute-done.15 = bf16[2,2,16,256]{3,2,1,0:T(8,128)(2,1)S(1)} collective-permute-done((bf16[2,2,16,256]{3,2,1,0:T(8,128)(2,1)S(1)}, bf16[2,2,16,256]{3,2,1,0:T(8,128)(2,1)S(1)}, u32[]{:S(2)}, u32[]{:S(2)}) %collective-permute-start.15) | collective-permute-done | bytes 32800 | tf_op jit(solution)/shard_map/ppermute | solution.py:45
  140.5 9.4 %all_to_all.38 = bf16[8,64,256]{2,1,0:T(8,128)(2,1)S(1)} all-to-all(bf16[8,64,256]{2,1,0:T(8,128)(2,1)S(1)} %broadcast_in_dim.35), channel_id=1, replica_groups=mesh['outer'=2,'core'=2,'high'=2,'low'=2,'near'=2] {'outer','low','near'}, dimensions={0} | all-to-all | bytes 524288 | tf_op jit(solution)/shard_map/all_to_all | solution.py:446
  149.8 2.0 %last_terms.1 = (f32[2,8,2,16,256]{4,3,2,1,0:T(8,128)S(1)}, bf16[2,8,2,16,256]{4,3,2,1,0:T(8,128)(2,1)S(1)}) custom-call(s32[1]{0:T(128)} %bitcast.core_ref, bf16[2,4,2,2,16,256]{5,4,3,2,1,0:T(8,128)(2,1)S(1)} %bitcast.64, bf16[6,512,512]{2,1,0:T(8,128)(2,1)S(1)} %copy-done.2, bf16[2,16,16,1536]{3,2,1,0:T(8,128)(2,1)S(1)} %get-tuple-element.49.joined_ref), custom_call_target="tpu_custom_call" | custom-call | flops 1610612736 | bytes 4980738 | tf_op jit(solution)/shard_map/last_terms/pallas_call | solution.py:284
  151.9 0.5 collective-permute-start.16
  152.4 1.0 collective-permute-done.16
  153.6 13.0 %all_to_all.39 = bf16[16,32,256]{2,1,0:T(8,128)(2,1)S(1)} all-to-all(bf16[16,32,256]{2,1,0:T(8,128)(2,1)S(1)} %bitcast.68), channel_id=1, replica_groups=mesh['outer'=2,'core'=2,'high'=2,'low'=2,'near'=2] {'outer','high','low'..., dimensions={0} | all-to-all | bytes 524288 | tf_op jit(solution)/shard_map/all_to_all | solution.py:455
  166.7 0.6 pad_maximum_fusion.3
  (72 shorter events, 1.4 us)
Async XLA Ops:
  0.0 10.9 %copy-start = (bf16[96,96]{1,0:T(8,128)(2,1)S(1)}, bf16[96,96]{1,0:T(8,128)(2,1)}, u32[]{:S(2)}) copy-start(bf16[96,96]{1,0:T(8,128)(2,1)} %param.10) | copy-start | bytes 55300
  2.3 7.4 %copy-start.4 = (bf16[16,512]{1,0:T(8,128)(2,1)S(1)}, bf16[16,512]{1,0:T(8,128)(2,1)}, u32[]{:S(2)}) copy-start(bf16[16,512]{1,0:T(8,128)(2,1)} %param.11) | copy-start | bytes 49156
  2.3 8.0 %copy-start.6 = (s32[8]{0:T(128)S(1)}, s32[8]{0:T(128)}, u32[]{:S(2)}) copy-start(s32[8]{0:T(128)} %param.13) | copy-start | bytes 100
  2.3 8.4 %copy-start.7 = (s32[96]{0:T(128)S(1)}, s32[96]{0:T(128)}, u32[]{:S(2)}) copy-start(s32[96]{0:T(128)} %param.12) | copy-start | bytes 1156
  2.3 9.5 %copy-start.5 = (bf16[16,512]{1,0:T(8,128)(2,1)S(1)}, bf16[16,512]{1,0:T(8,128)(2,1)}, u32[]{:S(2)}) copy-start(bf16[16,512]{1,0:T(8,128)(2,1)} %param.7) | copy-start | bytes 49156
  2.3 47.6 %all-to-all-start = ((bf16[32,48,512]{2,1,0:T(8,128)(2,1)}), bf16[32,48,512]{2,1,0:T(8,128)(2,1)S(1)}, u32[]{:S(2)}, u32[]{:S(2)}) async-start(bf16[32,48,512]{2,1,0:T(8,128)(2,1)} %bitcast.66), calls=%async_computation | async-start | bytes 3145728 | tf_op jit(solution)/shard_map/all_to_all | solution.py:388
  9.7 2.9 %collective-permute-start = (bf16[16,256]{1,0:T(8,128)(2,1)S(1)}, bf16[16,256]{1,0:T(8,128)(2,1)S(1)}, u32[]{:S(2)}, u32[]{:S(2)}) collective-permute-start(bf16[16,256]{1,0:T(8,128)(2,1)S(1)} %broadcast_select_fusion.2), channel_id=1, source_target_pairs={{0,8},{8,0},{1,9},{9,1},{2,10},{10,2},{3,11},{11,3},{4,12},{12,4},... | collective-permute-start | bytes 24584 | tf_op jit(solution)/shard_map/ppermute | solution.py:38
  10.0 42.5 %collective-permute-start.4 = (bf16[3,512,512]{2,1,0:T(8,128)(2,1)}, bf16[3,512,512]{2,1,0:T(8,128)(2,1)}, u32[]{:S(2)}, u32[]{:S(2)}) collective-permute-start(bf16[3,512,512]{2,1,0:T(8,128)(2,1)} %own_ref.1), channel_id=1, source_target_pairs={{0,8},{8,0},{1,9},{9,1},{2,10},{10,2},{3,11},{11,3},{4,12},{12,4},... | collective-permute-start | bytes 4718600 | tf_op jit(solution)/shard_map/ppermute | solution.py:38
  12.6 28.2 %collective-permute-start.3 = (bf16[4,16,256]{2,1,0:T(8,128)(2,1)S(1)}, bf16[4,16,256]{2,1,0:T(8,128)(2,1)S(1)}, u32[]{:S(2)}, u32[]{:S(2)}) collective-permute-start(bf16[4,16,256]{2,1,0:T(8,128)(2,1)S(1)} %pad_maximum_fusion.1), channel_id=1, source_target_pairs={{6,0},{4,2},{2,4},{0,6},{7,1},{5,3},{3,5},{1,7},{14,8},{12,10},{10... | collective-permute-start | bytes 98312 | tf_op jit(solution)/shard_map/ppermute | solution.py:58
  16.3 33.6 %collective-permute-start.2 = (bf16[4,16,256]{2,1,0:T(8,128)(2,1)S(1)}, bf16[4,16,256]{2,1,0:T(8,128)(2,1)S(1)}, u32[]{:S(2)}, u32[]{:S(2)}) collective-permute-start(bf16[4,16,256]{2,1,0:T(8,128)(2,1)S(1)} %pad_maximum_fusion.1), channel_id=1, source_target_pairs={{4,0},{6,2},{0,4},{2,6},{5,1},{7,3},{1,5},{3,7},{12,8},{14,10},{8,... | collective-permute-start | bytes 98312 | tf_op jit(solution)/shard_map/ppermute | solution.py:58
  16.3 33.6 %collective-permute-start.1 = (bf16[4,16,256]{2,1,0:T(8,128)(2,1)S(1)}, bf16[4,16,256]{2,1,0:T(8,128)(2,1)S(1)}, u32[]{:S(2)}, u32[]{:S(2)}) collective-permute-start(bf16[4,16,256]{2,1,0:T(8,128)(2,1)S(1)} %pad_maximum_fusion.1), channel_id=1, source_target_pairs={{2,0},{0,2},{6,4},{4,6},{3,1},{1,3},{7,5},{5,7},{10,8},{8,10},{14,... | collective-permute-start | bytes 98312 | tf_op jit(solution)/shard_map/ppermute | solution.py:58
  52.4 42.5 %all-to-all-start.1 = ((bf16[32,96,256]{2,1,0:T(8,128)(2,1)}), bf16[32,96,256]{2,1,0:T(8,128)(2,1)S(1)}, u32[]{:S(2)}, u32[]{:S(2)}) async-start(bf16[32,96,256]{2,1,0:T(8,128)(2,1)} %bitcast.21), calls=%async_computation.1 | async-start | bytes 3145728 | tf_op jit(solution)/shard_map/all_to_all | solution.py:425
  56.1 22.8 %collective-permute-start.10 = (bf16[4,4,16,256]{3,2,1,0:T(8,128)(2,1)S(1)}, bf16[4,4,16,256]{3,2,1,0:T(8,128)(2,1)S(1)}, u32[]{:S(2)}, u32[]{:S(2)}) collective-permute-start(bf16[4,4,16,256]{3,2,1,0:T(8,128)(2,1)S(1)} %pad_maximum_fusion.refs_0_), channel_id=1, source_target_pairs={{17,0},{16,1},{1,16},{0,17},{19,2},{18,3},{3,18},{2,19},{21,4},{20... | collective-permute-start | bytes 393224 | tf_op jit(solution)/shard_map/ppermute | solution.py:58
  58.8 21.1 %collective-permute-start.8 = (bf16[4,4,16,256]{3,2,1,0:T(8,128)(2,1)S(1)}, bf16[4,4,16,256]{3,2,1,0:T(8,128)(2,1)S(1)}, u32[]{:S(2)}, u32[]{:S(2)}) collective-permute-start(bf16[4,4,16,256]{3,2,1,0:T(8,128)(2,1)S(1)} %pad_maximum_fusion.refs_0_), channel_id=1, source_target_pairs={{16,0},{17,1},{0,16},{1,17},{18,2},{19,3},{2,18},{3,19},{20,4},{21... | collective-permute-start | bytes 393224 | tf_op jit(solution)/shard_map/ppermute | solution.py:58
  59.4 20.7 %collective-permute-start.6 = (bf16[4,4,16,256]{3,2,1,0:T(8,128)(2,1)S(1)}, bf16[4,4,16,256]{3,2,1,0:T(8,128)(2,1)S(1)}, u32[]{:S(2)}, u32[]{:S(2)}) collective-permute-start(bf16[4,4,16,256]{3,2,1,0:T(8,128)(2,1)S(1)} %pad_maximum_fusion.refs_0_), channel_id=1, source_target_pairs={{1,0},{0,1},{17,16},{16,17},{3,2},{2,3},{19,18},{18,19},{5,4},{4,5... | collective-permute-start | bytes 393224 | tf_op jit(solution)/shard_map/ppermute | solution.py:58
  59.6 20.9 %collective-permute-start.5 = (bf16[4,2,16,256]{3,2,1,0:T(8,128)(2,1)S(1)}, bf16[4,2,16,256]{3,2,1,0:T(8,128)(2,1)S(1)}, u32[]{:S(2)}, u32[]{:S(2)}) collective-permute-start(bf16[4,2,16,256]{3,2,1,0:T(8,128)(2,1)S(1)} %slice.56), channel_id=1, source_target_pairs={{0,8},{8,0},{1,9},{9,1},{2,10},{10,2},{3,11},{11,3},{4,12},{12,4},... | collective-permute-start | bytes 196616 | tf_op jit(solution)/shard_map/ppermute | solution.py:38
  78.9 1.7 %collective-permute-start.11 = (bf16[4,2,16,256]{3,2,1,0:T(8,128)(2,1)S(1)}, bf16[4,2,16,256]{3,2,1,0:T(8,128)(2,1)S(1)}, u32[]{:S(2)}, u32[]{:S(2)}) collective-permute-start(bf16[4,2,16,256]{3,2,1,0:T(8,128)(2,1)S(1)} %slice.70), channel_id=1, source_target_pairs={{0,8},{8,0},{1,9},{9,1},{2,10},{10,2},{3,11},{11,3},{4,12},{12,4},... | collective-permute-start | bytes 196616 | tf_op jit(solution)/shard_map/ppermute | solution.py:38
  79.9 1.3 collective-permute-start.9
  80.1 1.3 collective-permute-start.7
  82.1 0.8 copy-start.3
  91.0 1.9 %copy-start.1 = (bf16[6,512,512]{2,1,0:T(8,128)(2,1)S(1)}, bf16[6,512,512]{2,1,0:T(8,128)(2,1)}, u32[]{:S(2)}) copy-start(bf16[6,512,512]{2,1,0:T(8,128)(2,1)} %build.1.built_ref) | copy-start | bytes 9437188
  94.9 27.1 %copy-start.2 = (bf16[6,512,512]{2,1,0:T(8,128)(2,1)S(1)}, bf16[6,512,512]{2,1,0:T(8,128)(2,1)}, u32[]{:S(2)}) copy-start(bf16[6,512,512]{2,1,0:T(8,128)(2,1)} %build.1.built_ref) | copy-start | bytes 9437188
  95.9 1.6 collective-permute-start.12
  107.6 4.9 %collective-permute-start.13 = (bf16[2,2,16,256]{3,2,1,0:T(8,128)(2,1)S(1)}, bf16[2,2,16,256]{3,2,1,0:T(8,128)(2,1)S(1)}, u32[]{:S(2)}, u32[]{:S(2)}) collective-permute-start(bf16[2,2,16,256]{3,2,1,0:T(8,128)(2,1)S(1)} %multiply_convert_fusion.3), channel_id=1, source_target_pairs={{0,4},{4,0},{1,5},{5,1},{2,6},{6,2},{3,7},{7,3},{8,12},{12,8},{9,1... | collective-permute-start | bytes 98312 | tf_op jit(solution)/shard_map/ppermute | solution.py:45
  123.8 1.6 collective-permute-start.14
  135.5 4.9 %collective-permute-start.15 = (bf16[2,2,16,256]{3,2,1,0:T(8,128)(2,1)S(1)}, bf16[2,2,16,256]{3,2,1,0:T(8,128)(2,1)S(1)}, u32[]{:S(2)}, u32[]{:S(2)}) collective-permute-start(bf16[2,2,16,256]{3,2,1,0:T(8,128)(2,1)S(1)} %multiply_convert_fusion.1), channel_id=1, source_target_pairs={{0,4},{4,0},{1,5},{5,1},{2,6},{6,2},{3,7},{7,3},{8,12},{12,8},{9,1... | collective-permute-start | bytes 98312 | tf_op jit(solution)/shard_map/ppermute | solution.py:45
  151.8 1.6 collective-permute-start.17
  151.9 1.5 collective-permute-start.16
